TPU v7x, 32 devices: a whole 2x2x4 slice. The times are simulated.
32 devices in a mesh: grp: 2 (over x), ax: 8 (over z, y), nr: 2 (over core).
Axes of the slice: x: 2, y: 2, z: 4, core: 2. Of those that a mesh axis runs over, the one named last changes fastest.
Arguments:
- pair_map: bfloat16 [1024, 512, 128], P(('grp', 'ax', 'nr')), parts along dimension 0, may hold values from -24 to 24
- chain_ids: int32 [1024], P('grp'), parts along dimension 0, may hold values from 0 to 7, never falling along the last dimension, each value on 1 to 128 neighbouring positions
- token_mask: int32 [1024], P('grp'), parts along dimension 0, may hold values 0 or 1
- band_start: int32 [2], P('grp'), parts along dimension 0, may hold values from 0 to 464
- chain_embed: float32 [128], replicated, may hold values from -8 to 8
- gain_in: float32 [128], replicated, may hold values from 0.1 to 1.9
- gain_out: float32 [128], replicated, may hold values from 0.1 to 1.9
- w_left: bfloat16 [128, 256], P(None, 'nr'), may hold values from -0.5 to 0.5
- w_right: bfloat16 [128, 256], P(None, 'nr'), may hold values from -0.5 to 0.5
- w_gate: bfloat16 [128, 128], P(None, 'nr'), may hold values from -0.5 to 0.5
- w_out: bfloat16 [128, 128], P(None, 'nr'), may hold values from -0.5 to 0.5
Outputs:
- update: bfloat16 [1024, 48, 128], P(('grp', 'ax', 'nr')), parts along dimension 0
There are 2 independent parts, one for each index of `grp`. A program takes and returns all parts, laid end to end along the dimension named above; an argument that names none is the same for every part. Nothing has to cross between parts.
Inputs may be any that keep to these rules, and one draw needn't show every extreme that they name: `chain_ids`: non-decreasing along tokens; a chain holds 1 to 128 tokens, one exactly 128.
All inputs are finite; a program needn't handle non-finite values.
Results may differ from a plain program's by a relative error of at most 0.0075.
Values may be sent and summed in bfloat16 or wider, within the bound.
No kernel may reach another device: no remote copies, remote signals or barrier semaphores. Data moves between devices by JAX's collectives and lax.ppermute only.
A program may use at most 192 MiB of HBM per device.

v0:
```python
import jax
import jax.numpy as jnp
from jax import lax
from jax.sharding import PartitionSpec as P

BAND = 48


norm_eps = 1e-05


def layer_norm(values, gain_vec):
    average = jnp.mean(values, -1, keepdims=True)
    centered = values - average
    variance = jnp.mean(centered * centered, -1, keepdims=True)
    return centered * lax.rsqrt(variance + norm_eps) * gain_vec


def normalize(block_rows, same_chain, chain_embed, gain_in):
    shifted = block_rows.astype(jnp.float32) + same_chain[..., None] * chain_embed
    return layer_norm(shifted, gain_in).astype(jnp.bfloat16)


def gated_proj(normed, weight, pair_weight):
    half_width = weight.shape[0]
    both_proj = jnp.dot(normed, weight, preferred_element_type=jnp.float32)
    gate_half = both_proj[..., :half_width]
    value_half = both_proj[..., half_width:]
    return (jax.nn.sigmoid(gate_half) * value_half * pair_weight[..., None]).astype(jnp.bfloat16)


def body(
    pair_map,
    chain_ids,
    token_mask,
    band_start,
    chain_embed,
    gain_in,
    gain_out,
    w_left,
    w_right,
    w_gate,
    w_out,
):
    row_count, col_count, channels = pair_map.shape
    band_width = BAND
    w_left, w_right, w_gate, w_out = (
        lax.all_gather(w_left, "nr", axis=1, tiled=True),
        lax.all_gather(w_right, "nr", axis=1, tiled=True),
        lax.all_gather(w_gate, "nr", axis=1, tiled=True),
        lax.all_gather(w_out, "nr", axis=1, tiled=True),
    )
    first_row_id = lax.axis_index(("ax", "nr")) * row_count
    band_first = band_start[0]
    token_weight = token_mask.astype(jnp.float32)
    row_chain = lax.dynamic_slice_in_dim(chain_ids, first_row_id, row_count)
    row_mask = lax.dynamic_slice_in_dim(token_weight, first_row_id, row_count)
    band_chain = lax.dynamic_slice_in_dim(chain_ids, band_first, band_width)
    band_mask = lax.dynamic_slice_in_dim(token_weight, band_first, band_width)
    block_size = row_count // 4
    row_blocks = pair_map.reshape(4, block_size, col_count, channels)

    def make_left(pieces):
        block_rows, block_chain, block_mask = pieces
        same_chain = (block_chain[:, None] == chain_ids[None, :]).astype(jnp.float32)
        normed = normalize(block_rows, same_chain, chain_embed, gain_in)
        return gated_proj(normed, w_left, block_mask[:, None] * token_weight[None, :])

    left_proj = lax.map(
        make_left, (row_blocks, row_chain.reshape(4, block_size), row_mask.reshape(4, block_size))
    )
    left_proj = left_proj.reshape(row_count, col_count, channels)
    band_rows = lax.dynamic_slice_in_dim(pair_map, band_first, band_width, 1)
    same_band = (row_chain[:, None] == band_chain[None, :]).astype(jnp.float32)
    band_normed = normalize(band_rows, same_band, chain_embed, gain_in)
    right_proj = gated_proj(band_normed, w_right, row_mask[:, None] * band_mask[None, :])
    gate_values = jax.nn.sigmoid(jnp.dot(band_normed, w_gate, preferred_element_type=jnp.float32))
    columns = lax.all_to_all(left_proj, ("ax", "nr"), split_axis=1, concat_axis=0, tiled=True)
    triangle = jnp.einsum(
        "kic,kjc->ijc",
        columns,
        lax.all_gather(right_proj, ("ax", "nr"), axis=0, tiled=True),
        preferred_element_type=jnp.float32,
    )
    normed_out = layer_norm(triangle, gain_out).astype(jnp.bfloat16)
    projected = jnp.dot(normed_out, w_out, preferred_element_type=jnp.float32)
    return (gate_values * projected).astype(jnp.bfloat16)


def solution(mesh):
    in_specs = (
        P(("grp", "ax", "nr"), None, None),
        P("grp"),
        P("grp"),
        P("grp"),
        P(),
        P(),
        P(),
        P(None, "nr"),
        P(None, "nr"),
        P(None, "nr"),
        P(None, "nr"),
    )
    out_specs = P(("grp", "ax", "nr"), None, None)
    return jax.shard_map(body, mesh=mesh, in_specs=in_specs, out_specs=out_specs, check_vma=False)
```

profile of v0, /device:TPU:13, one launch (start us, length us, event | category | flops | bytes accessed | tf_op | source)
XLA Modules:
  0.0 225.7 jit_solution(4221866654693653898)
XLA Ops:
  9.6 1.6 fusion.31
  11.2 1.7 multiply_reduce_fusion.2
  12.9 2.5 %all_gather.16 = bf16[128,256]{1,0:T(8,128)(2,1)S(1)} all-gather(bf16[128,128]{1,0:T(8,128)(2,1)} %param.21), channel_id=1, replica_groups=mesh['grp'=2,'ax'=8,'nr'=2] {'nr'}, dimensions={1}, use_global_device_ids=true | all-gather | bytes 98304 | tf_op jit(solution)/shard_map/all_gather | solution.py:49
  15.5 2.0 fusion.32
  18.7 1.8 all_gather.18
  20.6 46.6 %while.10 = (s32[]{:T(128)}, bf16[4,8,512,128]{3,1,0,2:T(8,128)(2,1)}, bf16[4,8,512,128]{3,2,1,0:T(8,128)(2,1)}, s32[4,8]{1,0:T(4,128)S(1)}, s32[512]{0:T(512)S(...) while((s32[]{:T(128)}, ...), condition=%wide.region_5.6_spmd, body=%wide.region_2.0_spmd.sunk | while | flops 280510464 | bytes 14998845 | solution.py:69
  20.7 2.3 %fusion.49 = f32[8,512]{1,0:T(8,128)S(1)} fusion(f32[128]{0:T(128)S(1)} %get-tuple-element.168, f32[8,512]{1,0:T(8,128)S(1)} %compare_convert_fusion.3, bf16[4,8,512,128]{3,2,1,0:T(8,128)(2,1)} %get-tuple-element.165, s32[]{:T(128)} %get-tuple-element.152), kind=kLoop, calls=%fused_computation.11.clone.1 | loop fusion | flops 2093056 | bytes 1081860 | tf_op jit(solution)/shard_map/while/body/eval_jaxpr/reduce_sum | solution.py:13
  23.0 2.9 %multiply_reduce_fusion.4 = f32[8,512]{1,0:T(8,128)S(1)} fusion(f32[8,512]{1,0:T(8,128)S(1)} %broadcast_multiply_fusion.8, f32[128]{0:T(128)S(1)} %get-tuple-element.168, f32[8,512]{1,0:T(8,128)S(1)} %compare_convert_fusion.3, bf16[4,8,512,128]{3,2,1,0:T(8,128)(2,1)} %get-tuple-element.165, s32[]{:T(128)} %get-tuple-element.152), kind=kLoop, calls=%fused_computation.9.clone.1 | loop fusion | flops 3141632 | bytes 1098244 | tf_op jit(solution)/shard_map/while/body/eval_jaxpr/reduce_sum | solution.py:15
  25.9 3.7 %fusion.50 = f32[8,512,256]{2,1,0:T(8,128)S(1)} fusion(f32[128]{0:T(128)S(1)} %get-tuple-element.169, f32[8,512]{1,0:T(8,128)S(1)} %add_rsqrt_fusion.4, f32[8,512]{1,0:T(8,128)S(1)} %broadcast_multiply_fusion.8, f32[128]{0:T(128)S(1)} %get-tuple-element.168, f32[8,512]{1,0:T(8,128)S(1)} %compare_convert_fusion.3, ...), kind=kOutput, calls=%fused_computation.12.clone.1 | convolution fusion | flops 272105472 | bytes 5359104 | tf_op jit(solution)/shard_map/while/body/eval_jaxpr/dot_general | solution.py:26
  30.5 1.7 copy_dynamic-update-slice_fusion.2
  32.3 2.3 %fusion.49 = f32[8,512]{1,0:T(8,128)S(1)} fusion(f32[128]{0:T(128)S(1)} %get-tuple-element.168, f32[8,512]{1,0:T(8,128)S(1)} %compare_convert_fusion.3, bf16[4,8,512,128]{3,2,1,0:T(8,128)(2,1)} %get-tuple-element.165, s32[]{:T(128)} %get-tuple-element.152), kind=kLoop, calls=%fused_computation.11.clone.1 | loop fusion | flops 2093056 | bytes 1081860 | tf_op jit(solution)/shard_map/while/body/eval_jaxpr/reduce_sum | solution.py:13
  34.6 2.9 %multiply_reduce_fusion.4 = f32[8,512]{1,0:T(8,128)S(1)} fusion(f32[8,512]{1,0:T(8,128)S(1)} %broadcast_multiply_fusion.8, f32[128]{0:T(128)S(1)} %get-tuple-element.168, f32[8,512]{1,0:T(8,128)S(1)} %compare_convert_fusion.3, bf16[4,8,512,128]{3,2,1,0:T(8,128)(2,1)} %get-tuple-element.165, s32[]{:T(128)} %get-tuple-element.152), kind=kLoop, calls=%fused_computation.9.clone.1 | loop fusion | flops 3141632 | bytes 1098244 | tf_op jit(solution)/shard_map/while/body/eval_jaxpr/reduce_sum | solution.py:15
  37.5 3.7 %fusion.50 = f32[8,512,256]{2,1,0:T(8,128)S(1)} fusion(f32[128]{0:T(128)S(1)} %get-tuple-element.169, f32[8,512]{1,0:T(8,128)S(1)} %add_rsqrt_fusion.4, f32[8,512]{1,0:T(8,128)S(1)} %broadcast_multiply_fusion.8, f32[128]{0:T(128)S(1)} %get-tuple-element.168, f32[8,512]{1,0:T(8,128)S(1)} %compare_convert_fusion.3, ...), kind=kOutput, calls=%fused_computation.12.clone.1 | convolution fusion | flops 272105472 | bytes 5359104 | tf_op jit(solution)/shard_map/while/body/eval_jaxpr/dot_general | solution.py:26
  42.1 1.8 copy_dynamic-update-slice_fusion.2
  43.9 2.3 %fusion.49 = f32[8,512]{1,0:T(8,128)S(1)} fusion(f32[128]{0:T(128)S(1)} %get-tuple-element.168, f32[8,512]{1,0:T(8,128)S(1)} %compare_convert_fusion.3, bf16[4,8,512,128]{3,2,1,0:T(8,128)(2,1)} %get-tuple-element.165, s32[]{:T(128)} %get-tuple-element.152), kind=kLoop, calls=%fused_computation.11.clone.1 | loop fusion | flops 2093056 | bytes 1081860 | tf_op jit(solution)/shard_map/while/body/eval_jaxpr/reduce_sum | solution.py:13
  46.3 2.9 %multiply_reduce_fusion.4 = f32[8,512]{1,0:T(8,128)S(1)} fusion(f32[8,512]{1,0:T(8,128)S(1)} %broadcast_multiply_fusion.8, f32[128]{0:T(128)S(1)} %get-tuple-element.168, f32[8,512]{1,0:T(8,128)S(1)} %compare_convert_fusion.3, bf16[4,8,512,128]{3,2,1,0:T(8,128)(2,1)} %get-tuple-element.165, s32[]{:T(128)} %get-tuple-element.152), kind=kLoop, calls=%fused_computation.9.clone.1 | loop fusion | flops 3141632 | bytes 1098244 | tf_op jit(solution)/shard_map/while/body/eval_jaxpr/reduce_sum | solution.py:15
  49.2 3.8 %fusion.50 = f32[8,512,256]{2,1,0:T(8,128)S(1)} fusion(f32[128]{0:T(128)S(1)} %get-tuple-element.169, f32[8,512]{1,0:T(8,128)S(1)} %add_rsqrt_fusion.4, f32[8,512]{1,0:T(8,128)S(1)} %broadcast_multiply_fusion.8, f32[128]{0:T(128)S(1)} %get-tuple-element.168, f32[8,512]{1,0:T(8,128)S(1)} %compare_convert_fusion.3, ...), kind=kOutput, calls=%fused_computation.12.clone.1 | convolution fusion | flops 272105472 | bytes 5359104 | tf_op jit(solution)/shard_map/while/body/eval_jaxpr/dot_general | solution.py:26
  53.8 1.8 copy_dynamic-update-slice_fusion.2
  55.7 2.4 %fusion.49 = f32[8,512]{1,0:T(8,128)S(1)} fusion(f32[128]{0:T(128)S(1)} %get-tuple-element.168, f32[8,512]{1,0:T(8,128)S(1)} %compare_convert_fusion.3, bf16[4,8,512,128]{3,2,1,0:T(8,128)(2,1)} %get-tuple-element.165, s32[]{:T(128)} %get-tuple-element.152), kind=kLoop, calls=%fused_computation.11.clone.1 | loop fusion | flops 2093056 | bytes 1081860 | tf_op jit(solution)/shard_map/while/body/eval_jaxpr/reduce_sum | solution.py:13
  58.0 2.9 %multiply_reduce_fusion.4 = f32[8,512]{1,0:T(8,128)S(1)} fusion(f32[8,512]{1,0:T(8,128)S(1)} %broadcast_multiply_fusion.8, f32[128]{0:T(128)S(1)} %get-tuple-element.168, f32[8,512]{1,0:T(8,128)S(1)} %compare_convert_fusion.3, bf16[4,8,512,128]{3,2,1,0:T(8,128)(2,1)} %get-tuple-element.165, s32[]{:T(128)} %get-tuple-element.152), kind=kLoop, calls=%fused_computation.9.clone.1 | loop fusion | flops 3141632 | bytes 1098244 | tf_op jit(solution)/shard_map/while/body/eval_jaxpr/reduce_sum | solution.py:15
  61.0 3.7 %fusion.50 = f32[8,512,256]{2,1,0:T(8,128)S(1)} fusion(f32[128]{0:T(128)S(1)} %get-tuple-element.169, f32[8,512]{1,0:T(8,128)S(1)} %add_rsqrt_fusion.4, f32[8,512]{1,0:T(8,128)S(1)} %broadcast_multiply_fusion.8, f32[128]{0:T(128)S(1)} %get-tuple-element.168, f32[8,512]{1,0:T(8,128)S(1)} %compare_convert_fusion.3, ...), kind=kOutput, calls=%fused_computation.12.clone.1 | convolution fusion | flops 272105472 | bytes 5359104 | tf_op jit(solution)/shard_map/while/body/eval_jaxpr/dot_general | solution.py:26
  65.5 1.7 copy_dynamic-update-slice_fusion.2
  67.2 6.3 %all-to-all-start = ((bf16[32,512,128]{2,0,1:T(8,128)(2,1)}), bf16[32,512,128]{2,0,1:T(8,128)(2,1)}, u32[]{:S(2)}, u32[]{:S(2)}) async-start(bf16[32,512,128]{2,0,1:T(8,128)(2,1)} %bitcast.9), calls=%async_computation | async-start | bytes 8388608 | tf_op jit(solution)/shard_map/all_to_all | solution.py:78
  73.5 1.9 all_gather.15
  75.4 2.0 all_gather.19
  77.4 2.0 fusion.22
  79.4 89.8 %all-to-all-done = bf16[32,512,128]{2,0,1:T(8,128)(2,1)} async-done(((bf16[32,512,128]{2,0,1:T(8,128)(2,1)}), bf16[32,512,128]{2,0,1:T(8,128)(2,1)}, u32[]{:S(2)}, u32[]{:S(2)}) %all-to-all-start) | async-done | bytes 4194336 | tf_op jit(solution)/shard_map/all_to_all | solution.py:78
  169.2 5.9 %copy.20 = bf16[16,32,32,128]{3,2,1,0:T(8,128)(2,1)} copy(bf16[16,32,32,128]{3,1,2,0:T(8,128)(2,1)} %bitcast.12) | data formatting | bytes 8388608 | tf_op jit(solution)/shard_map/all_to_all | solution.py:78
  175.1 8.6 %copy.22 = bf16[512,32,128]{0,1,2:T(8,128)(2,1)} copy(bf16[512,32,128]{2,1,0:T(8,128)(2,1)} %bitcast.61) | data formatting | bytes 8388608 | tf_op jit(solution)/shard_map/all_to_all | solution.py:78
  183.8 23.1 %copy.21 = bf16[512,48,128]{1,0,2:T(8,128)(2,1)} copy(bf16[512,48,128]{2,1,0:T(8,128)(2,1)} %all-gather.2.cloned.1.call-done) | data formatting | bytes 12582912 | tf_op jit(solution)/shard_map/all_gather | solution.py:82
  206.8 9.7 %bitcast_reduce_fusion = (f32[32,48]{1,0:T(8,128)S(1)}, f32[128,48,32]{1,2,0:T(8,128)S(1)}) fusion(bf16[512,32,128]{0,1,2:T(8,128)(2,1)} %copy.22, bf16[512,48,128]{1,0,2:T(8,128)(2,1)} %copy.21), kind=kOutput, calls=%fused_computation.33 | convolution fusion | flops 201521664 | bytes 11278336 | tf_op jit(solution)/shard_map/kic,kjc->ijc/dot_general | solution.py:79
  217.5 1.3 fusion.23
  (62 shorter events, 8.2 us)
Async XLA Ops:
  6.5 177.2 %all-gather.2.cloned.1.call-start = ((), (), s32[]{:S(2)}) async-start(), calls=%async_computation.1 | async-start | bytes 6684672 | tf_op jit(solution)/shard_map/all_gather | solution.py:82
  15.5 3.2 %copy-start.2 = (bf16[128,128]{1,0:T(8,128)(2,1)S(1)}, bf16[128,128]{1,0:T(8,128)(2,1)}, u32[]{:S(2)}) copy-start(bf16[128,128]{1,0:T(8,128)(2,1)} %param.20) | copy-start | bytes 98308
  15.5 5.1 %copy-start = (f32[128]{0:T(128)S(1)}, f32[128]{0:T(128)}, u32[]{:S(2)}) copy-start(f32[128]{0:T(128)} %param.17) | copy-start | bytes 1540
  15.5 5.1 %copy-start.1 = (s32[512]{0:T(512)S(1)}, s32[512]{0:T(512)}, u32[]{:S(2)}) copy-start(s32[512]{0:T(512)} %param.14) | copy-start | bytes 6148
  15.5 5.1 %copy-start.3 = (f32[128]{0:T(128)S(1)}, f32[128]{0:T(128)}, u32[]{:S(2)}) copy-start(f32[128]{0:T(128)} %param.18) | copy-start | bytes 1540
  67.2 6.3 %copy-start.4 = (bf16[128,64]{0,1:T(8,128)(2,1)S(1)}, bf16[128,64]{0,1:T(8,128)(2,1)}, u32[]{:S(2)}) copy-start(bf16[128,64]{0,1:T(8,128)(2,1)} %param.22) | copy-start | bytes 49156
  67.2 8.2 %copy-start.5 = (bf16[128,64]{0,1:T(8,128)(2,1)S(1)}, bf16[128,64]{0,1:T(8,128)(2,1)}, u32[]{:S(2)}) copy-start(bf16[128,64]{0,1:T(8,128)(2,1)} %param.23) | copy-start | bytes 49156
  67.2 102.0 %all-to-all-start = ((bf16[32,512,128]{2,0,1:T(8,128)(2,1)}), bf16[32,512,128]{2,0,1:T(8,128)(2,1)}, u32[]{:S(2)}, u32[]{:S(2)}) async-start(bf16[32,512,128]{2,0,1:T(8,128)(2,1)} %bitcast.9), calls=%async_computation | async-start | bytes 8388608 | tf_op jit(solution)/shard_map/all_to_all | solution.py:78
  216.5 0.7 copy-start.6
Sparse Core Ops, SparseCore 0:
  18.7 63.7 all-gather.1
where the time goes:
time: 227 us; the launch traced here: 226 us
  waiting for transfers between devices  89.9 us (40%)
  local copies, waits for them, and re-layouts  46.7 us (21%)
  other arithmetic  30.2 us (13%)
  matrix products  30 us (13%)
  between operations  14.1 us (6%)
  blocking collectives  8.17 us (4%)
  starting transfers between devices  6.34 us (3%)
    all_to_all x1, waiting for transfers between devices, body(): lax.all_to_all(left_proj, ('ax', 'nr'), split_axis=1, concat_axis=0, tile...  89.8 us
    all_gather x1, local copies, waits for them, and re-layouts, body(): lax.all_gather(right_proj, ('ax', 'nr'), axis=0, tiled=True)  23.1 us
    dot_general x5, matrix products, gated_proj(): both_proj = jnp.dot(normed, weight, preferred_element_type=jnp.float32)  17 us
    all_to_all x2, local copies, waits for them, and re-layouts, body(): lax.all_to_all(left_proj, ('ax', 'nr'), split_axis=1, concat_axis=0, tile...  14.5 us
    reduce_sum x6, other arithmetic, layer_norm(): variance = jnp.mean(centered * centered, -1, keepdims=True)  13.6 us
    reduce_sum x5, other arithmetic, layer_norm(): average = jnp.mean(values, -1, keepdims=True)  10.9 us
    dot_general x1, matrix products, body(): jnp.einsum('kic,kjc->ijc', columns, lax.all_gather(right_proj, ('ax', 'nr...  9.66 us
    dynamic_update_slice x4, local copies, waits for them, and re-layouts, body(): lax.map(make_left, (row_blocks, row_chain.reshape(4, block_size), row_mas...  6.91 us
  transfers between devices with their start and end apart: 2, of which 1 were waited for; matrix products, arithmetic and copies ran while one was open for 28% of the time, Pallas kernels for 0%

commit v1 on v0

v1 whole, which is shorter than its diff:
```python
import functools

import jax
import jax.numpy as jnp
from jax import lax
from jax.experimental import pallas as pl
from jax.experimental.pallas import tpu as pltpu
from jax.sharding import PartitionSpec as P

BAND = 48
NORM_EPS = 1e-05
F32, BF16, I32 = jnp.float32, jnp.bfloat16, jnp.int32
LAST = (((1,), (1,)), ((), ()))


def layer_norm(values, gain):
    mean = jnp.mean(values, -1, keepdims=True)
    centered = values - mean
    var = jnp.mean(centered * centered, -1, keepdims=True)
    return centered * lax.rsqrt(var + NORM_EPS) * gain


def halves(own, other, first):
    return jnp.where(first, own, other), jnp.where(first, other, own)


def right_kernel(
    chain_s, mask_s, meta, own_band, other_band, chain_cols, embed, gain, w_own, w_other, row_mask, right_ref, gate_ref,
    normed_scr, right_scr,
):
    rows, band, width = own_band.shape
    both = 2 * rows
    start = meta[4]
    first = meta[1] == 0
    band_chain = chain_cols[pl.ds(start, band), :]
    emb, gn = embed[...], gain[...]
    for source, base, ref in ((0, meta[2], own_band), (1, meta[3], other_band)):
        for k in range(rows):
            same = band_chain == chain_s[base + k]
            shifted = ref[k].astype(F32) + jnp.where(same, emb, 0.0)
            keep = mask_s[base + k].astype(F32)
            row = (source * rows + k) * band
            normed_scr[row : row + band, :] = layer_norm(shifted, gn) * keep
    w_gate_half, w_value_half = halves(w_own[width : 2 * width, :], w_other[width : 2 * width, :], first)
    w_right = jnp.concatenate([w_gate_half, w_value_half], 0)
    half = width // 2
    low, high = halves(w_own[2 * width : 2 * width + half, :], w_other[2 * width : 2 * width + half, :], first)
    w_gate = jnp.concatenate([low, high], 0)
    mask_i = row_mask[...]
    for j in range(band):
        normed = normed_scr[pl.ds(j, both, stride=band), :].astype(BF16)
        proj = lax.dot_general(w_right, normed, LAST, preferred_element_type=F32)
        edge = jax.nn.sigmoid(proj[:width]) * proj[width:] * mask_s[start + j].astype(F32)
        right_scr[pl.ds(j, width, stride=band), 0:both] = edge
        gate = lax.dot_general(normed[0:rows], w_gate, LAST, preferred_element_type=F32)
        gate_ref[j] = jax.nn.sigmoid(gate) * mask_i
    right_ref[...] = right_scr[:, 0:both].reshape(width, band, both).astype(BF16)


def triangle_kernel(group, tile, out_type, chain_s, mask_s, meta, *refs):
    own = refs[:group]
    other = refs[group : 2 * group]
    chain_cols = refs[2 * group : 3 * group]
    embed, gain, w_own, w_other, right_ref = refs[3 * group : 3 * group + 5]
    outs = refs[3 * group + 5 : 4 * group + 5]
    left_scr, tri_scr = refs[4 * group + 5 :]
    width, band, both = right_ref.shape
    rows = both // 2
    size = own[0].shape[2]
    lanes = group * size
    step = pl.program_id(0)
    first = meta[1] == 0
    w_gate_half, w_value_half = halves(w_own[0:width, :], w_other[0:width, :], first)
    w_left = jnp.concatenate([w_gate_half, w_value_half], 0)
    chains = jnp.concatenate([ref[...] for ref in chain_cols], 0)
    emb, gn = embed[...], gain[...]

    def normed(source, k):
        base = meta[3] if source else meta[2]
        values = jnp.concatenate([ref[k, 0] for ref in (other if source else own)], 0)
        same = chains == chain_s[base + step * tile + k]
        return layer_norm(values.astype(F32) + jnp.where(same, emb, 0.0), gn).astype(BF16)

    for k in range(tile):
        pair = jnp.concatenate([normed(0, k), normed(1, k)], 0)
        proj = lax.dot_general(w_left, pair, LAST, preferred_element_type=F32)
        edge = jax.nn.sigmoid(proj[:width]) * proj[width:]
        at = step * tile + k
        left_scr[pl.ds(at, width, stride=both), :] = edge[:, :lanes]
        left_scr[pl.ds(at + rows, width, stride=both), :] = edge[:, lanes:]

    @pl.when(step == pl.num_programs(0) - 1)
    def _():
        unroll = 8

        def channels(block, carry):
            for u in range(unroll):
                c = block * unroll + u
                left = left_scr[pl.ds(pl.multiple_of(c * both, both), both), :].astype(BF16)
                tri = jnp.dot(right_ref[c], left, preferred_element_type=F32)
                tri_scr[pl.ds(pl.multiple_of(c * band, 8), band), :] = tri
            return carry

        lax.fori_loop(0, width // unroll, channels, 0)
        for j in range(band):
            turned = tri_scr[pl.ds(j, width, stride=band), :].T
            for b in range(group):
                outs[b][j] = turned[b * size : (b + 1) * size].astype(out_type)


def final_kernel(count, keep_ref, *refs):
    arrived = refs[:count]
    gate_ref, gain, w_own, w_other, nr_s, out_ref, scr = refs[count:]
    band, rows, width = keep_ref.shape
    half = width // 2
    low, high = halves(w_own[2 * width + half :, :], w_other[2 * width + half :, :], nr_s[1] == 0)
    w_out = jnp.concatenate([low, high], 0)
    total = keep_ref[...]
    for ref in arrived:
        total = total + ref[...].astype(F32)
    normed = layer_norm(total.reshape(band * rows, width), gain[...]).astype(BF16)
    projected = lax.dot_general(normed, w_out, LAST, preferred_element_type=F32)
    for j in range(band):
        scr[pl.ds(j, rows, stride=band), :] = projected[j * rows : (j + 1) * rows] * gate_ref[j]
    out_ref[...] = scr[...].reshape(rows, band, width).astype(BF16)


def body(pair_map, chain_ids, token_mask, band_start, chain_embed, gain_in, gain_out, w_left, w_right, w_gate, w_out):
    rows, tokens, width = pair_map.shape
    n_ax = lax.axis_size("ax")
    ax, nr = lax.axis_index("ax"), lax.axis_index("nr")
    band = BAND
    both = 2 * rows

    def swap_core(x):
        return lax.ppermute(x, "nr", [(0, 1), (1, 0)])

    def swap(x, bit):
        return lax.ppermute(x, "ax", [(s, s ^ bit) for s in range(n_ax)])

    start = band_start[0]
    own_row, other_row = (ax * 2 + nr) * rows, (ax * 2 + 1 - nr) * rows
    meta = jnp.stack([ax, nr, own_row, other_row, start]).astype(I32)

    w_own = jnp.concatenate([w_left.T, w_right.T, w_gate.T, w_out.T], 0)
    w_other = swap_core(w_own)
    own_band = lax.dynamic_slice_in_dim(pair_map, start, band, 1)
    other_band = swap_core(own_band)
    blocks = pair_map.reshape(rows, n_ax // 2, 2, 2, rows, width)

    def for_other_core(parity):
        part = lax.dynamic_slice(
            blocks, (0, 0, parity, 1 - nr, 0, 0), (rows, n_ax // 2, 1, 1, rows, width)
        ).reshape(rows, n_ax // 2, rows, width)
        return swap_core(part)

    other_far, other_near = for_other_core(1 - (ax & 1)), for_other_core(ax & 1)
    own_blocks = pair_map.reshape(rows, tokens // rows, rows, width)
    chain_cols = jnp.broadcast_to(chain_ids[:, None], (tokens, 128))
    row_mask = jnp.broadcast_to(
        lax.dynamic_slice_in_dim(token_mask, own_row, rows).astype(F32)[:, None], (rows, width)
    )
    embed, gain, gain_o = chain_embed[None], gain_in[None], gain_out[None]

    vmem = pl.BlockSpec(memory_space=pltpu.VMEM)
    right, gate = pl.pallas_call(
        right_kernel,
        grid_spec=pltpu.PrefetchScalarGridSpec(
            num_scalar_prefetch=3,
            grid=(),
            in_specs=[vmem] * 8,
            out_specs=[vmem] * 2,
            scratch_shapes=[pltpu.VMEM((both * band, width), F32), pltpu.VMEM((width * band, 128), F32)],
        ),
        out_shape=[
            jax.ShapeDtypeStruct((width, band, both), BF16),
            jax.ShapeDtypeStruct((band, rows, width), F32),
        ],
        compiler_params=pltpu.CompilerParams(vmem_limit_bytes=40 << 20),
        cost_estimate=pl.CostEstimate(flops=4 * 10**9, bytes_accessed=2 * 10**6, transcendentals=0),
        name="right",
    )(chain_ids, token_mask, meta, own_band, other_band, chain_cols, embed, gain, w_own, w_other, row_mask)

    def triangle(relative, other_part, out_type):
        group = len(relative)
        tile = 8
        row_specs, part_specs, chain_specs = [], [], []
        for r in relative:
            row_specs.append(
                pl.BlockSpec((tile, 1, rows, width), lambda t, c, m, meta, r=r: (t, (meta[0] ^ r) * 2 + meta[1], 0, 0))
            )
            part_specs.append(
                pl.BlockSpec((tile, 1, rows, width), lambda t, c, m, meta, r=r: (t, (meta[0] ^ r) >> 1, 0, 0))
            )
            chain_specs.append(pl.BlockSpec((rows, 128), lambda t, c, m, meta, r=r: ((meta[0] ^ r) * 2 + meta[1], 0)))
        whole = lambda shape: pl.BlockSpec(shape, lambda t, c, m, meta: (0,) * len(shape))
        out_shape = (band, rows, width)
        return pl.pallas_call(
            functools.partial(triangle_kernel, group, tile, out_type),
            grid_spec=pltpu.PrefetchScalarGridSpec(
                num_scalar_prefetch=3,
                grid=(rows // tile,),
                in_specs=row_specs
                + part_specs
                + chain_specs
                + [whole((1, width)), whole((1, width)), whole(w_own.shape), whole(w_own.shape), whole((width, band, both))],
                out_specs=[whole(out_shape)] * group,
                scratch_shapes=[
                    pltpu.VMEM((width * both, group * rows), F32),
                    pltpu.VMEM((width * band, group * rows), F32),
                ],
            ),
            out_shape=[jax.ShapeDtypeStruct(out_shape, out_type)] * group,
            compiler_params=pltpu.CompilerParams(vmem_limit_bytes=48 << 20),
            cost_estimate=pl.CostEstimate(flops=8 * 10**9, bytes_accessed=4 * 10**6, transcendentals=0),
            name="triangle",
        )(
            chain_ids, token_mask, meta, *([own_blocks] * group), *([other_part] * group), *([chain_cols] * group),
            embed, gain, w_own, w_other, right,
        )

    size = min(128 // rows, n_ax // 2)
    odd, even = list(range(n_ax - 1, 0, -2)), list(range(n_ax - 2, -1, -2))
    parts = {}
    arrived = {r: [] for r in even}
    for at in range(0, len(odd), size):
        group = odd[at : at + size]
        for r, part in zip(group, triangle(group, other_far, BF16)):
            arrived[r - 1].append(swap(part, 1))
    for at in range(0, len(even), size):
        group = even[at : at + size]
        for r, part in zip(group, triangle(group, other_near, F32)):
            parts[r] = part
    for r in even[:-1]:
        total = parts[r]
        for piece in arrived[r]:
            total = total + piece.astype(F32)
        bit = r & -r
        arrived[r - bit].append(swap(total.astype(BF16), bit))

    pieces = arrived[0]
    return pl.pallas_call(
        functools.partial(final_kernel, len(pieces)),
        in_specs=[vmem] * (len(pieces) + 5) + [pl.BlockSpec(memory_space=pltpu.SMEM)],
        out_specs=vmem,
        out_shape=jax.ShapeDtypeStruct((rows, band, width), BF16),
        scratch_shapes=[pltpu.VMEM((rows * band, width), F32)],
        compiler_params=pltpu.CompilerParams(vmem_limit_bytes=32 << 20),
        cost_estimate=pl.CostEstimate(flops=10**9, bytes_accessed=3 * 10**6, transcendentals=0),
        name="final",
    )(parts[0], *pieces, gate, gain_o, w_own, w_other, meta)


def solution(mesh):
    in_specs = (
        P(("grp", "ax", "nr"), None, None),
        P("grp"),
        P("grp"),
        P("grp"),
        P(),
        P(),
        P(),
        P(None, "nr"),
        P(None, "nr"),
        P(None, "nr"),
        P(None, "nr"),
    )
    out_specs = P(("grp", "ax", "nr"), None, None)
    return jax.shard_map(body, mesh=mesh, in_specs=in_specs, out_specs=out_specs, check_vma=False)
```

time: 227 us -> 77.7 us (0.34)
  the two profiles are of different devices: /device:TPU:13 before, /device:TPU:0 now
where the time goes in v1:
time: 77.7 us; the launch traced here: 77.4 us
  Pallas kernels  31.4 us (40%)
  waiting for transfers between devices  24.7 us (32%)
  starting transfers between devices  14.6 us (19%)
  local copies, waits for them, and re-layouts  5.29 us (7%)
  between operations  0.85 us (1%)
    pallas_call x2, Pallas kernels, triangle(): pl.pallas_call(functools.partial(triangle_kernel, group, tile, out_type),...  25.5 us
    ppermute x7, waiting for transfers between devices, swap(): return lax.ppermute(x, 'ax', [(s, s ^ bit) for s in range(n_ax)])  24 us
    ppermute x7, starting transfers between devices, swap(): return lax.ppermute(x, 'ax', [(s, s ^ bit) for s in range(n_ax)])  13.4 us
    pallas_call x1, Pallas kernels, body(): pl.pallas_call(right_kernel, grid_spec=pltpu.PrefetchScalarGridSpec(num_s...  3.86 us
    reshape x1, local copies, waits for them, and re-layouts, for_other_core(): part = lax.dynamic_slice(blocks, (0, 0, parity, 1 - nr, 0, 0), (rows, n_a...  3.59 us
    pallas_call x1, Pallas kernels, body(): pl.pallas_call(functools.partial(final_kernel, len(pieces)), in_specs=[vm...  2.13 us
  transfers between devices with their start and end apart: 11, of which 6 were waited for; matrix products, arithmetic and copies ran while one was open for 3% of the time, Pallas kernels for 38%

profile of v1, /device:TPU:0, one launch (start us, length us, event | category | flops | bytes accessed | tf_op | source)
XLA Modules:
  0.0 77.4 jit_solution(2899122100831103318)
XLA Ops:
  0.1 3.6 %dynamic-slice_bitcast_fusion = (bf16[32,4,32,128]{3,2,1,0:T(8,128)(2,1)}, bf16[32,4,32,128]{3,2,1,0:T(8,128)(2,1)}) fusion(bf16[32,4,2,2,32,128]{5,4,3,2,1,0:T(8,128)(2,1)} %bitcast.32, s32[]{:T(128)S(6)} %select_n.20, s32[]{:T(128)S(6)} %select_n.17, s32[]{:T(128)S(6)} %select_n.16), kind=kLoop, calls=%fused_computation | loop fusion | bytes 4194316 | tf_op jit(solution)/shard_map/reshape | solution.py:154
  3.6 0.5 collective-permute-start.3
  4.8 1.2 %constant_dynamic-slice_fusion.own_band = bf16[32,48,128]{2,1,0:T(8,128)(2,1)S(1)} fusion(bf16[32,512,128]{2,1,0:T(8,128)(2,1)} %param.11, s32[]{:T(128)S(6)} %select_n.18), kind=kLoop, calls=%fused_computation.6 | loop fusion | bytes 786436 | tf_op jit(solution)/shard_map/dynamic_slice | solution.py:147
  5.9 0.1 collective-permute-start.2
  6.0 0.1 copy.13
  6.2 0.1 copy.14
  6.3 0.5 collective-permute-start.1
  6.8 0.1 collective-permute-start
  6.9 0.1 stack.19.meta.refs_7_
  7.0 0.1 dynamic-slice_convert_fusion
  7.1 0.8 collective-permute-done.1.w_other.refs_15_.refs_6_
  7.8 0.1 broadcast_in_dim.24.row_mask
  7.9 0.1 broadcast_in_dim.10.chain_cols.refs_8_.refs_9_.refs_10_.refs_11_
  8.1 3.9 %right.1 = (bf16[128,48,64]{2,1,0:T(8,128)(2,1)S(1)}, f32[48,32,128]{2,1,0:T(8,128)S(1)}) custom-call(s32[512]{0:T(512)S(1)} %copy-done, s32[512]{0:T(512)S(1)} %copy-done.1, s32[5]{0:T(128)S(1)} %stack.19.meta.refs_7_, bf16[32,48,128]{2,1,0:T(8,128)(2,1)S(1)} %constant_dynamic-slice_fusion.own_band, ...), custom_call_target="tpu_custom_call" | custom-call | flops 4000000000 | bytes 2000000 | tf_op jit(solution)/shard_map/right/pallas_call | solution.py:166
  12.0 12.3 %triangle.3 = (bf16[48,32,128]{2,1,0:T(8,128)(2,1)S(1)}, bf16[48,32,128]{2,1,0:T(8,128)(2,1)S(1)}, bf16[48,32,128]{2,1,0:T(8,128)(2,1)S(1)}, bf16[48,32,128]{2,1,0:T(8,128)(2,1)S(1)}) custom-call(s32[512]{0:T(512)S(1)} %copy-done, s32[512]{0:T(512)S(1)} %copy-done.1, s32[5]{0:T(128)S(1)} %stack.19.meta.refs_7_, bf16[32,16,32,128]{3,2,1,0:T(8,128)(2,1)} %bitcast.33, ...), custom_call_target="tpu_custom_call" | custom-call | flops 8000000000 | bytes 4000000 | tf_op jit(solution)/shard_map/triangle/pallas_call | solution.py:198
  24.3 2.9 %collective-permute-start.5 = (bf16[48,32,128]{2,1,0:T(8,128)(2,1)S(1)}, bf16[48,32,128]{2,1,0:T(8,128)(2,1)S(1)}, u32[]{:S(2)}, u32[]{:S(2)}) collective-permute-start(bf16[48,32,128]{2,1,0:T(8,128)(2,1)S(1)} %get-tuple-element.19), channel_id=1, source_target_pairs={{0,2},{2,0},{4,6},{6,4},{8,10},{10,8},{12,14},{14,12},{1,3},{3,1},... | collective-permute-start | bytes 1179656 | tf_op jit(solution)/shard_map/ppermute | solution.py:139
  27.2 0.1 collective-permute-start.6
  27.3 1.9 %collective-permute-start.9 = (bf16[48,32,128]{2,1,0:T(8,128)(2,1)S(1)}, bf16[48,32,128]{2,1,0:T(8,128)(2,1)S(1)}, u32[]{:S(2)}, u32[]{:S(2)}) collective-permute-start(bf16[48,32,128]{2,1,0:T(8,128)(2,1)S(1)} %get-tuple-element.23), channel_id=1, source_target_pairs={{0,2},{2,0},{4,6},{6,4},{8,10},{10,8},{12,14},{14,12},{1,3},{3,1},... | collective-permute-start | bytes 1179656 | tf_op jit(solution)/shard_map/ppermute | solution.py:139
  29.2 13.1 %triangle.2 = (f32[48,32,128]{2,1,0:T(8,128)S(1)}, f32[48,32,128]{2,1,0:T(8,128)S(1)}, f32[48,32,128]{2,1,0:T(8,128)S(1)}, f32[48,32,128]{2,1,0:T(8,128)S(1)}) custom-call(s32[512]{0:T(512)S(1)} %copy-done, s32[512]{0:T(512)S(1)} %copy-done.1, s32[5]{0:T(128)S(1)} %stack.19.meta.refs_7_, bf16[32,16,32,128]{3,2,1,0:T(8,128)(2,1)} %bitcast.37, ...), custom_call_target="tpu_custom_call" | custom-call | flops 8000000000 | bytes 4000000 | tf_op jit(solution)/shard_map/triangle/pallas_call | solution.py:198
  42.4 3.1 %collective-permute-done.6 = bf16[48,32,128]{2,1,0:T(8,128)(2,1)S(1)} collective-permute-done((bf16[48,32,128]{2,1,0:T(8,128)(2,1)S(1)}, bf16[48,32,128]{2,1,0:T(8,128)(2,1)S(1)}, u32[]{:S(2)}, u32[]{:S(2)}) %collective-permute-start.6) | collective-permute-done | bytes 393248 | tf_op jit(solution)/shard_map/ppermute | solution.py:139
  45.5 0.1 add_convert_fusion.2
  45.6 2.2 %collective-permute-start.7 = (bf16[48,32,128]{2,1,0:T(8,128)(2,1)S(1)}, bf16[48,32,128]{2,1,0:T(8,128)(2,1)S(1)}, u32[]{:S(2)}, u32[]{:S(2)}) collective-permute-start(bf16[48,32,128]{2,1,0:T(8,128)(2,1)S(1)} %add_convert_fusion.2), channel_id=1, source_target_pairs={{0,4},{2,6},{4,0},{6,2},{8,12},{10,14},{12,8},{14,10},{1,5},{3,7},... | collective-permute-start | bytes 1179656 | tf_op jit(solution)/shard_map/ppermute | solution.py:139
  47.8 1.5 %collective-permute-start.4 = (bf16[48,32,128]{2,1,0:T(8,128)(2,1)S(1)}, bf16[48,32,128]{2,1,0:T(8,128)(2,1)S(1)}, u32[]{:S(2)}, u32[]{:S(2)}) collective-permute-start(bf16[48,32,128]{2,1,0:T(8,128)(2,1)S(1)} %get-tuple-element.17), channel_id=1, source_target_pairs={{0,2},{2,0},{4,6},{6,4},{8,10},{10,8},{12,14},{14,12},{1,3},{3,1},... | collective-permute-start | bytes 1179656 | tf_op jit(solution)/shard_map/ppermute | solution.py:139
  49.3 4.6 %collective-permute-done.9 = bf16[48,32,128]{2,1,0:T(8,128)(2,1)S(1)} collective-permute-done((bf16[48,32,128]{2,1,0:T(8,128)(2,1)S(1)}, bf16[48,32,128]{2,1,0:T(8,128)(2,1)S(1)}, u32[]{:S(2)}, u32[]{:S(2)}) %collective-permute-start.9) | collective-permute-done | bytes 393248 | tf_op jit(solution)/shard_map/ppermute | solution.py:139
  53.9 0.1 add_convert_fusion
  54.1 2.2 %collective-permute-start.10 = (bf16[48,32,128]{2,1,0:T(8,128)(2,1)S(1)}, bf16[48,32,128]{2,1,0:T(8,128)(2,1)S(1)}, u32[]{:S(2)}, u32[]{:S(2)}) collective-permute-start(bf16[48,32,128]{2,1,0:T(8,128)(2,1)S(1)} %add_convert_fusion), channel_id=1, source_target_pairs={{0,4},{2,6},{4,0},{6,2},{8,12},{10,14},{12,8},{14,10},{1,5},{3,7},... | collective-permute-start | bytes 1179656 | tf_op jit(solution)/shard_map/ppermute | solution.py:139
  56.2 0.2 add_convert_fusion.1
  56.4 2.7 %collective-permute-start.8 = (bf16[48,32,128]{2,1,0:T(8,128)(2,1)S(1)}, bf16[48,32,128]{2,1,0:T(8,128)(2,1)S(1)}, u32[]{:S(2)}, u32[]{:S(2)}) collective-permute-start(bf16[48,32,128]{2,1,0:T(8,128)(2,1)S(1)} %add_convert_fusion.1), channel_id=1, source_target_pairs={{0,8},{2,10},{4,12},{6,14},{8,0},{10,2},{12,4},{14,6},{1,9},{3,11}... | collective-permute-start | bytes 1179656 | tf_op jit(solution)/shard_map/ppermute | solution.py:139
  59.1 2.9 %collective-permute-done.4.refs_0_ = bf16[48,32,128]{2,1,0:T(8,128)(2,1)S(1)} collective-permute-done((bf16[48,32,128]{2,1,0:T(8,128)(2,1)S(1)}, bf16[48,32,128]{2,1,0:T(8,128)(2,1)S(1)}, u32[]{:S(2)}, u32[]{:S(2)}) %collective-permute-start.4) | collective-permute-done | bytes 393248 | tf_op jit(solution)/shard_map/ppermute | solution.py:139
  62.0 10.6 %collective-permute-done.10.refs_2_ = bf16[48,32,128]{2,1,0:T(8,128)(2,1)S(1)} collective-permute-done((bf16[48,32,128]{2,1,0:T(8,128)(2,1)S(1)}, bf16[48,32,128]{2,1,0:T(8,128)(2,1)S(1)}, u32[]{:S(2)}, u32[]{:S(2)}) %collective-permute-start.10) | collective-permute-done | bytes 393248 | tf_op jit(solution)/shard_map/ppermute | solution.py:139
  72.5 2.7 %collective-permute-done.8.refs_1_ = bf16[48,32,128]{2,1,0:T(8,128)(2,1)S(1)} collective-permute-done((bf16[48,32,128]{2,1,0:T(8,128)(2,1)S(1)}, bf16[48,32,128]{2,1,0:T(8,128)(2,1)S(1)}, u32[]{:S(2)}, u32[]{:S(2)}) %collective-permute-start.8) | collective-permute-done | bytes 393248 | tf_op jit(solution)/shard_map/ppermute | solution.py:139
  75.3 2.1 %final.1 = bf16[32,48,128]{2,1,0:T(8,128)(2,1)} custom-call(f32[48,32,128]{2,1,0:T(8,128)S(1)} %get-tuple-element.16.keep_ref, bf16[48,32,128]{2,1,0:T(8,128)(2,1)S(1)} %collective-permute-done.4.refs_0_, bf16[48,32,128]{2,1,0:T(8,128)(2,1)S(1)} %collective-permute-done.8.refs_1_, bf16[48,32,128]{2,1,0:T(8,128)(2,1)S(1)} %collective-permute-done.10.refs_2_, ...), custom_call_target="tpu_custom_call" | custom-call | flops 1000000000 | bytes 3000000 | tf_op jit(solution)/shard_map/final/pallas_call | solution.py:242
  (26 shorter events, 0.1 us)
Async XLA Ops:
  0.0 6.0 %copy-start.6 = (bf16[128,128]{1,0:T(8,128)(2,1)S(1)}, bf16[128,128]{1,0:T(8,128)(2,1)}, u32[]{:S(2)}) copy-start(bf16[128,128]{1,0:T(8,128)(2,1)} %param.18) | copy-start | bytes 98308
  0.0 6.2 %copy-start.7 = (bf16[128,128]{1,0:T(8,128)(2,1)S(1)}, bf16[128,128]{1,0:T(8,128)(2,1)}, u32[]{:S(2)}) copy-start(bf16[128,128]{1,0:T(8,128)(2,1)} %param.19) | copy-start | bytes 98308
  0.0 6.3 %copy-start.8 = (bf16[128,64]{0,1:T(8,128)(2,1)S(1)}, bf16[128,64]{0,1:T(8,128)(2,1)}, u32[]{:S(2)}) copy-start(bf16[128,64]{0,1:T(8,128)(2,1)} %param.21) | copy-start | bytes 49156
  0.0 6.3 %copy-start.9 = (bf16[128,64]{0,1:T(8,128)(2,1)S(1)}, bf16[128,64]{0,1:T(8,128)(2,1)}, u32[]{:S(2)}) copy-start(bf16[128,64]{0,1:T(8,128)(2,1)} %param.20) | copy-start | bytes 49156
  0.0 7.0 %copy-start.1 = (s32[512]{0:T(512)S(1)}, s32[512]{0:T(512)}, u32[]{:S(2)}) copy-start(s32[512]{0:T(512)} %mask_s.5) | copy-start | bytes 6148
  0.0 8.0 %copy-start.3 = (f32[128]{0:T(128)S(1)}, f32[128]{0:T(128)}, u32[]{:S(2)}) copy-start(f32[128]{0:T(128)} %param.16) | copy-start | bytes 1540
  0.0 8.0 %copy-start.2 = (f32[128]{0:T(128)S(1)}, f32[128]{0:T(128)}, u32[]{:S(2)}) copy-start(f32[128]{0:T(128)} %param.15) | copy-start | bytes 1540
  0.0 7.9 %copy-start = (s32[512]{0:T(512)S(1)}, s32[512]{0:T(512)}, u32[]{:S(2)}) copy-start(s32[512]{0:T(512)} %chain_s.5) | copy-start | bytes 6148
  3.6 8.3 %collective-permute-start.3 = (bf16[32,4,32,128]{3,2,1,0:T(8,128)(2,1)}, bf16[32,4,32,128]{3,2,1,0:T(8,128)(2,1)S(1)}, u32[]{:S(2)}, u32[]{:S(2)}) collective-permute-start(bf16[32,4,32,128]{3,2,1,0:T(8,128)(2,1)} %get-tuple-element.25), channel_id=1, source_target_pairs={{0,1},{1,0},{2,3},{3,2},{4,5},{5,4},{6,7},{7,6},{8,9},{9,8},{10,11... | collective-permute-start | bytes 3145736 | tf_op jit(solution)/shard_map/ppermute | solution.py:136
  5.9 1.9 %collective-permute-start.2 = (bf16[32,48,128]{2,1,0:T(8,128)(2,1)S(1)}, bf16[32,48,128]{2,1,0:T(8,128)(2,1)S(1)}, u32[]{:S(2)}, u32[]{:S(2)}) collective-permute-start(bf16[32,48,128]{2,1,0:T(8,128)(2,1)S(1)} %constant_dynamic-slice_fusion.own_band), channel_id=1, source_target_pairs={{0,1},{1,0},{2,3},{3,2},{4,5},{5,4},{6,7},{7,6},{8,9},{9,8},{10,11... | collective-permute-start | bytes 1179656 | tf_op jit(solution)/shard_map/ppermute | solution.py:136
  6.3 1.5 %collective-permute-start.1 = (bf16[384,128]{1,0:T(8,128)(2,1)S(1)}, bf16[384,128]{1,0:T(8,128)(2,1)S(1)}, u32[]{:S(2)}, u32[]{:S(2)}) collective-permute-start(bf16[384,128]{1,0:T(8,128)(2,1)S(1)} %pad_maximum_fusion.w_own.refs_14_.refs_5_), channel_id=1, source_target_pairs={{0,1},{1,0},{2,3},{3,2},{4,5},{5,4},{6,7},{7,6},{8,9},{9,8},{10,11... | collective-permute-start | bytes 294920 | tf_op jit(solution)/shard_map/ppermute | solution.py:136
  6.8 22.4 %collective-permute-start = (bf16[32,4,32,128]{3,2,1,0:T(8,128)(2,1)}, bf16[32,4,32,128]{3,2,1,0:T(8,128)(2,1)S(1)}, u32[]{:S(2)}, u32[]{:S(2)}) collective-permute-start(bf16[32,4,32,128]{3,2,1,0:T(8,128)(2,1)} %get-tuple-element.26), channel_id=1, source_target_pairs={{0,1},{1,0},{2,3},{3,2},{4,5},{5,4},{6,7},{7,6},{8,9},{9,8},{10,11... | collective-permute-start | bytes 3145736 | tf_op jit(solution)/shard_map/ppermute | solution.py:136
  11.9 12.4 %copy-start.5 = (bf16[128,48,64]{2,1,0:T(8,128)(2,1)}, bf16[128,48,64]{2,1,0:T(8,128)(2,1)S(1)}, u32[]{:S(2)}) copy-start(bf16[128,48,64]{2,1,0:T(8,128)(2,1)S(1)} %get-tuple-element.15.refs_16_) | copy-start | bytes 2359300
  24.3 31.9 %collective-permute-start.5 = (bf16[48,32,128]{2,1,0:T(8,128)(2,1)S(1)}, bf16[48,32,128]{2,1,0:T(8,128)(2,1)S(1)}, u32[]{:S(2)}, u32[]{:S(2)}) collective-permute-start(bf16[48,32,128]{2,1,0:T(8,128)(2,1)S(1)} %get-tuple-element.19), channel_id=1, source_target_pairs={{0,2},{2,0},{4,6},{6,4},{8,10},{10,8},{12,14},{14,12},{1,3},{3,1},... | collective-permute-start | bytes 1179656 | tf_op jit(solution)/shard_map/ppermute | solution.py:139
  27.2 18.3 %collective-permute-start.6 = (bf16[48,32,128]{2,1,0:T(8,128)(2,1)S(1)}, bf16[48,32,128]{2,1,0:T(8,128)(2,1)S(1)}, u32[]{:S(2)}, u32[]{:S(2)}) collective-permute-start(bf16[48,32,128]{2,1,0:T(8,128)(2,1)S(1)} %get-tuple-element.21), channel_id=1, source_target_pairs={{0,2},{2,0},{4,6},{6,4},{8,10},{10,8},{12,14},{14,12},{1,3},{3,1},... | collective-permute-start | bytes 1179656 | tf_op jit(solution)/shard_map/ppermute | solution.py:139
  27.3 26.7 %collective-permute-start.9 = (bf16[48,32,128]{2,1,0:T(8,128)(2,1)S(1)}, bf16[48,32,128]{2,1,0:T(8,128)(2,1)S(1)}, u32[]{:S(2)}, u32[]{:S(2)}) collective-permute-start(bf16[48,32,128]{2,1,0:T(8,128)(2,1)S(1)} %get-tuple-element.23), channel_id=1, source_target_pairs={{0,2},{2,0},{4,6},{6,4},{8,10},{10,8},{12,14},{14,12},{1,3},{3,1},... | collective-permute-start | bytes 1179656 | tf_op jit(solution)/shard_map/ppermute | solution.py:139
  42.4 32.9 %copy-start.4 = (f32[128]{0:T(128)S(1)}, f32[128]{0:T(128)}, u32[]{:S(2)}) copy-start(f32[128]{0:T(128)} %param.17) | copy-start | bytes 1540
  45.6 10.6 %collective-permute-start.7 = (bf16[48,32,128]{2,1,0:T(8,128)(2,1)S(1)}, bf16[48,32,128]{2,1,0:T(8,128)(2,1)S(1)}, u32[]{:S(2)}, u32[]{:S(2)}) collective-permute-start(bf16[48,32,128]{2,1,0:T(8,128)(2,1)S(1)} %add_convert_fusion.2), channel_id=1, source_target_pairs={{0,4},{2,6},{4,0},{6,2},{8,12},{10,14},{12,8},{14,10},{1,5},{3,7},... | collective-permute-start | bytes 1179656 | tf_op jit(solution)/shard_map/ppermute | solution.py:139
  47.8 14.2 %collective-permute-start.4 = (bf16[48,32,128]{2,1,0:T(8,128)(2,1)S(1)}, bf16[48,32,128]{2,1,0:T(8,128)(2,1)S(1)}, u32[]{:S(2)}, u32[]{:S(2)}) collective-permute-start(bf16[48,32,128]{2,1,0:T(8,128)(2,1)S(1)} %get-tuple-element.17), channel_id=1, source_target_pairs={{0,2},{2,0},{4,6},{6,4},{8,10},{10,8},{12,14},{14,12},{1,3},{3,1},... | collective-permute-start | bytes 1179656 | tf_op jit(solution)/shard_map/ppermute | solution.py:139
  54.1 18.5 %collective-permute-start.10 = (bf16[48,32,128]{2,1,0:T(8,128)(2,1)S(1)}, bf16[48,32,128]{2,1,0:T(8,128)(2,1)S(1)}, u32[]{:S(2)}, u32[]{:S(2)}) collective-permute-start(bf16[48,32,128]{2,1,0:T(8,128)(2,1)S(1)} %add_convert_fusion), channel_id=1, source_target_pairs={{0,4},{2,6},{4,0},{6,2},{8,12},{10,14},{12,8},{14,10},{1,5},{3,7},... | collective-permute-start | bytes 1179656 | tf_op jit(solution)/shard_map/ppermute | solution.py:139
  56.4 18.9 %collective-permute-start.8 = (bf16[48,32,128]{2,1,0:T(8,128)(2,1)S(1)}, bf16[48,32,128]{2,1,0:T(8,128)(2,1)S(1)}, u32[]{:S(2)}, u32[]{:S(2)}) collective-permute-start(bf16[48,32,128]{2,1,0:T(8,128)(2,1)S(1)} %add_convert_fusion.1), channel_id=1, source_target_pairs={{0,8},{2,10},{4,12},{6,14},{8,0},{10,2},{12,4},{14,6},{1,9},{3,11}... | collective-permute-start | bytes 1179656 | tf_op jit(solution)/shard_map/ppermute | solution.py:139

commit v2 on v1

v2 whole, which is shorter than its diff:
```python
import functools

import jax
import jax.numpy as jnp
from jax import lax
from jax.experimental import pallas as pl
from jax.experimental.pallas import tpu as pltpu
from jax.sharding import PartitionSpec as P

BAND = 48
NORM_EPS = 1e-05
GROUP = 4
F32, BF16, I32 = jnp.float32, jnp.bfloat16, jnp.int32
LAST = (((1,), (1,)), ((), ()))


def layer_norm(values, gain):
    mean = jnp.mean(values, -1, keepdims=True)
    centered = values - mean
    var = jnp.mean(centered * centered, -1, keepdims=True)
    return centered * lax.rsqrt(var + NORM_EPS) * gain


def place_of(label, ax, nr):
    swapped = (label & ~3) | ((label & 1) << 1) | ((label >> 1) & 1)
    return ax ^ (label + (swapped - label) * nr)


def pack_kernel(far_labels, near_labels, meta, pairs, weights, first, far, near, sems):
    window = first.shape[1] - 16
    ax, other = meta[0], 1 - meta[1]
    base = pl.multiple_of(meta[5], 16)
    copies = [pltpu.make_async_copy(pairs.at[:, pl.ds(base, window), :], first.at[:, 0:window, :], sems.at[0])]
    size = far.shape[2]
    for part, labels in ((far, far_labels), (near, near_labels)):
        for m, label in enumerate(labels):
            block = place_of(label, ax, other) * 2 + other
            rows = pl.ds(pl.multiple_of(block * size, size), size)
            copies.append(pltpu.make_async_copy(pairs.at[:, rows, :], part.at[:, m], sems.at[len(copies)]))
    for copy in copies:
        copy.start()
    half = weights.shape[0] // 3
    turned = [weights[n * half : (n + 1) * half].astype(F32).T.astype(BF16) for n in range(2)] + [weights[2 * half :]]
    turned = jnp.concatenate(turned + turned[:1], 0)
    for row in range(first.shape[0]):
        first[row, window:, :] = turned[row * 16 : row * 16 + 16]
    for copy in copies:
        copy.wait()


def right_kernel(
    chain_s, mask_s, meta, own, other, chain_cols, embed, gain, right_ref, w_left_ref, w_gate_ref, w_out_ref, band_ref,
    normed_scr, right_scr,
):
    rows, window, width = own.shape
    window -= 16
    band = BAND
    both = 2 * rows
    pitch, turn = window + 8, band + 8
    base = pl.multiple_of(meta[5], 16)
    offset = meta[4] - meta[5]
    first = meta[1] == 0
    chains = chain_cols[pl.ds(base, window), :]
    emb, gn = embed[...], gain[...]
    w_own = own[:, window:, :].reshape(rows * 16, width)
    w_other = other[:, window:, :].reshape(rows * 16, width)
    low, high = jnp.where(first, w_own, w_other), jnp.where(first, w_other, w_own)

    def weight(start, size):
        return jnp.concatenate([low[start : start + size], high[start : start + size]], 0)

    w_left_ref[...] = weight(0, width)
    w_right = weight(width, width)
    w_gate_ref[...] = weight(2 * width, width // 2)
    w_out_ref[...] = weight(2 * width + width // 2, width // 2)
    for source, start, ref in ((0, meta[2], own), (1, meta[3], other)):
        for k in range(rows):
            same = chains == chain_s[start + k]
            shifted = ref[k, 0:window].astype(F32) + jnp.where(same, emb, 0.0)
            keep = mask_s[start + k].astype(F32)
            row = (source * rows + k) * pitch
            normed_scr[row : row + window, :] = layer_norm(shifted, gn * keep)
    channel = lax.broadcasted_iota(I32, (width, 2 * both), 0)
    lane = lax.broadcasted_iota(I32, (width, 2 * both), 1)
    spread = ((channel & 1) == lane // both).astype(F32)
    for j in range(0, band, 2):
        normed = [normed_scr[pl.ds(offset + j + u, both, stride=pitch), :].astype(BF16) for u in range(2)]
        doubled = jnp.concatenate([normed[0], normed[0], normed[1], normed[1]], 0)
        proj = lax.dot_general(w_right, doubled, LAST, preferred_element_type=F32)
        edge = jax.nn.sigmoid(proj[:width]) * proj[width:]
        for u in range(2):
            keep = spread * mask_s[meta[4] + j + u].astype(F32)
            right_scr[pl.ds(j + u, width, stride=turn), :] = edge[:, u * 2 * both : (u + 1) * 2 * both] * keep
            band_ref[j + u] = normed[u][0:rows]
    for g in range(width // 2):
        pair = [right_scr[(2 * g + u) * turn : (2 * g + u) * turn + band, :] for u in range(2)]
        right_ref[g] = jnp.concatenate(pair, 0).astype(BF16)


def gate_kernel(band_ref, w_gate, mask_i, gate_ref):
    band, rows, width = band_ref.shape
    gate = lax.dot_general(band_ref[...].reshape(band * rows, width), w_gate[...], LAST, preferred_element_type=F32)
    gate_ref[...] = jax.nn.sigmoid(gate).reshape(band, rows, width) * mask_i[...][None]


def triangle_kernel(group, tile, stack, out_type, chain_s, mask_s, meta, *refs):
    own = refs[:group]
    other = refs[group : 2 * group]
    chain_cols = refs[2 * group : 3 * group]
    embed, gain, w_left_ref, right_ref = refs[3 * group : 3 * group + 4]
    outs = refs[3 * group + 4 : -2]
    left_scr, tri_scr = refs[-2:]
    pairs, wide, both2 = right_ref.shape
    width, band, both = pairs * 2, wide // 2, both2 // 2
    rows = both // 2
    pitch, turn = both + 8, band + 8
    size = own[0].shape[2]
    lanes = group * size
    step = pl.program_id(0)
    w_left = w_left_ref[...]
    chains = jnp.concatenate([ref[...] for ref in chain_cols], 0)
    emb, gn = embed[...], gain[...]

    def normed(source, k):
        base = meta[3] if source else meta[2]
        values = jnp.concatenate([ref[k, 0] for ref in (other if source else own)], 0)
        same = chains == chain_s[base + step * tile + k]
        return layer_norm(values.astype(F32) + jnp.where(same, emb, 0.0), gn).astype(BF16)

    for k in range(tile):
        pair = jnp.concatenate([normed(0, k), normed(1, k)], 0)
        proj = lax.dot_general(w_left, pair, LAST, preferred_element_type=F32)
        edge = jax.nn.sigmoid(proj[:width]) * proj[width:]
        at = step * tile + k
        left_scr[pl.ds(at, width, stride=pitch), :] = edge[:, :lanes]
        left_scr[pl.ds(at + rows, width, stride=pitch), :] = edge[:, lanes:]

    @pl.when(step == pl.num_programs(0) - 1)
    def _():
        for g in range(pairs):
            left = jnp.concatenate([left_scr[c * pitch : c * pitch + both, :] for c in (2 * g, 2 * g + 1)], 0)
            tri = jnp.dot(right_ref[g], left.astype(BF16), preferred_element_type=F32)
            tri_scr[2 * g * turn : 2 * g * turn + band, :] = tri[:band]
            tri_scr[(2 * g + 1) * turn : (2 * g + 1) * turn + band, :] = tri[band:]
        for j in range(band):
            turned = tri_scr[pl.ds(j, width, stride=turn), :].T
            for b in range(group):
                outs[b // stack][b % stack * band + j] = turned[b * size : (b + 1) * size].astype(out_type)


def final_kernel(starts, *refs):
    pieces = refs[: len(starts)]
    gate_ref, gain, w_out, out_ref, scr = refs[len(starts) :]
    band, rows, width = gate_ref.shape
    turn = band + 8
    total = pieces[0][...]
    for ref, start in zip(pieces[1:], starts[1:]):
        total = total + ref[start : start + band].astype(F32)
    normed = layer_norm(total.reshape(band * rows, width), gain[...]).astype(BF16)
    projected = lax.dot_general(normed, w_out[...], LAST, preferred_element_type=F32)
    for j in range(band):
        scr[pl.ds(j, rows, stride=turn), :] = projected[j * rows : (j + 1) * rows] * gate_ref[j]
    for i in range(rows):
        out_ref[i] = scr[i * turn : i * turn + band, :].astype(BF16)


def body(pair_map, chain_ids, token_mask, band_start, chain_embed, gain_in, gain_out, w_left, w_right, w_gate, w_out):
    rows, tokens, width = pair_map.shape
    n_ax = lax.axis_size("ax")
    ax, nr = lax.axis_index("ax"), lax.axis_index("nr")
    band, tile = BAND, 8
    odd, even = list(range(n_ax - 1, 0, -2)), list(range(n_ax - 2, -1, -2))
    both = 2 * rows
    window = band + 16
    vmem = pl.BlockSpec(memory_space=pltpu.VMEM)
    smem = pl.BlockSpec(memory_space=pltpu.SMEM)
    hbm = pl.BlockSpec(memory_space=pltpu.HBM)

    def swap_core(x):
        return lax.ppermute(x, "nr", [(0, 1), (1, 0)])

    def swap(x, bit):
        pairs = []
        for s in range(n_ax):
            for core in range(2):
                pairs.append((s * 2 + core, place_of(bit, s, core) * 2 + core))
        return lax.ppermute(x, ("ax", "nr"), pairs)

    def after(x, done):
        return lax.optimization_barrier((x, done))[0]

    start = band_start[0]
    own_row, other_row = (ax * 2 + nr) * rows, (ax * 2 + 1 - nr) * rows
    meta = jnp.stack([ax, nr, own_row, other_row, start, jnp.minimum(start // 16 * 16, tokens - window)]).astype(I32)

    part_shape = jax.ShapeDtypeStruct((rows, n_ax // 2, rows, width), BF16)
    weights = jnp.concatenate([w_left, w_right, w_gate.T, w_out.T], 0)
    own_first, far, near = pl.pallas_call(
        functools.partial(pack_kernel, odd, even),
        in_specs=[smem, hbm, vmem],
        out_specs=[vmem] * 3,
        out_shape=[jax.ShapeDtypeStruct((rows, window + 16, width), BF16), part_shape, part_shape],
        scratch_shapes=[pltpu.SemaphoreType.DMA((1 + n_ax,))],
        compiler_params=pltpu.CompilerParams(vmem_limit_bytes=10 << 20),
        name="pack",
    )(meta, pair_map, weights)
    other_first, other_far, other_near = swap_core(own_first), swap_core(far), swap_core(near)
    own_blocks = pair_map.reshape(rows, tokens // rows, rows, width)
    chain_cols = jnp.broadcast_to(chain_ids[:, None], (tokens, 128))
    row_mask = jnp.broadcast_to(
        lax.dynamic_slice_in_dim(token_mask, own_row, rows).astype(F32)[:, None], (rows, width)
    )
    embed, gain, gain_o = chain_embed[None], gain_in[None], gain_out[None]

    right, w_left, w_gate, w_out, own_band = pl.pallas_call(
        right_kernel,
        grid_spec=pltpu.PrefetchScalarGridSpec(
            num_scalar_prefetch=3,
            grid=(),
            in_specs=[vmem] * 5,
            out_specs=[vmem] * 5,
            scratch_shapes=[
                pltpu.VMEM((both * (window + 8), width), F32),
                pltpu.VMEM((width * (band + 8), 2 * both), F32),
            ],
        ),
        out_shape=[
            jax.ShapeDtypeStruct((width // 2, 2 * band, 2 * both), BF16),
            jax.ShapeDtypeStruct((2 * width, width), BF16),
            jax.ShapeDtypeStruct((width, width), BF16),
            jax.ShapeDtypeStruct((width, width), BF16),
            jax.ShapeDtypeStruct((band, rows, width), BF16),
        ],
        compiler_params=pltpu.CompilerParams(vmem_limit_bytes=18 << 20),
        cost_estimate=pl.CostEstimate(flops=4 * 10**9, bytes_accessed=2 * 10**6, transcendentals=0),
        name="right",
    )(chain_ids, token_mask, meta, own_first, other_first, chain_cols, embed, gain)

    def triangle(labels, other_part, out_type, stack, scalars):
        group = len(labels)
        row_specs, part_specs, chain_specs = [], [], []
        for v in labels:
            row_specs.append(
                pl.BlockSpec(
                    (tile, 1, rows, width),
                    lambda t, c, m, meta, v=v: (t, place_of(v, meta[0], meta[1]) * 2 + meta[1], 0, 0),
                )
            )
            at = (odd if v & 1 else even).index(v)
            part_specs.append(pl.BlockSpec((tile, 1, rows, width), lambda t, c, m, meta, at=at: (t, at, 0, 0)))
            chain_specs.append(
                pl.BlockSpec((rows, 128), lambda t, c, m, meta, v=v: (place_of(v, meta[0], meta[1]) * 2 + meta[1], 0))
            )
        whole = lambda shape: pl.BlockSpec(shape, lambda t, c, m, meta: (0,) * len(shape))
        out_shape = (stack * band, rows, width)
        return pl.pallas_call(
            functools.partial(triangle_kernel, group, tile, stack, out_type),
            grid_spec=pltpu.PrefetchScalarGridSpec(
                num_scalar_prefetch=3,
                grid=(rows // tile,),
                in_specs=row_specs
                + part_specs
                + chain_specs
                + [whole((1, width)), whole((1, width)), whole(w_left.shape), whole(right.shape)],
                out_specs=[whole(out_shape)] * (group // stack),
                scratch_shapes=[
                    pltpu.VMEM((width * (both + 8), group * rows), F32),
                    pltpu.VMEM((width * (band + 8), group * rows), F32),
                ],
            ),
            out_shape=[jax.ShapeDtypeStruct(out_shape, out_type)] * (group // stack),
            compiler_params=pltpu.CompilerParams(vmem_limit_bytes=28 << 20),
            cost_estimate=pl.CostEstimate(flops=8 * 10**9, bytes_accessed=4 * 10**6, transcendentals=0),
            name="triangle",
        )(
            chain_ids, token_mask, scalars, *([own_blocks] * group), *([other_part] * group), *([chain_cols] * group),
            embed, gain, w_left, right,
        )

    size = GROUP
    pairs, kept = [], {}
    for at in range(0, len(odd), size):
        pairs += triangle(odd[at : at + size], other_far, BF16, 2, meta)
    for at in range(0, len(even), size):
        labels = even[at : at + size]
        kept.update(zip(labels, triangle(labels, other_near, F32, 1, after(meta, pairs[-1]))))
    gate = pl.pallas_call(
        gate_kernel,
        in_specs=[vmem] * 3,
        out_specs=vmem,
        out_shape=jax.ShapeDtypeStruct((band, rows, width), F32),
        compiler_params=pltpu.CompilerParams(vmem_limit_bytes=10 << 20),
        cost_estimate=pl.CostEstimate(flops=10**9, bytes_accessed=2 * 10**6, transcendentals=0),
        name="gate",
    )(own_band, w_gate, after(row_mask, kept[0]))

    arrived = {v: [(kept[v], 0)] for v in even}

    def send_pair(n, x):
        moved = swap(x, 1)
        for m in range(2):
            arrived[odd[2 * n + m] - 1].append((moved, m * band))

    def send(v):
        total = sum(piece[start : start + band].astype(F32) for piece, start in arrived[v])
        bit = v & -v
        arrived[v - bit].append((swap(total.astype(BF16), bit), 0))
        return arrived[v - bit][-1][0]

    send_pair(0, pairs[0])
    first_sent = send(even[0])
    for n in range(1, len(pairs)):
        send_pair(n, after(pairs[n], first_sent))
    for v in even[1:-1]:
        send(v)

    pieces, starts = zip(*arrived[0])
    return pl.pallas_call(
        functools.partial(final_kernel, starts),
        in_specs=[vmem] * (len(pieces) + 3),
        out_specs=vmem,
        out_shape=jax.ShapeDtypeStruct((rows, band, width), BF16),
        scratch_shapes=[pltpu.VMEM((rows * (band + 8), width), F32)],
        compiler_params=pltpu.CompilerParams(vmem_limit_bytes=14 << 20),
        cost_estimate=pl.CostEstimate(flops=10**9, bytes_accessed=3 * 10**6, transcendentals=0),
        name="final",
    )(*pieces, gate, gain_o, w_out)


def solution(mesh):
    in_specs = (
        P(("grp", "ax", "nr"), None, None),
        P("grp"),
        P("grp"),
        P("grp"),
        P(),
        P(),
        P(),
        P(None, "nr"),
        P(None, "nr"),
        P(None, "nr"),
        P(None, "nr"),
    )
    out_specs = P(("grp", "ax", "nr"), None, None)
    return jax.shard_map(body, mesh=mesh, in_specs=in_specs, out_specs=out_specs, check_vma=False)
```

time: 77.7 us -> 65.4 us (0.84)
  the two profiles are of different devices: /device:TPU:0 before, /device:TPU:1 now
where the time goes in v2:
time: 65.4 us; the launch traced here: 65.2 us
  waiting for transfers between devices  31.3 us (48%)
  Pallas kernels  18.9 us (29%)
  starting transfers between devices  9.51 us (15%)
  local copies, waits for them, and re-layouts  2.49 us (4%)
  other arithmetic  2.09 us (3%)
  between operations  0.86 us (1%)
    ppermute x5, waiting for transfers between devices, swap(): return lax.ppermute(x, ('ax', 'nr'), pairs)  28.3 us
    pallas_call x2, Pallas kernels, triangle(): pl.pallas_call(functools.partial(triangle_kernel, group, tile, stack, out...  13 us
    ppermute x5, starting transfers between devices, swap(): return lax.ppermute(x, ('ax', 'nr'), pairs)  8.86 us
    pallas_call x1, Pallas kernels, body(): pl.pallas_call(right_kernel, grid_spec=pltpu.PrefetchScalarGridSpec(num_s...  3.19 us
    ppermute x3, waiting for transfers between devices, swap_core(): return lax.ppermute(x, 'nr', [(0, 1), (1, 0)])  3.01 us
    unnamed x14, local copies, waits for them, and re-layouts  2.21 us
    pallas_call x1, Pallas kernels, body(): pl.pallas_call(functools.partial(final_kernel, starts), in_specs=[vmem] *...  1.47 us
  transfers between devices with their start and end apart: 8, of which 5 were waited for; matrix products, arithmetic and copies ran while one was open for 2% of the time, Pallas kernels for 25%

profile of v2, /device:TPU:1, one launch (start us, length us, event | category | flops | bytes accessed | tf_op | source)
XLA Modules:
  0.0 65.2 jit_solution(17624897899578158619)
XLA Ops:
  0.7 0.8 %pad_maximum_fusion.weights = bf16[384,128]{1,0:T(8,128)(2,1)S(1)} fusion(bf16[64,128]{1,0:T(8,128)(2,1)} %bitcast.31, bf16[64,128]{1,0:T(8,128)(2,1)} %bitcast.32, bf16[128,128]{1,0:T(8,128)(2,1)} %param.19, bf16[128,128]{1,0:T(8,128)(2,1)} %param.18), kind=kLoop, calls=%fused_computation.3 | loop fusion | flops 393216 | bytes 196608 | tf_op jit(solution)/shard_map/concatenate | solution.py:197
  1.6 0.1 stack.23.meta
  1.6 2.2 %copy-done = bf16[32,512,128]{2,1,0:T(8,128)(2,1)S(1)} copy-done((bf16[32,512,128]{2,1,0:T(8,128)(2,1)S(1)}, bf16[32,512,128]{2,1,0:T(8,128)(2,1)}, u32[]{:S(2)}) %copy-start) | copy-done | bytes 4194328
  3.8 1.0 %pack.1 = (bf16[32,80,128]{2,1,0:T(8,128)(2,1)S(1)}, bf16[32,4,32,128]{3,2,1,0:T(8,128)(2,1)S(1)}, bf16[32,4,32,128]{3,2,1,0:T(8,128)(2,1)S(1)}) custom-call(s32[6]{0:T(128)S(1)} %stack.23.meta, bf16[32,512,128]{2,1,0:T(8,128)(2,1)S(1)} %copy-done, bf16[384,128]{1,0:T(8,128)(2,1)S(1)} %pad_maximum_fusion.weights), custom_call_target="tpu_custom_call" | custom-call | tf_op jit(solution)/shard_map/pack/pallas_call | solution.py:198
  4.8 0.1 collective-permute-start
  4.9 0.4 collective-permute-start.1
  5.4 0.1 collective-permute-start.2
  5.5 3.0 %collective-permute-done.1.other = bf16[32,80,128]{2,1,0:T(8,128)(2,1)S(1)} collective-permute-done((bf16[32,80,128]{2,1,0:T(8,128)(2,1)S(1)}, bf16[32,80,128]{2,1,0:T(8,128)(2,1)S(1)}, u32[]{:S(2)}, u32[]{:S(2)}) %collective-permute-start.1) | collective-permute-done | bytes 655392 | tf_op jit(solution)/shard_map/ppermute | solution.py:180
  8.5 0.1 broadcast_in_dim.10.chain_cols.refs_8_.refs_9_.refs_10_.refs_11_
  8.6 0.0 copy-start.1
  8.6 3.2 %right.1 = (bf16[64,96,128]{2,1,0:T(8,128)(2,1)S(1)}, bf16[256,128]{1,0:T(8,128)(2,1)S(1)}, bf16[128,128]{1,0:T(8,128)(2,1)S(1)}, bf16[128,128]{1,0:T(8,128)(2,1)S(1)}, bf16[48,32,128]{2,1,0:T(8,128)(2,1)S(1)}) custom-call(s32[512]{0:T(512)S(1)} %copy-done.2, s32[512]{0:T(512)S(1)} %copy-done.3, s32[6]{0:T(128)S(1)} %stack.23.meta, ...), custom_call_target="tpu_custom_call" | custom-call | flops 4000000000 | bytes 2000000 | tf_op jit(solution)/shard_map/right/pallas_call | solution.py:215
  11.8 0.0 collective-permute-done.refs_4_.refs_5_.refs_6_.refs_7_
  11.9 6.3 %triangle.2 = (bf16[96,32,128]{2,1,0:T(8,128)(2,1)S(1)}, bf16[96,32,128]{2,1,0:T(8,128)(2,1)S(1)}) custom-call(s32[512]{0:T(512)S(1)} %copy-done.2, s32[512]{0:T(512)S(1)} %copy-done.3, s32[6]{0:T(128)S(1)} %stack.23.meta, bf16[32,16,32,128]{3,2,1,0:T(8,128)(2,1)S(1)} %bitcast.16, bf16[32,16,32,128]{3,2,1,0:T(8,128)(2,1)S(1)} %bitcast.17, ...), custom_call_target="tpu_custom_call" | custom-call | flops 8000000000 | bytes 4000000 | tf_op jit(solution)/shard_map/triangle/pallas_call | solution.py:256
  18.2 2.5 %collective-permute-start.3 = (bf16[96,32,128]{2,1,0:T(8,128)(2,1)S(1)}, bf16[96,32,128]{2,1,0:T(8,128)(2,1)S(1)}, u32[]{:S(2)}, u32[]{:S(2)}) collective-permute-start(bf16[96,32,128]{2,1,0:T(8,128)(2,1)S(1)} %get-tuple-element.31), channel_id=1, source_target_pairs={{0,2},{1,5},{2,0},{3,7},{4,6},{5,1},{6,4},{7,3},{8,10},{9,13},{10,... | collective-permute-start | bytes 2359304 | tf_op jit(solution)/shard_map/ppermute | solution.py:187
  20.7 0.0 collective-permute-done.2.refs_4_.refs_5_.refs_6_.refs_7_
  20.7 6.7 %triangle.3 = (f32[48,32,128]{2,1,0:T(8,128)S(1)}, f32[48,32,128]{2,1,0:T(8,128)S(1)}, f32[48,32,128]{2,1,0:T(8,128)S(1)}, f32[48,32,128]{2,1,0:T(8,128)S(1)}) custom-call(s32[512]{0:T(512)S(1)} %copy-done.2, s32[512]{0:T(512)S(1)} %copy-done.3, s32[6]{0:T(128)S(1)} %stack.23.meta, bf16[32,16,32,128]{3,2,1,0:T(8,128)(2,1)S(1)} %bitcast.20, ...), custom_call_target="tpu_custom_call" | custom-call | flops 8000000000 | bytes 4000000 | tf_op jit(solution)/shard_map/triangle/pallas_call | solution.py:256
  27.4 3.0 %collective-permute-done.3 = bf16[96,32,128]{2,1,0:T(8,128)(2,1)S(1)} collective-permute-done((bf16[96,32,128]{2,1,0:T(8,128)(2,1)S(1)}, bf16[96,32,128]{2,1,0:T(8,128)(2,1)S(1)}, u32[]{:S(2)}, u32[]{:S(2)}) %collective-permute-start.3) | collective-permute-done | bytes 786464 | tf_op jit(solution)/shard_map/ppermute | solution.py:187
  30.4 0.1 add_convert_fusion.2
  30.5 1.5 %collective-permute-start.4 = (bf16[48,32,128]{2,1,0:T(8,128)(2,1)S(1)}, bf16[48,32,128]{2,1,0:T(8,128)(2,1)S(1)}, u32[]{:S(2)}, u32[]{:S(2)}) collective-permute-start(bf16[48,32,128]{2,1,0:T(8,128)(2,1)S(1)} %add_convert_fusion.2), channel_id=1, source_target_pairs={{0,4},{1,3},{2,6},{3,1},{4,0},{5,7},{6,2},{7,5},{8,12},{9,11},{10,... | collective-permute-start | bytes 1179656 | tf_op jit(solution)/shard_map/ppermute | solution.py:187
  32.0 5.5 %collective-permute-done.4 = bf16[48,32,128]{2,1,0:T(8,128)(2,1)S(1)} collective-permute-done((bf16[48,32,128]{2,1,0:T(8,128)(2,1)S(1)}, bf16[48,32,128]{2,1,0:T(8,128)(2,1)S(1)}, u32[]{:S(2)}, u32[]{:S(2)}) %collective-permute-start.4) | collective-permute-done | bytes 393248 | tf_op jit(solution)/shard_map/ppermute | solution.py:187
  37.5 1.5 %collective-permute-start.5 = (bf16[96,32,128]{2,1,0:T(8,128)(2,1)S(1)}, bf16[96,32,128]{2,1,0:T(8,128)(2,1)S(1)}, u32[]{:S(2)}, u32[]{:S(2)}) collective-permute-start(bf16[96,32,128]{2,1,0:T(8,128)(2,1)S(1)} %get-tuple-element.32), channel_id=1, source_target_pairs={{0,2},{1,5},{2,0},{3,7},{4,6},{5,1},{6,4},{7,3},{8,10},{9,13},{10,... | collective-permute-start | bytes 2359304 | tf_op jit(solution)/shard_map/ppermute | solution.py:187
  39.0 0.9 %add_convert_fusion.1 = bf16[48,32,128]{2,1,0:T(8,128)(2,1)} fusion(bf16[48,32,128]{2,1,0:T(8,128)(2,1)S(1)} %collective-permute-done.4, f32[48,32,128]{2,1,0:T(8,128)S(1)} %get-tuple-element.33, bf16[96,32,128]{2,1,0:T(8,128)(2,1)S(1)} %collective-permute-done.3), kind=kLoop, calls=%fused_computation.1 | loop fusion | flops 983040 | bytes 1966080 | tf_op jit(solution)/shard_map/convert_element_type | solution.py:307
  39.9 2.3 %collective-permute-start.6 = (bf16[48,32,128]{2,1,0:T(8,128)(2,1)}, bf16[48,32,128]{2,1,0:T(8,128)(2,1)S(1)}, u32[]{:S(2)}, u32[]{:S(2)}) collective-permute-start(bf16[48,32,128]{2,1,0:T(8,128)(2,1)} %add_convert_fusion.1), channel_id=1, source_target_pairs={{0,8},{1,9},{2,10},{3,11},{4,12},{5,13},{6,14},{7,15},{8,0},{9,1},... | collective-permute-start | bytes 1179656 | tf_op jit(solution)/shard_map/ppermute | solution.py:187
  42.2 14.7 %collective-permute-done.5.refs_1_ = bf16[96,32,128]{2,1,0:T(8,128)(2,1)S(1)} collective-permute-done((bf16[96,32,128]{2,1,0:T(8,128)(2,1)S(1)}, bf16[96,32,128]{2,1,0:T(8,128)(2,1)S(1)}, u32[]{:S(2)}, u32[]{:S(2)}) %collective-permute-start.5) | collective-permute-done | bytes 786464 | tf_op jit(solution)/shard_map/ppermute | solution.py:187
  56.9 0.1 add_convert_fusion
  57.0 1.1 %collective-permute-start.7 = (bf16[48,32,128]{2,1,0:T(8,128)(2,1)S(1)}, bf16[48,32,128]{2,1,0:T(8,128)(2,1)S(1)}, u32[]{:S(2)}, u32[]{:S(2)}) collective-permute-start(bf16[48,32,128]{2,1,0:T(8,128)(2,1)S(1)} %add_convert_fusion), channel_id=1, source_target_pairs={{0,4},{1,3},{2,6},{3,1},{4,0},{5,7},{6,2},{7,5},{8,12},{9,11},{10,... | collective-permute-start | bytes 1179656 | tf_op jit(solution)/shard_map/ppermute | solution.py:187
  58.2 0.1 dynamic-slice_convert_fusion
  58.2 0.1 broadcast_in_dim.24.mask_i
  58.3 0.3 gate.1.refs_4_
  58.6 0.0 collective-permute-done.6.refs_2_
  58.6 5.1 %collective-permute-done.7.refs_3_ = bf16[48,32,128]{2,1,0:T(8,128)(2,1)S(1)} collective-permute-done((bf16[48,32,128]{2,1,0:T(8,128)(2,1)S(1)}, bf16[48,32,128]{2,1,0:T(8,128)(2,1)S(1)}, u32[]{:S(2)}, u32[]{:S(2)}) %collective-permute-start.7) | collective-permute-done | bytes 393248 | tf_op jit(solution)/shard_map/ppermute | solution.py:187
  63.7 1.5 %final.1 = bf16[32,48,128]{2,1,0:T(8,128)(2,1)} custom-call(f32[48,32,128]{2,1,0:T(8,128)S(1)} %get-tuple-element.29.refs_0_, bf16[96,32,128]{2,1,0:T(8,128)(2,1)S(1)} %collective-permute-done.5.refs_1_, bf16[48,32,128]{2,1,0:T(8,128)(2,1)S(1)} %collective-permute-done.6.refs_2_, bf16[48,32,128]{2,1,0:T(8,128)(2,1)S(1)} %collective-permute-done.7.refs_3_, ...), custom_call_target="tpu_custom_call" | custom-call | flops 1000000000 | bytes 3000000 | tf_op jit(solution)/shard_map/final/pallas_call | solution.py:318
  (12 shorter events, 0.0 us)
Async XLA Ops:
  0.0 8.5 %copy-start.2 = (s32[512]{0:T(512)S(1)}, s32[512]{0:T(512)}, u32[]{:S(2)}) copy-start(s32[512]{0:T(512)} %chain_s.5) | copy-start | bytes 6148
  0.0 8.6 %copy-start.5 = (f32[128]{0:T(128)S(1)}, f32[128]{0:T(128)}, u32[]{:S(2)}) copy-start(f32[128]{0:T(128)} %param.16) | copy-start | bytes 1540
  0.0 8.6 %copy-start.4 = (f32[128]{0:T(128)S(1)}, f32[128]{0:T(128)}, u32[]{:S(2)}) copy-start(f32[128]{0:T(128)} %param.15) | copy-start | bytes 1540
  0.0 8.6 %copy-start.3 = (s32[512]{0:T(512)S(1)}, s32[512]{0:T(512)}, u32[]{:S(2)}) copy-start(s32[512]{0:T(512)} %mask_s.5) | copy-start | bytes 6148
  1.6 2.2 %copy-start = (bf16[32,512,128]{2,1,0:T(8,128)(2,1)S(1)}, bf16[32,512,128]{2,1,0:T(8,128)(2,1)}, u32[]{:S(2)}) copy-start(bf16[32,512,128]{2,1,0:T(8,128)(2,1)} %pairs.1) | copy-start | bytes 12582916
  4.8 7.0 %collective-permute-start = (bf16[32,4,32,128]{3,2,1,0:T(8,128)(2,1)S(1)}, bf16[32,4,32,128]{3,2,1,0:T(8,128)(2,1)S(1)}, u32[]{:S(2)}, u32[]{:S(2)}) collective-permute-start(bf16[32,4,32,128]{3,2,1,0:T(8,128)(2,1)S(1)} %get-tuple-element.22), channel_id=1, source_target_pairs={{0,1},{1,0},{2,3},{3,2},{4,5},{5,4},{6,7},{7,6},{8,9},{9,8},{10,11... | collective-permute-start | bytes 3145736 | tf_op jit(solution)/shard_map/ppermute | solution.py:180
  4.9 3.5 %collective-permute-start.1 = (bf16[32,80,128]{2,1,0:T(8,128)(2,1)S(1)}, bf16[32,80,128]{2,1,0:T(8,128)(2,1)S(1)}, u32[]{:S(2)}, u32[]{:S(2)}) collective-permute-start(bf16[32,80,128]{2,1,0:T(8,128)(2,1)S(1)} %get-tuple-element.23.own), channel_id=1, source_target_pairs={{0,1},{1,0},{2,3},{3,2},{4,5},{5,4},{6,7},{7,6},{8,9},{9,8},{10,11... | collective-permute-start | bytes 1966088 | tf_op jit(solution)/shard_map/ppermute | solution.py:180
  5.4 15.3 %collective-permute-start.2 = (bf16[32,4,32,128]{3,2,1,0:T(8,128)(2,1)S(1)}, bf16[32,4,32,128]{3,2,1,0:T(8,128)(2,1)S(1)}, u32[]{:S(2)}, u32[]{:S(2)}) collective-permute-start(bf16[32,4,32,128]{3,2,1,0:T(8,128)(2,1)S(1)} %get-tuple-element.28), channel_id=1, source_target_pairs={{0,1},{1,0},{2,3},{3,2},{4,5},{5,4},{6,7},{7,6},{8,9},{9,8},{10,11... | collective-permute-start | bytes 3145736 | tf_op jit(solution)/shard_map/ppermute | solution.py:180
  8.6 3.2 %copy-start.1 = (bf16[32,512,128]{2,1,0:T(8,128)(2,1)S(1)}, bf16[32,512,128]{2,1,0:T(8,128)(2,1)}, u32[]{:S(2)}) copy-start(bf16[32,512,128]{2,1,0:T(8,128)(2,1)} %pairs.1) | copy-start | bytes 12582916
  18.2 12.2 %collective-permute-start.3 = (bf16[96,32,128]{2,1,0:T(8,128)(2,1)S(1)}, bf16[96,32,128]{2,1,0:T(8,128)(2,1)S(1)}, u32[]{:S(2)}, u32[]{:S(2)}) collective-permute-start(bf16[96,32,128]{2,1,0:T(8,128)(2,1)S(1)} %get-tuple-element.31), channel_id=1, source_target_pairs={{0,2},{1,5},{2,0},{3,7},{4,6},{5,1},{6,4},{7,3},{8,10},{9,13},{10,... | collective-permute-start | bytes 2359304 | tf_op jit(solution)/shard_map/ppermute | solution.py:187
  30.4 33.3 %copy-start.6 = (f32[128]{0:T(128)S(1)}, f32[128]{0:T(128)}, u32[]{:S(2)}) copy-start(f32[128]{0:T(128)} %param.17) | copy-start | bytes 1540
  30.5 7.0 %collective-permute-start.4 = (bf16[48,32,128]{2,1,0:T(8,128)(2,1)S(1)}, bf16[48,32,128]{2,1,0:T(8,128)(2,1)S(1)}, u32[]{:S(2)}, u32[]{:S(2)}) collective-permute-start(bf16[48,32,128]{2,1,0:T(8,128)(2,1)S(1)} %add_convert_fusion.2), channel_id=1, source_target_pairs={{0,4},{1,3},{2,6},{3,1},{4,0},{5,7},{6,2},{7,5},{8,12},{9,11},{10,... | collective-permute-start | bytes 1179656 | tf_op jit(solution)/shard_map/ppermute | solution.py:187
  37.5 19.4 %collective-permute-start.5 = (bf16[96,32,128]{2,1,0:T(8,128)(2,1)S(1)}, bf16[96,32,128]{2,1,0:T(8,128)(2,1)S(1)}, u32[]{:S(2)}, u32[]{:S(2)}) collective-permute-start(bf16[96,32,128]{2,1,0:T(8,128)(2,1)S(1)} %get-tuple-element.32), channel_id=1, source_target_pairs={{0,2},{1,5},{2,0},{3,7},{4,6},{5,1},{6,4},{7,3},{8,10},{9,13},{10,... | collective-permute-start | bytes 2359304 | tf_op jit(solution)/shard_map/ppermute | solution.py:187
  39.9 18.7 %collective-permute-start.6 = (bf16[48,32,128]{2,1,0:T(8,128)(2,1)}, bf16[48,32,128]{2,1,0:T(8,128)(2,1)S(1)}, u32[]{:S(2)}, u32[]{:S(2)}) collective-permute-start(bf16[48,32,128]{2,1,0:T(8,128)(2,1)} %add_convert_fusion.1), channel_id=1, source_target_pairs={{0,8},{1,9},{2,10},{3,11},{4,12},{5,13},{6,14},{7,15},{8,0},{9,1},... | collective-permute-start | bytes 1179656 | tf_op jit(solution)/shard_map/ppermute | solution.py:187
  57.0 6.7 %collective-permute-start.7 = (bf16[48,32,128]{2,1,0:T(8,128)(2,1)S(1)}, bf16[48,32,128]{2,1,0:T(8,128)(2,1)S(1)}, u32[]{:S(2)}, u32[]{:S(2)}) collective-permute-start(bf16[48,32,128]{2,1,0:T(8,128)(2,1)S(1)} %add_convert_fusion), channel_id=1, source_target_pairs={{0,4},{1,3},{2,6},{3,1},{4,0},{5,7},{6,2},{7,5},{8,12},{9,11},{10,... | collective-permute-start | bytes 1179656 | tf_op jit(solution)/shard_map/ppermute | solution.py:187

commit v3 on v2

--- a/solution.py
+++ b/solution.py
@@ -9,6 +9,7 @@
 
 BAND = 48
 NORM_EPS = 1e-05
+STACKS = (2, 1, 1)
 GROUP = 4
 F32, BF16, I32 = jnp.float32, jnp.bfloat16, jnp.int32
 LAST = (((1,), (1,)), ((), ()))
@@ -103,12 +104,13 @@
     gate_ref[...] = jax.nn.sigmoid(gate).reshape(band, rows, width) * mask_i[...][None]
 
 
-def triangle_kernel(group, tile, stack, out_type, chain_s, mask_s, meta, *refs):
+def triangle_kernel(group, tile, stacks, out_type, chain_s, mask_s, meta, *refs):
     own = refs[:group]
     other = refs[group : 2 * group]
     chain_cols = refs[2 * group : 3 * group]
     embed, gain, w_left_ref, right_ref = refs[3 * group : 3 * group + 4]
     outs = refs[3 * group + 4 : -2]
+    slots = [(n, m) for n, stack in enumerate(stacks) for m in range(stack)]
     left_scr, tri_scr = refs[-2:]
     pairs, wide, both2 = right_ref.shape
     width, band, both = pairs * 2, wide // 2, both2 // 2
@@ -145,7 +147,7 @@
         for j in range(band):
             turned = tri_scr[pl.ds(j, width, stride=turn), :].T
             for b in range(group):
-                outs[b // stack][b % stack * band + j] = turned[b * size : (b + 1) * size].astype(out_type)
+                outs[slots[b][0]][slots[b][1] * band + j] = turned[b * size : (b + 1) * size].astype(out_type)
 
 
 def final_kernel(starts, *refs):
@@ -204,7 +206,8 @@
         compiler_params=pltpu.CompilerParams(vmem_limit_bytes=10 << 20),
         name="pack",
     )(meta, pair_map, weights)
-    other_first, other_far, other_near = swap_core(own_first), swap_core(far), swap_core(near)
+    other_first = swap_core(own_first)
+    other_far = swap_core(after(far, other_first))
     own_blocks = pair_map.reshape(rows, tokens // rows, rows, width)
     chain_cols = jnp.broadcast_to(chain_ids[:, None], (tokens, 128))
     row_mask = jnp.broadcast_to(
@@ -236,7 +239,9 @@
         name="right",
     )(chain_ids, token_mask, meta, own_first, other_first, chain_cols, embed, gain)
 
-    def triangle(labels, other_part, out_type, stack, scalars):
+    other_near = swap_core(after(near, right))
+
+    def triangle(labels, other_part, out_type, stacks, scalars):
         group = len(labels)
         row_specs, part_specs, chain_specs = [], [], []
         for v in labels:
@@ -252,9 +257,9 @@
                 pl.BlockSpec((rows, 128), lambda t, c, m, meta, v=v: (place_of(v, meta[0], meta[1]) * 2 + meta[1], 0))
             )
         whole = lambda shape: pl.BlockSpec(shape, lambda t, c, m, meta: (0,) * len(shape))
-        out_shape = (stack * band, rows, width)
+        out_shapes = [(stack * band, rows, width) for stack in stacks]
         return pl.pallas_call(
-            functools.partial(triangle_kernel, group, tile, stack, out_type),
+            functools.partial(triangle_kernel, group, tile, stacks, out_type),
             grid_spec=pltpu.PrefetchScalarGridSpec(
                 num_scalar_prefetch=3,
                 grid=(rows // tile,),
@@ -262,13 +267,13 @@
                 + part_specs
                 + chain_specs
                 + [whole((1, width)), whole((1, width)), whole(w_left.shape), whole(right.shape)],
-                out_specs=[whole(out_shape)] * (group // stack),
+                out_specs=[whole(shape) for shape in out_shapes],
                 scratch_shapes=[
                     pltpu.VMEM((width * (both + 8), group * rows), F32),
                     pltpu.VMEM((width * (band + 8), group * rows), F32),
                 ],
             ),
-            out_shape=[jax.ShapeDtypeStruct(out_shape, out_type)] * (group // stack),
+            out_shape=[jax.ShapeDtypeStruct(shape, out_type) for shape in out_shapes],
             compiler_params=pltpu.CompilerParams(vmem_limit_bytes=28 << 20),
             cost_estimate=pl.CostEstimate(flops=8 * 10**9, bytes_accessed=4 * 10**6, transcendentals=0),
             name="triangle",
@@ -278,12 +283,15 @@
         )
 
     size = GROUP
-    pairs, kept = [], {}
+    far_stacks, kept = [], {}
     for at in range(0, len(odd), size):
-        pairs += triangle(odd[at : at + size], other_far, BF16, 2, meta)
+        outs = triangle(odd[at : at + size], other_far, BF16, STACKS, meta)
+        for n, x in enumerate(outs):
+            first_at = at + sum(STACKS[:n])
+            far_stacks.append((odd[first_at : first_at + STACKS[n]], x))
     for at in range(0, len(even), size):
         labels = even[at : at + size]
-        kept.update(zip(labels, triangle(labels, other_near, F32, 1, after(meta, pairs[-1]))))
+        kept.update(zip(labels, triangle(labels, other_near, F32, (1,) * size, after(meta, far_stacks[-1][1]))))
     gate = pl.pallas_call(
         gate_kernel,
         in_specs=[vmem] * 3,
@@ -296,24 +304,31 @@
 
     arrived = {v: [(kept[v], 0)] for v in even}
 
-    def send_pair(n, x):
+    def send_far(n, *earlier):
+        labels, x = far_stacks[n]
+        for y in earlier:
+            x = after(x, y)
         moved = swap(x, 1)
-        for m in range(2):
-            arrived[odd[2 * n + m] - 1].append((moved, m * band))
-
-    def send(v):
-        total = sum(piece[start : start + band].astype(F32) for piece, start in arrived[v])
+        for m, label in enumerate(labels):
+            arrived[label - 1].append((moved, m * band))
+        return moved
+
+    def total(v):
+        return sum(piece[start : start + band].astype(F32) for piece, start in arrived[v]).astype(BF16)
+
+    def send(v, x=None):
+        x = total(v) if x is None else x
         bit = v & -v
-        arrived[v - bit].append((swap(total.astype(BF16), bit), 0))
-        return arrived[v - bit][-1][0]
-
-    send_pair(0, pairs[0])
-    first_sent = send(even[0])
-    for n in range(1, len(pairs)):
-        send_pair(n, after(pairs[n], first_sent))
+        moved = swap(x, bit)
+        arrived[v - bit].append((moved, 0))
+        return moved
+
+    send_far(0)
+    moved = send(even[0])
+    for n in range(1, len(far_stacks)):
+        send_far(n, kept[0] if n == 1 else moved)
     for v in even[1:-1]:
         send(v)
-
     pieces, starts = zip(*arrived[0])
     return pl.pallas_call(
         functools.partial(final_kernel, starts),

time: 65.4 us -> 62.2 us (0.951)
  the two profiles are of different devices: /device:TPU:1 before, /device:TPU:0 now
where the time goes in v3:
time: 62.2 us; the launch traced here: 62 us
  waiting for transfers between devices  25.5 us (41%)
  Pallas kernels  18.9 us (30%)
  starting transfers between devices  12.2 us (20%)
  local copies, waits for them, and re-layouts  2.49 us (4%)
  other arithmetic  2.09 us (3%)
  between operations  0.84 us (1%)
    ppermute x6, waiting for transfers between devices, swap(): return lax.ppermute(x, ('ax', 'nr'), pairs)  23.7 us
    pallas_call x2, Pallas kernels, triangle(): pl.pallas_call(functools.partial(triangle_kernel, group, tile, stacks, ou...  13 us
    ppermute x6, starting transfers between devices, swap(): return lax.ppermute(x, ('ax', 'nr'), pairs)  11 us
    pallas_call x1, Pallas kernels, body(): pl.pallas_call(right_kernel, grid_spec=pltpu.PrefetchScalarGridSpec(num_s...  3.19 us
    unnamed x14, local copies, waits for them, and re-layouts  2.21 us
    ppermute x3, waiting for transfers between devices, swap_core(): return lax.ppermute(x, 'nr', [(0, 1), (1, 0)])  1.73 us
    pallas_call x1, Pallas kernels, body(): pl.pallas_call(functools.partial(final_kernel, starts), in_specs=[vmem] *...  1.47 us
  transfers between devices with their start and end apart: 9, of which 5 were waited for; matrix products, arithmetic and copies ran while one was open for 2% of the time, Pallas kernels for 27%

profile of v3, /device:TPU:0, one launch (start us, length us, event | category | flops | bytes accessed | tf_op | source)
XLA Modules:
  0.0 62.0 jit_solution(8765401999765528946)
XLA Ops:
  0.7 0.8 %pad_maximum_fusion.weights = bf16[384,128]{1,0:T(8,128)(2,1)S(1)} fusion(bf16[64,128]{1,0:T(8,128)(2,1)} %bitcast.31, bf16[64,128]{1,0:T(8,128)(2,1)} %bitcast.32, bf16[128,128]{1,0:T(8,128)(2,1)} %param.19, bf16[128,128]{1,0:T(8,128)(2,1)} %param.18), kind=kLoop, calls=%fused_computation.3 | loop fusion | flops 393216 | bytes 196608 | tf_op jit(solution)/shard_map/concatenate | solution.py:199
  1.6 0.1 stack.23.meta
  1.6 2.2 %copy-done = bf16[32,512,128]{2,1,0:T(8,128)(2,1)S(1)} copy-done((bf16[32,512,128]{2,1,0:T(8,128)(2,1)S(1)}, bf16[32,512,128]{2,1,0:T(8,128)(2,1)}, u32[]{:S(2)}) %copy-start) | copy-done | bytes 4194328
  3.8 1.0 %pack.1 = (bf16[32,80,128]{2,1,0:T(8,128)(2,1)S(1)}, bf16[32,4,32,128]{3,2,1,0:T(8,128)(2,1)S(1)}, bf16[32,4,32,128]{3,2,1,0:T(8,128)(2,1)S(1)}) custom-call(s32[6]{0:T(128)S(1)} %stack.23.meta, bf16[32,512,128]{2,1,0:T(8,128)(2,1)S(1)} %copy-done, bf16[384,128]{1,0:T(8,128)(2,1)S(1)} %pad_maximum_fusion.weights), custom_call_target="tpu_custom_call" | custom-call | tf_op jit(solution)/shard_map/pack/pallas_call | solution.py:200
  4.8 0.5 collective-permute-start
  5.3 1.7 %collective-permute-done.other = bf16[32,80,128]{2,1,0:T(8,128)(2,1)S(1)} collective-permute-done((bf16[32,80,128]{2,1,0:T(8,128)(2,1)S(1)}, bf16[32,80,128]{2,1,0:T(8,128)(2,1)S(1)}, u32[]{:S(2)}, u32[]{:S(2)}) %collective-permute-start) | collective-permute-done | bytes 655392 | tf_op jit(solution)/shard_map/ppermute | solution.py:182
  7.1 0.4 collective-permute-start.1
  7.4 0.1 broadcast_in_dim.10.chain_cols.refs_8_.refs_9_.refs_10_.refs_11_
  7.6 0.0 copy-start.1
  7.6 3.2 %right.1 = (bf16[64,96,128]{2,1,0:T(8,128)(2,1)S(1)}, bf16[256,128]{1,0:T(8,128)(2,1)S(1)}, bf16[128,128]{1,0:T(8,128)(2,1)S(1)}, bf16[128,128]{1,0:T(8,128)(2,1)S(1)}, bf16[48,32,128]{2,1,0:T(8,128)(2,1)S(1)}) custom-call(s32[512]{0:T(512)S(1)} %copy-done.2, s32[512]{0:T(512)S(1)} %copy-done.3, s32[6]{0:T(128)S(1)} %stack.23.meta, ...), custom_call_target="tpu_custom_call" | custom-call | flops 4000000000 | bytes 2000000 | tf_op jit(solution)/shard_map/right/pallas_call | solution.py:218
  10.8 0.2 collective-permute-start.2
  11.0 0.0 collective-permute-done.1.refs_4_.refs_5_.refs_6_.refs_7_
  11.0 6.3 %triangle.2 = (bf16[96,32,128]{2,1,0:T(8,128)(2,1)S(1)}, bf16[48,32,128]{2,1,0:T(8,128)(2,1)S(1)}, bf16[48,32,128]{2,1,0:T(8,128)(2,1)S(1)}) custom-call(s32[512]{0:T(512)S(1)} %copy-done.2, s32[512]{0:T(512)S(1)} %copy-done.3, s32[6]{0:T(128)S(1)} %stack.23.meta, bf16[32,16,32,128]{3,2,1,0:T(8,128)(2,1)S(1)} %bitcast.16, ...), custom_call_target="tpu_custom_call" | custom-call | flops 8000000000 | bytes 4000000 | tf_op jit(solution)/shard_map/triangle/pallas_call | solution.py:261
  17.3 3.0 %collective-permute-start.3 = (bf16[96,32,128]{2,1,0:T(8,128)(2,1)S(1)}, bf16[96,32,128]{2,1,0:T(8,128)(2,1)S(1)}, u32[]{:S(2)}, u32[]{:S(2)}) collective-permute-start(bf16[96,32,128]{2,1,0:T(8,128)(2,1)S(1)} %get-tuple-element.37), channel_id=1, source_target_pairs={{0,2},{1,5},{2,0},{3,7},{4,6},{5,1},{6,4},{7,3},{8,10},{9,13},{10,... | collective-permute-start | bytes 2359304 | tf_op jit(solution)/shard_map/ppermute | solution.py:189
  20.3 6.7 %triangle.3 = (f32[48,32,128]{2,1,0:T(8,128)S(1)}, f32[48,32,128]{2,1,0:T(8,128)S(1)}, f32[48,32,128]{2,1,0:T(8,128)S(1)}, f32[48,32,128]{2,1,0:T(8,128)S(1)}) custom-call(s32[512]{0:T(512)S(1)} %copy-done.2, s32[512]{0:T(512)S(1)} %copy-done.3, s32[6]{0:T(128)S(1)} %stack.23.meta, bf16[32,16,32,128]{3,2,1,0:T(8,128)(2,1)S(1)} %bitcast.20, ...), custom_call_target="tpu_custom_call" | custom-call | flops 8000000000 | bytes 4000000 | tf_op jit(solution)/shard_map/triangle/pallas_call | solution.py:261
  27.0 0.1 collective-permute-start.7
  27.1 3.2 %collective-permute-done.3 = bf16[96,32,128]{2,1,0:T(8,128)(2,1)S(1)} collective-permute-done((bf16[96,32,128]{2,1,0:T(8,128)(2,1)S(1)}, bf16[96,32,128]{2,1,0:T(8,128)(2,1)S(1)}, u32[]{:S(2)}, u32[]{:S(2)}) %collective-permute-start.3) | collective-permute-done | bytes 786464 | tf_op jit(solution)/shard_map/ppermute | solution.py:189
  30.3 0.1 add_convert_fusion.2
  30.4 2.1 %collective-permute-start.4 = (bf16[48,32,128]{2,1,0:T(8,128)(2,1)S(1)}, bf16[48,32,128]{2,1,0:T(8,128)(2,1)S(1)}, u32[]{:S(2)}, u32[]{:S(2)}) collective-permute-start(bf16[48,32,128]{2,1,0:T(8,128)(2,1)S(1)} %add_convert_fusion.2), channel_id=1, source_target_pairs={{0,4},{1,3},{2,6},{3,1},{4,0},{5,7},{6,2},{7,5},{8,12},{9,11},{10,... | collective-permute-start | bytes 1179656 | tf_op jit(solution)/shard_map/ppermute | solution.py:189
  32.5 4.4 %collective-permute-done.7 = bf16[48,32,128]{2,1,0:T(8,128)(2,1)S(1)} collective-permute-done((bf16[48,32,128]{2,1,0:T(8,128)(2,1)S(1)}, bf16[48,32,128]{2,1,0:T(8,128)(2,1)S(1)}, u32[]{:S(2)}, u32[]{:S(2)}) %collective-permute-start.7) | collective-permute-done | bytes 393248 | tf_op jit(solution)/shard_map/ppermute | solution.py:189
  36.9 0.1 add_convert_fusion
  37.1 1.8 %collective-permute-start.8 = (bf16[48,32,128]{2,1,0:T(8,128)(2,1)S(1)}, bf16[48,32,128]{2,1,0:T(8,128)(2,1)S(1)}, u32[]{:S(2)}, u32[]{:S(2)}) collective-permute-start(bf16[48,32,128]{2,1,0:T(8,128)(2,1)S(1)} %add_convert_fusion), channel_id=1, source_target_pairs={{0,4},{1,3},{2,6},{3,1},{4,0},{5,7},{6,2},{7,5},{8,12},{9,11},{10,... | collective-permute-start | bytes 1179656 | tf_op jit(solution)/shard_map/ppermute | solution.py:189
  38.8 0.0 collective-permute-done.4
  38.8 0.9 %add_convert_fusion.1 = bf16[48,32,128]{2,1,0:T(8,128)(2,1)} fusion(bf16[48,32,128]{2,1,0:T(8,128)(2,1)S(1)} %collective-permute-done.4, f32[48,32,128]{2,1,0:T(8,128)S(1)} %get-tuple-element.39, bf16[96,32,128]{2,1,0:T(8,128)(2,1)S(1)} %collective-permute-done.3), kind=kLoop, calls=%fused_computation.1 | loop fusion | flops 983040 | bytes 1966080 | tf_op jit(solution)/shard_map/convert_element_type | solution.py:317
  39.8 2.6 %collective-permute-start.6 = (bf16[48,32,128]{2,1,0:T(8,128)(2,1)}, bf16[48,32,128]{2,1,0:T(8,128)(2,1)S(1)}, u32[]{:S(2)}, u32[]{:S(2)}) collective-permute-start(bf16[48,32,128]{2,1,0:T(8,128)(2,1)} %add_convert_fusion.1), channel_id=1, source_target_pairs={{0,8},{1,9},{2,10},{3,11},{4,12},{5,13},{6,14},{7,15},{8,0},{9,1},... | collective-permute-start | bytes 1179656 | tf_op jit(solution)/shard_map/ppermute | solution.py:189
  42.3 1.5 %collective-permute-start.5 = (bf16[48,32,128]{2,1,0:T(8,128)(2,1)S(1)}, bf16[48,32,128]{2,1,0:T(8,128)(2,1)S(1)}, u32[]{:S(2)}, u32[]{:S(2)}) collective-permute-start(bf16[48,32,128]{2,1,0:T(8,128)(2,1)S(1)} %get-tuple-element.38), channel_id=1, source_target_pairs={{0,2},{1,5},{2,0},{3,7},{4,6},{5,1},{6,4},{7,3},{8,10},{9,13},{10,... | collective-permute-start | bytes 1179656 | tf_op jit(solution)/shard_map/ppermute | solution.py:189
  43.8 0.1 dynamic-slice_convert_fusion
  43.9 0.1 broadcast_in_dim.24.mask_i
  44.0 0.3 gate.1.refs_4_
  44.3 5.3 %collective-permute-done.8.refs_3_ = bf16[48,32,128]{2,1,0:T(8,128)(2,1)S(1)} collective-permute-done((bf16[48,32,128]{2,1,0:T(8,128)(2,1)S(1)}, bf16[48,32,128]{2,1,0:T(8,128)(2,1)S(1)}, u32[]{:S(2)}, u32[]{:S(2)}) %collective-permute-start.8) | collective-permute-done | bytes 393248 | tf_op jit(solution)/shard_map/ppermute | solution.py:189
  49.6 10.9 %collective-permute-done.6.refs_2_ = bf16[48,32,128]{2,1,0:T(8,128)(2,1)S(1)} collective-permute-done((bf16[48,32,128]{2,1,0:T(8,128)(2,1)}, bf16[48,32,128]{2,1,0:T(8,128)(2,1)S(1)}, u32[]{:S(2)}, u32[]{:S(2)}) %collective-permute-start.6) | collective-permute-done | bytes 393248 | tf_op jit(solution)/shard_map/ppermute | solution.py:189
  60.5 1.5 %final.1 = bf16[32,48,128]{2,1,0:T(8,128)(2,1)} custom-call(f32[48,32,128]{2,1,0:T(8,128)S(1)} %get-tuple-element.35.refs_0_, bf16[48,32,128]{2,1,0:T(8,128)(2,1)S(1)} %collective-permute-done.5.refs_1_, bf16[48,32,128]{2,1,0:T(8,128)(2,1)S(1)} %collective-permute-done.6.refs_2_, bf16[48,32,128]{2,1,0:T(8,128)(2,1)S(1)} %collective-permute-done.8.refs_3_, ...), custom_call_target="tpu_custom_call" | custom-call | flops 1000000000 | bytes 3000000 | tf_op jit(solution)/shard_map/final/pallas_call | solution.py:333
  (14 shorter events, 0.0 us)
Async XLA Ops:
  0.0 7.4 %copy-start.2 = (s32[512]{0:T(512)S(1)}, s32[512]{0:T(512)}, u32[]{:S(2)}) copy-start(s32[512]{0:T(512)} %chain_s.5) | copy-start | bytes 6148
  0.0 7.6 %copy-start.5 = (f32[128]{0:T(128)S(1)}, f32[128]{0:T(128)}, u32[]{:S(2)}) copy-start(f32[128]{0:T(128)} %param.16) | copy-start | bytes 1540
  0.0 7.6 %copy-start.4 = (f32[128]{0:T(128)S(1)}, f32[128]{0:T(128)}, u32[]{:S(2)}) copy-start(f32[128]{0:T(128)} %param.15) | copy-start | bytes 1540
  0.0 7.6 %copy-start.3 = (s32[512]{0:T(512)S(1)}, s32[512]{0:T(512)}, u32[]{:S(2)}) copy-start(s32[512]{0:T(512)} %mask_s.5) | copy-start | bytes 6148
  1.6 2.2 %copy-start = (bf16[32,512,128]{2,1,0:T(8,128)(2,1)S(1)}, bf16[32,512,128]{2,1,0:T(8,128)(2,1)}, u32[]{:S(2)}) copy-start(bf16[32,512,128]{2,1,0:T(8,128)(2,1)} %pairs.1) | copy-start | bytes 12582916
  4.8 2.2 %collective-permute-start = (bf16[32,80,128]{2,1,0:T(8,128)(2,1)S(1)}, bf16[32,80,128]{2,1,0:T(8,128)(2,1)S(1)}, u32[]{:S(2)}, u32[]{:S(2)}) collective-permute-start(bf16[32,80,128]{2,1,0:T(8,128)(2,1)S(1)} %get-tuple-element.27.own), channel_id=1, source_target_pairs={{0,1},{1,0},{2,3},{3,2},{4,5},{5,4},{6,7},{7,6},{8,9},{9,8},{10,11... | collective-permute-start | bytes 1966088 | tf_op jit(solution)/shard_map/ppermute | solution.py:182
  7.1 4.0 %collective-permute-start.1 = (bf16[32,4,32,128]{3,2,1,0:T(8,128)(2,1)S(1)}, bf16[32,4,32,128]{3,2,1,0:T(8,128)(2,1)S(1)}, u32[]{:S(2)}, u32[]{:S(2)}) collective-permute-start(bf16[32,4,32,128]{3,2,1,0:T(8,128)(2,1)S(1)} %get-tuple-element.28), channel_id=1, source_target_pairs={{0,1},{1,0},{2,3},{3,2},{4,5},{5,4},{6,7},{7,6},{8,9},{9,8},{10,11... | collective-permute-start | bytes 3145736 | tf_op jit(solution)/shard_map/ppermute | solution.py:182
  7.6 3.4 %copy-start.1 = (bf16[32,512,128]{2,1,0:T(8,128)(2,1)S(1)}, bf16[32,512,128]{2,1,0:T(8,128)(2,1)}, u32[]{:S(2)}) copy-start(bf16[32,512,128]{2,1,0:T(8,128)(2,1)} %pairs.1) | copy-start | bytes 12582916
  10.8 9.5 %collective-permute-start.2 = (bf16[32,4,32,128]{3,2,1,0:T(8,128)(2,1)S(1)}, bf16[32,4,32,128]{3,2,1,0:T(8,128)(2,1)S(1)}, u32[]{:S(2)}, u32[]{:S(2)}) collective-permute-start(bf16[32,4,32,128]{3,2,1,0:T(8,128)(2,1)S(1)} %get-tuple-element.34), channel_id=1, source_target_pairs={{0,1},{1,0},{2,3},{3,2},{4,5},{5,4},{6,7},{7,6},{8,9},{9,8},{10,11... | collective-permute-start | bytes 3145736 | tf_op jit(solution)/shard_map/ppermute | solution.py:182
  17.3 12.9 %collective-permute-start.3 = (bf16[96,32,128]{2,1,0:T(8,128)(2,1)S(1)}, bf16[96,32,128]{2,1,0:T(8,128)(2,1)S(1)}, u32[]{:S(2)}, u32[]{:S(2)}) collective-permute-start(bf16[96,32,128]{2,1,0:T(8,128)(2,1)S(1)} %get-tuple-element.37), channel_id=1, source_target_pairs={{0,2},{1,5},{2,0},{3,7},{4,6},{5,1},{6,4},{7,3},{8,10},{9,13},{10,... | collective-permute-start | bytes 2359304 | tf_op jit(solution)/shard_map/ppermute | solution.py:189
  27.0 9.9 %collective-permute-start.7 = (bf16[48,32,128]{2,1,0:T(8,128)(2,1)S(1)}, bf16[48,32,128]{2,1,0:T(8,128)(2,1)S(1)}, u32[]{:S(2)}, u32[]{:S(2)}) collective-permute-start(bf16[48,32,128]{2,1,0:T(8,128)(2,1)S(1)} %get-tuple-element.42), channel_id=1, source_target_pairs={{0,2},{1,5},{2,0},{3,7},{4,6},{5,1},{6,4},{7,3},{8,10},{9,13},{10,... | collective-permute-start | bytes 1179656 | tf_op jit(solution)/shard_map/ppermute | solution.py:189
  30.3 30.2 %copy-start.6 = (f32[128]{0:T(128)S(1)}, f32[128]{0:T(128)}, u32[]{:S(2)}) copy-start(f32[128]{0:T(128)} %param.17) | copy-start | bytes 1540
  30.4 8.4 %collective-permute-start.4 = (bf16[48,32,128]{2,1,0:T(8,128)(2,1)S(1)}, bf16[48,32,128]{2,1,0:T(8,128)(2,1)S(1)}, u32[]{:S(2)}, u32[]{:S(2)}) collective-permute-start(bf16[48,32,128]{2,1,0:T(8,128)(2,1)S(1)} %add_convert_fusion.2), channel_id=1, source_target_pairs={{0,4},{1,3},{2,6},{3,1},{4,0},{5,7},{6,2},{7,5},{8,12},{9,11},{10,... | collective-permute-start | bytes 1179656 | tf_op jit(solution)/shard_map/ppermute | solution.py:189
  37.1 12.5 %collective-permute-start.8 = (bf16[48,32,128]{2,1,0:T(8,128)(2,1)S(1)}, bf16[48,32,128]{2,1,0:T(8,128)(2,1)S(1)}, u32[]{:S(2)}, u32[]{:S(2)}) collective-permute-start(bf16[48,32,128]{2,1,0:T(8,128)(2,1)S(1)} %add_convert_fusion), channel_id=1, source_target_pairs={{0,4},{1,3},{2,6},{3,1},{4,0},{5,7},{6,2},{7,5},{8,12},{9,11},{10,... | collective-permute-start | bytes 1179656 | tf_op jit(solution)/shard_map/ppermute | solution.py:189
  39.8 20.7 %collective-permute-start.6 = (bf16[48,32,128]{2,1,0:T(8,128)(2,1)}, bf16[48,32,128]{2,1,0:T(8,128)(2,1)S(1)}, u32[]{:S(2)}, u32[]{:S(2)}) collective-permute-start(bf16[48,32,128]{2,1,0:T(8,128)(2,1)} %add_convert_fusion.1), channel_id=1, source_target_pairs={{0,8},{1,9},{2,10},{3,11},{4,12},{5,13},{6,14},{7,15},{8,0},{9,1},... | collective-permute-start | bytes 1179656 | tf_op jit(solution)/shard_map/ppermute | solution.py:189
  42.3 18.2 %collective-permute-start.5 = (bf16[48,32,128]{2,1,0:T(8,128)(2,1)S(1)}, bf16[48,32,128]{2,1,0:T(8,128)(2,1)S(1)}, u32[]{:S(2)}, u32[]{:S(2)}) collective-permute-start(bf16[48,32,128]{2,1,0:T(8,128)(2,1)S(1)} %get-tuple-element.38), channel_id=1, source_target_pairs={{0,2},{1,5},{2,0},{3,7},{4,6},{5,1},{6,4},{7,3},{8,10},{9,13},{10,... | collective-permute-start | bytes 1179656 | tf_op jit(solution)/shard_map/ppermute | solution.py:189

commit v4 on v3

--- a/solution.py
+++ b/solution.py
@@ -9,7 +9,6 @@
 
 BAND = 48
 NORM_EPS = 1e-05
-STACKS = (2, 1, 1)
 GROUP = 4
 F32, BF16, I32 = jnp.float32, jnp.bfloat16, jnp.int32
 LAST = (((1,), (1,)), ((), ()))
@@ -112,8 +111,8 @@
     outs = refs[3 * group + 4 : -2]
     slots = [(n, m) for n, stack in enumerate(stacks) for m in range(stack)]
     left_scr, tri_scr = refs[-2:]
-    pairs, wide, both2 = right_ref.shape
-    width, band, both = pairs * 2, wide // 2, both2 // 2
+    pairs, band2, both2 = right_ref.shape
+    width, band, both = pairs * 2, band2 // 2, both2 // 2
     rows = both // 2
     pitch, turn = both + 8, band + 8
     size = own[0].shape[2]
@@ -129,13 +128,14 @@
         same = chains == chain_s[base + step * tile + k]
         return layer_norm(values.astype(F32) + jnp.where(same, emb, 0.0), gn).astype(BF16)
 
-    for k in range(tile):
-        pair = jnp.concatenate([normed(0, k), normed(1, k)], 0)
-        proj = lax.dot_general(w_left, pair, LAST, preferred_element_type=F32)
+    wide = 2 * width // (2 * lanes)
+    for k in range(0, tile, wide):
+        several = jnp.concatenate([normed(source, k + m) for source in range(2) for m in range(wide)], 0)
+        proj = lax.dot_general(w_left, several, LAST, preferred_element_type=F32)
         edge = jax.nn.sigmoid(proj[:width]) * proj[width:]
-        at = step * tile + k
-        left_scr[pl.ds(at, width, stride=pitch), :] = edge[:, :lanes]
-        left_scr[pl.ds(at + rows, width, stride=pitch), :] = edge[:, lanes:]
+        for n in range(2 * wide):
+            at = step * tile + k + n // wide * rows + n % wide
+            left_scr[pl.ds(at, width, stride=pitch), :] = edge[:, n * lanes : (n + 1) * lanes]
 
     @pl.when(step == pl.num_programs(0) - 1)
     def _():
@@ -284,14 +284,20 @@
 
     size = GROUP
     far_stacks, kept = [], {}
-    for at in range(0, len(odd), size):
-        outs = triangle(odd[at : at + size], other_far, BF16, STACKS, meta)
-        for n, x in enumerate(outs):
-            first_at = at + sum(STACKS[:n])
-            far_stacks.append((odd[first_at : first_at + STACKS[n]], x))
+
+    def far_call(at, stacks, scalars):
+        labels = odd[at : at + sum(stacks)]
+        for x in triangle(labels, other_far, BF16, stacks, scalars):
+            count = x.shape[0] // band
+            far_stacks.append((labels[:count], x))
+            labels = labels[count:]
+
+    far_call(0, (2,), meta)
+    last = far_stacks[-1][1]
     for at in range(0, len(even), size):
         labels = even[at : at + size]
-        kept.update(zip(labels, triangle(labels, other_near, F32, (1,) * size, after(meta, far_stacks[-1][1]))))
+        kept.update(zip(labels, triangle(labels, other_near, F32, (1,) * size, after(meta, last))))
+        last = kept[labels[-1]]
     gate = pl.pallas_call(
         gate_kernel,
         in_specs=[vmem] * 3,
@@ -324,11 +330,16 @@
         return moved
 
     send_far(0)
-    moved = send(even[0])
+    x = total(even[0])
+    moved = send(even[0], x)
+    for at in range(2, len(odd), 2):
+        far_call(at, (1, 1), after(meta, x))
+        x = far_stacks[-1][1]
     for n in range(1, len(far_stacks)):
-        send_far(n, kept[0] if n == 1 else moved)
+        send_far(n)
     for v in even[1:-1]:
         send(v)
+
     pieces, starts = zip(*arrived[0])
     return pl.pallas_call(
         functools.partial(final_kernel, starts),

time: 62.2 us -> 60.7 us (0.976)
  waiting for transfers between devices: 25.5 us -> 21.4 us
  Pallas kernels: 18.9 us -> 22.7 us
  starting transfers between devices: 12.2 us -> 10.9 us
    ppermute x6, waiting for transfers between devices: 23.7 us -> 19.7 us  [swap(): return lax.ppermute(x, ('ax', 'nr'), pairs)]
    pallas_call x2 -> x3, Pallas kernels: 13 us -> 16.8 us  [triangle(): pl.pallas_call(functools.partial(triangle_kernel, group, tile, stacks, ou...]
    ppermute x6, starting transfers between devices: 11 us -> 9.85 us  [swap(): return lax.ppermute(x, ('ax', 'nr'), pairs)]
  transfers between devices with their start and end apart: 9 -> 9, of which waited for: 5 -> 6; matrix products, arithmetic and copies ran while one was open for 2% -> 2% of each run, Pallas kernels for 27% -> 34%
where the time goes in v4:
time: 60.7 us; the launch traced here: 60.4 us
  Pallas kernels  22.7 us (37%)
  waiting for transfers between devices  21.4 us (35%)
  starting transfers between devices  10.9 us (18%)
  local copies, waits for them, and re-layouts  2.49 us (4%)
  other arithmetic  2.09 us (3%)
  between operations  0.82 us (1%)
    ppermute x6, waiting for transfers between devices, swap(): return lax.ppermute(x, ('ax', 'nr'), pairs)  19.7 us
    pallas_call x3, Pallas kernels, triangle(): pl.pallas_call(functools.partial(triangle_kernel, group, tile, stacks, ou...  16.8 us
    ppermute x6, starting transfers between devices, swap(): return lax.ppermute(x, ('ax', 'nr'), pairs)  9.85 us
    pallas_call x1, Pallas kernels, body(): pl.pallas_call(right_kernel, grid_spec=pltpu.PrefetchScalarGridSpec(num_s...  3.19 us
    unnamed x14, local copies, waits for them, and re-layouts  2.22 us
    ppermute x3, waiting for transfers between devices, swap_core(): return lax.ppermute(x, 'nr', [(0, 1), (1, 0)])  1.73 us
    pallas_call x1, Pallas kernels, body(): pl.pallas_call(functools.partial(final_kernel, starts), in_specs=[vmem] *...  1.47 us
  transfers between devices with their start and end apart: 9, of which 6 were waited for; matrix products, arithmetic and copies ran while one was open for 2% of the time, Pallas kernels for 34%

profile of v4, /device:TPU:0, one launch (start us, length us, event | category | flops | bytes accessed | tf_op | source)
XLA Modules:
  0.0 60.4 jit_solution(16440805495575450695)
XLA Ops:
  0.7 0.8 %pad_maximum_fusion.weights = bf16[384,128]{1,0:T(8,128)(2,1)S(1)} fusion(bf16[64,128]{1,0:T(8,128)(2,1)} %bitcast.33, bf16[64,128]{1,0:T(8,128)(2,1)} %bitcast.34, bf16[128,128]{1,0:T(8,128)(2,1)} %param.19, bf16[128,128]{1,0:T(8,128)(2,1)} %param.18), kind=kLoop, calls=%fused_computation.3 | loop fusion | flops 393216 | bytes 196608 | tf_op jit(solution)/shard_map/concatenate | solution.py:199
  1.5 0.1 stack.23.meta
  1.6 2.2 %copy-done = bf16[32,512,128]{2,1,0:T(8,128)(2,1)S(1)} copy-done((bf16[32,512,128]{2,1,0:T(8,128)(2,1)S(1)}, bf16[32,512,128]{2,1,0:T(8,128)(2,1)}, u32[]{:S(2)}) %copy-start) | copy-done | bytes 4194328
  3.8 1.0 %pack.1 = (bf16[32,80,128]{2,1,0:T(8,128)(2,1)S(1)}, bf16[32,4,32,128]{3,2,1,0:T(8,128)(2,1)S(1)}, bf16[32,4,32,128]{3,2,1,0:T(8,128)(2,1)S(1)}) custom-call(s32[6]{0:T(128)S(1)} %stack.23.meta, bf16[32,512,128]{2,1,0:T(8,128)(2,1)S(1)} %copy-done, bf16[384,128]{1,0:T(8,128)(2,1)S(1)} %pad_maximum_fusion.weights), custom_call_target="tpu_custom_call" | custom-call | tf_op jit(solution)/shard_map/pack/pallas_call | solution.py:200
  4.8 0.5 collective-permute-start
  5.3 1.7 %collective-permute-done.other = bf16[32,80,128]{2,1,0:T(8,128)(2,1)S(1)} collective-permute-done((bf16[32,80,128]{2,1,0:T(8,128)(2,1)S(1)}, bf16[32,80,128]{2,1,0:T(8,128)(2,1)S(1)}, u32[]{:S(2)}, u32[]{:S(2)}) %collective-permute-start) | collective-permute-done | bytes 655392 | tf_op jit(solution)/shard_map/ppermute | solution.py:182
  7.0 0.4 collective-permute-start.1
  7.4 0.1 broadcast_in_dim.10.chain_cols.refs_4_.refs_5_.refs_8_.refs_9_.refs_10_.refs_11_
  7.6 0.0 copy-start.1
  7.6 3.2 %right.1 = (bf16[64,96,128]{2,1,0:T(8,128)(2,1)S(1)}, bf16[256,128]{1,0:T(8,128)(2,1)S(1)}, bf16[128,128]{1,0:T(8,128)(2,1)S(1)}, bf16[128,128]{1,0:T(8,128)(2,1)S(1)}, bf16[48,32,128]{2,1,0:T(8,128)(2,1)S(1)}) custom-call(s32[512]{0:T(512)S(1)} %copy-done.2, s32[512]{0:T(512)S(1)} %copy-done.3, s32[6]{0:T(128)S(1)} %stack.23.meta, ...), custom_call_target="tpu_custom_call" | custom-call | flops 4000000000 | bytes 2000000 | tf_op jit(solution)/shard_map/right/pallas_call | solution.py:218
  10.8 0.2 collective-permute-start.2
  11.0 5.0 %triangle.3 = bf16[96,32,128]{2,1,0:T(8,128)(2,1)S(1)} custom-call(s32[512]{0:T(512)S(1)} %copy-done.2, s32[512]{0:T(512)S(1)} %copy-done.3, s32[6]{0:T(128)S(1)} %stack.23.meta, bf16[32,16,32,128]{3,2,1,0:T(8,128)(2,1)S(1)} %bitcast.16, bf16[32,16,32,128]{3,2,1,0:T(8,128)(2,1)S(1)} %bitcast.17, ...), custom_call_target="tpu_custom_call" | custom-call | flops 8000000000 | bytes 4000000 | tf_op jit(solution)/shard_map/triangle/pallas_call | solution.py:261
  16.0 2.9 %collective-permute-start.3 = (bf16[96,32,128]{2,1,0:T(8,128)(2,1)S(1)}, bf16[96,32,128]{2,1,0:T(8,128)(2,1)S(1)}, u32[]{:S(2)}, u32[]{:S(2)}) collective-permute-start(bf16[96,32,128]{2,1,0:T(8,128)(2,1)S(1)} %triangle.3), channel_id=1, source_target_pairs={{0,2},{1,5},{2,0},{3,7},{4,6},{5,1},{6,4},{7,3},{8,10},{9,13},{10,... | collective-permute-start | bytes 2359304 | tf_op jit(solution)/shard_map/ppermute | solution.py:189
  19.0 6.7 %triangle.4 = (f32[48,32,128]{2,1,0:T(8,128)S(1)}, f32[48,32,128]{2,1,0:T(8,128)S(1)}, f32[48,32,128]{2,1,0:T(8,128)S(1)}, f32[48,32,128]{2,1,0:T(8,128)S(1)}) custom-call(s32[512]{0:T(512)S(1)} %copy-done.2, s32[512]{0:T(512)S(1)} %copy-done.3, s32[6]{0:T(128)S(1)} %stack.23.meta, bf16[32,16,32,128]{3,2,1,0:T(8,128)(2,1)S(1)} %bitcast.18, ...), custom_call_target="tpu_custom_call" | custom-call | flops 8000000000 | bytes 4000000 | tf_op jit(solution)/shard_map/triangle/pallas_call | solution.py:261
  25.7 3.3 %collective-permute-done.3 = bf16[96,32,128]{2,1,0:T(8,128)(2,1)S(1)} collective-permute-done((bf16[96,32,128]{2,1,0:T(8,128)(2,1)S(1)}, bf16[96,32,128]{2,1,0:T(8,128)(2,1)S(1)}, u32[]{:S(2)}, u32[]{:S(2)}) %collective-permute-start.3) | collective-permute-done | bytes 786464 | tf_op jit(solution)/shard_map/ppermute | solution.py:189
  28.9 0.1 add_convert_fusion.2
  29.1 2.1 %collective-permute-start.5 = (bf16[48,32,128]{2,1,0:T(8,128)(2,1)S(1)}, bf16[48,32,128]{2,1,0:T(8,128)(2,1)S(1)}, u32[]{:S(2)}, u32[]{:S(2)}) collective-permute-start(bf16[48,32,128]{2,1,0:T(8,128)(2,1)S(1)} %add_convert_fusion.2), channel_id=1, source_target_pairs={{0,4},{1,3},{2,6},{3,1},{4,0},{5,7},{6,2},{7,5},{8,12},{9,11},{10,... | collective-permute-start | bytes 1179656 | tf_op jit(solution)/shard_map/ppermute | solution.py:189
  31.2 5.1 %triangle.5 = (bf16[48,32,128]{2,1,0:T(8,128)(2,1)S(1)}, bf16[48,32,128]{2,1,0:T(8,128)(2,1)S(1)}) custom-call(s32[512]{0:T(512)S(1)} %copy-done.2, s32[512]{0:T(512)S(1)} %copy-done.3, s32[6]{0:T(128)S(1)} %stack.23.meta, bf16[32,16,32,128]{3,2,1,0:T(8,128)(2,1)S(1)} %bitcast.22, bf16[32,16,32,128]{3,2,1,0:T(8,128)(2,1)S(1)} %bitcast.23, ...), custom_call_target="tpu_custom_call" | custom-call | flops 8000000000 | bytes 4000000 | tf_op jit(solution)/shard_map/triangle/pallas_call | solution.py:261
  36.3 1.6 %collective-permute-start.7 = (bf16[48,32,128]{2,1,0:T(8,128)(2,1)S(1)}, bf16[48,32,128]{2,1,0:T(8,128)(2,1)S(1)}, u32[]{:S(2)}, u32[]{:S(2)}) collective-permute-start(bf16[48,32,128]{2,1,0:T(8,128)(2,1)S(1)} %get-tuple-element.38), channel_id=1, source_target_pairs={{0,2},{1,5},{2,0},{3,7},{4,6},{5,1},{6,4},{7,3},{8,10},{9,13},{10,... | collective-permute-start | bytes 1179656 | tf_op jit(solution)/shard_map/ppermute | solution.py:189
  37.9 0.5 collective-permute-start.4
  38.4 0.9 %add_convert_fusion.1 = bf16[48,32,128]{2,1,0:T(8,128)(2,1)} fusion(bf16[48,32,128]{2,1,0:T(8,128)(2,1)S(1)} %collective-permute-done.5, f32[48,32,128]{2,1,0:T(8,128)S(1)} %get-tuple-element.36, bf16[96,32,128]{2,1,0:T(8,128)(2,1)S(1)} %collective-permute-done.3), kind=kLoop, calls=%fused_computation.1 | loop fusion | flops 983040 | bytes 1966080 | tf_op jit(solution)/shard_map/convert_element_type | solution.py:323
  39.3 2.6 %collective-permute-start.6 = (bf16[48,32,128]{2,1,0:T(8,128)(2,1)}, bf16[48,32,128]{2,1,0:T(8,128)(2,1)S(1)}, u32[]{:S(2)}, u32[]{:S(2)}) collective-permute-start(bf16[48,32,128]{2,1,0:T(8,128)(2,1)} %add_convert_fusion.1), channel_id=1, source_target_pairs={{0,8},{1,9},{2,10},{3,11},{4,12},{5,13},{6,14},{7,15},{8,0},{9,1},... | collective-permute-start | bytes 1179656 | tf_op jit(solution)/shard_map/ppermute | solution.py:189
  41.9 2.2 %collective-permute-done.7 = bf16[48,32,128]{2,1,0:T(8,128)(2,1)S(1)} collective-permute-done((bf16[48,32,128]{2,1,0:T(8,128)(2,1)S(1)}, bf16[48,32,128]{2,1,0:T(8,128)(2,1)S(1)}, u32[]{:S(2)}, u32[]{:S(2)}) %collective-permute-start.7) | collective-permute-done | bytes 393248 | tf_op jit(solution)/shard_map/ppermute | solution.py:189
  44.1 0.1 add_convert_fusion
  44.3 0.1 collective-permute-start.8
  44.4 0.1 dynamic-slice_convert_fusion
  44.4 0.1 broadcast_in_dim.24.mask_i
  44.5 0.3 gate.1.refs_4_
  44.8 3.6 %collective-permute-done.4.refs_1_ = bf16[48,32,128]{2,1,0:T(8,128)(2,1)S(1)} collective-permute-done((bf16[48,32,128]{2,1,0:T(8,128)(2,1)S(1)}, bf16[48,32,128]{2,1,0:T(8,128)(2,1)S(1)}, u32[]{:S(2)}, u32[]{:S(2)}) %collective-permute-start.4) | collective-permute-done | bytes 393248 | tf_op jit(solution)/shard_map/ppermute | solution.py:189
  48.3 7.2 %collective-permute-done.6.refs_2_ = bf16[48,32,128]{2,1,0:T(8,128)(2,1)S(1)} collective-permute-done((bf16[48,32,128]{2,1,0:T(8,128)(2,1)}, bf16[48,32,128]{2,1,0:T(8,128)(2,1)S(1)}, u32[]{:S(2)}, u32[]{:S(2)}) %collective-permute-start.6) | collective-permute-done | bytes 393248 | tf_op jit(solution)/shard_map/ppermute | solution.py:189
  55.6 3.4 %collective-permute-done.8.refs_3_ = bf16[48,32,128]{2,1,0:T(8,128)(2,1)S(1)} collective-permute-done((bf16[48,32,128]{2,1,0:T(8,128)(2,1)S(1)}, bf16[48,32,128]{2,1,0:T(8,128)(2,1)S(1)}, u32[]{:S(2)}, u32[]{:S(2)}) %collective-permute-start.8) | collective-permute-done | bytes 393248 | tf_op jit(solution)/shard_map/ppermute | solution.py:189
  59.0 1.5 %final.1 = bf16[32,48,128]{2,1,0:T(8,128)(2,1)} custom-call(f32[48,32,128]{2,1,0:T(8,128)S(1)} %get-tuple-element.32.refs_0_, bf16[48,32,128]{2,1,0:T(8,128)(2,1)S(1)} %collective-permute-done.4.refs_1_, bf16[48,32,128]{2,1,0:T(8,128)(2,1)S(1)} %collective-permute-done.6.refs_2_, bf16[48,32,128]{2,1,0:T(8,128)(2,1)S(1)} %collective-permute-done.8.refs_3_, ...), custom_call_target="tpu_custom_call" | custom-call | flops 1000000000 | bytes 3000000 | tf_op jit(solution)/shard_map/final/pallas_call | solution.py:344
  (15 shorter events, 0.0 us)
Async XLA Ops:
  0.0 7.5 %copy-start.3 = (s32[512]{0:T(512)S(1)}, s32[512]{0:T(512)}, u32[]{:S(2)}) copy-start(s32[512]{0:T(512)} %mask_s.7) | copy-start | bytes 6148
  0.0 7.4 %copy-start.2 = (s32[512]{0:T(512)S(1)}, s32[512]{0:T(512)}, u32[]{:S(2)}) copy-start(s32[512]{0:T(512)} %chain_s.7) | copy-start | bytes 6148
  0.0 7.5 %copy-start.4 = (f32[128]{0:T(128)S(1)}, f32[128]{0:T(128)}, u32[]{:S(2)}) copy-start(f32[128]{0:T(128)} %param.15) | copy-start | bytes 1540
  0.0 7.5 %copy-start.5 = (f32[128]{0:T(128)S(1)}, f32[128]{0:T(128)}, u32[]{:S(2)}) copy-start(f32[128]{0:T(128)} %param.16) | copy-start | bytes 1540
  1.6 2.2 %copy-start = (bf16[32,512,128]{2,1,0:T(8,128)(2,1)S(1)}, bf16[32,512,128]{2,1,0:T(8,128)(2,1)}, u32[]{:S(2)}) copy-start(bf16[32,512,128]{2,1,0:T(8,128)(2,1)} %pairs.1) | copy-start | bytes 12582916
  4.8 2.2 %collective-permute-start = (bf16[32,80,128]{2,1,0:T(8,128)(2,1)S(1)}, bf16[32,80,128]{2,1,0:T(8,128)(2,1)S(1)}, u32[]{:S(2)}, u32[]{:S(2)}) collective-permute-start(bf16[32,80,128]{2,1,0:T(8,128)(2,1)S(1)} %get-tuple-element.25.own), channel_id=1, source_target_pairs={{0,1},{1,0},{2,3},{3,2},{4,5},{5,4},{6,7},{7,6},{8,9},{9,8},{10,11... | collective-permute-start | bytes 1966088 | tf_op jit(solution)/shard_map/ppermute | solution.py:182
  7.0 3.9 %collective-permute-start.1 = (bf16[32,4,32,128]{3,2,1,0:T(8,128)(2,1)S(1)}, bf16[32,4,32,128]{3,2,1,0:T(8,128)(2,1)S(1)}, u32[]{:S(2)}, u32[]{:S(2)}) collective-permute-start(bf16[32,4,32,128]{3,2,1,0:T(8,128)(2,1)S(1)} %get-tuple-element.26), channel_id=1, source_target_pairs={{0,1},{1,0},{2,3},{3,2},{4,5},{5,4},{6,7},{7,6},{8,9},{9,8},{10,11... | collective-permute-start | bytes 3145736 | tf_op jit(solution)/shard_map/ppermute | solution.py:182
  7.6 3.4 %copy-start.1 = (bf16[32,512,128]{2,1,0:T(8,128)(2,1)S(1)}, bf16[32,512,128]{2,1,0:T(8,128)(2,1)}, u32[]{:S(2)}) copy-start(bf16[32,512,128]{2,1,0:T(8,128)(2,1)} %pairs.1) | copy-start | bytes 12582916
  10.8 8.2 %collective-permute-start.2 = (bf16[32,4,32,128]{3,2,1,0:T(8,128)(2,1)S(1)}, bf16[32,4,32,128]{3,2,1,0:T(8,128)(2,1)S(1)}, u32[]{:S(2)}, u32[]{:S(2)}) collective-permute-start(bf16[32,4,32,128]{3,2,1,0:T(8,128)(2,1)S(1)} %get-tuple-element.31), channel_id=1, source_target_pairs={{0,1},{1,0},{2,3},{3,2},{4,5},{5,4},{6,7},{7,6},{8,9},{9,8},{10,11... | collective-permute-start | bytes 3145736 | tf_op jit(solution)/shard_map/ppermute | solution.py:182
  16.0 12.9 %collective-permute-start.3 = (bf16[96,32,128]{2,1,0:T(8,128)(2,1)S(1)}, bf16[96,32,128]{2,1,0:T(8,128)(2,1)S(1)}, u32[]{:S(2)}, u32[]{:S(2)}) collective-permute-start(bf16[96,32,128]{2,1,0:T(8,128)(2,1)S(1)} %triangle.3), channel_id=1, source_target_pairs={{0,2},{1,5},{2,0},{3,7},{4,6},{5,1},{6,4},{7,3},{8,10},{9,13},{10,... | collective-permute-start | bytes 2359304 | tf_op jit(solution)/shard_map/ppermute | solution.py:189
  29.1 9.3 %collective-permute-start.5 = (bf16[48,32,128]{2,1,0:T(8,128)(2,1)S(1)}, bf16[48,32,128]{2,1,0:T(8,128)(2,1)S(1)}, u32[]{:S(2)}, u32[]{:S(2)}) collective-permute-start(bf16[48,32,128]{2,1,0:T(8,128)(2,1)S(1)} %add_convert_fusion.2), channel_id=1, source_target_pairs={{0,4},{1,3},{2,6},{3,1},{4,0},{5,7},{6,2},{7,5},{8,12},{9,11},{10,... | collective-permute-start | bytes 1179656 | tf_op jit(solution)/shard_map/ppermute | solution.py:189
  36.3 22.7 %copy-start.6 = (f32[128]{0:T(128)S(1)}, f32[128]{0:T(128)}, u32[]{:S(2)}) copy-start(f32[128]{0:T(128)} %param.17) | copy-start | bytes 1540
  36.3 7.8 %collective-permute-start.7 = (bf16[48,32,128]{2,1,0:T(8,128)(2,1)S(1)}, bf16[48,32,128]{2,1,0:T(8,128)(2,1)S(1)}, u32[]{:S(2)}, u32[]{:S(2)}) collective-permute-start(bf16[48,32,128]{2,1,0:T(8,128)(2,1)S(1)} %get-tuple-element.38), channel_id=1, source_target_pairs={{0,2},{1,5},{2,0},{3,7},{4,6},{5,1},{6,4},{7,3},{8,10},{9,13},{10,... | collective-permute-start | bytes 1179656 | tf_op jit(solution)/shard_map/ppermute | solution.py:189
  37.9 10.5 %collective-permute-start.4 = (bf16[48,32,128]{2,1,0:T(8,128)(2,1)S(1)}, bf16[48,32,128]{2,1,0:T(8,128)(2,1)S(1)}, u32[]{:S(2)}, u32[]{:S(2)}) collective-permute-start(bf16[48,32,128]{2,1,0:T(8,128)(2,1)S(1)} %get-tuple-element.35), channel_id=1, source_target_pairs={{0,2},{1,5},{2,0},{3,7},{4,6},{5,1},{6,4},{7,3},{8,10},{9,13},{10,... | collective-permute-start | bytes 1179656 | tf_op jit(solution)/shard_map/ppermute | solution.py:189
  39.3 16.2 %collective-permute-start.6 = (bf16[48,32,128]{2,1,0:T(8,128)(2,1)}, bf16[48,32,128]{2,1,0:T(8,128)(2,1)S(1)}, u32[]{:S(2)}, u32[]{:S(2)}) collective-permute-start(bf16[48,32,128]{2,1,0:T(8,128)(2,1)} %add_convert_fusion.1), channel_id=1, source_target_pairs={{0,8},{1,9},{2,10},{3,11},{4,12},{5,13},{6,14},{7,15},{8,0},{9,1},... | collective-permute-start | bytes 1179656 | tf_op jit(solution)/shard_map/ppermute | solution.py:189
  44.3 14.7 %collective-permute-start.8 = (bf16[48,32,128]{2,1,0:T(8,128)(2,1)S(1)}, bf16[48,32,128]{2,1,0:T(8,128)(2,1)S(1)}, u32[]{:S(2)}, u32[]{:S(2)}) collective-permute-start(bf16[48,32,128]{2,1,0:T(8,128)(2,1)S(1)} %add_convert_fusion), channel_id=1, source_target_pairs={{0,4},{1,3},{2,6},{3,1},{4,0},{5,7},{6,2},{7,5},{8,12},{9,11},{10,... | collective-permute-start | bytes 1179656 | tf_op jit(solution)/shard_map/ppermute | solution.py:189

commit v5 on v4

--- a/solution.py
+++ b/solution.py
@@ -26,11 +26,11 @@
     return ax ^ (label + (swapped - label) * nr)
 
 
-def pack_kernel(far_labels, near_labels, meta, pairs, weights, first, far, near, sems):
-    window = first.shape[1] - 16
+def pack_kernel(far_labels, near_labels, meta, pairs, first, far, near, sems):
+    window = first.shape[1]
     ax, other = meta[0], 1 - meta[1]
     base = pl.multiple_of(meta[5], 16)
-    copies = [pltpu.make_async_copy(pairs.at[:, pl.ds(base, window), :], first.at[:, 0:window, :], sems.at[0])]
+    copies = [pltpu.make_async_copy(pairs.at[:, pl.ds(base, window), :], first, sems.at[0])]
     size = far.shape[2]
     for part, labels in ((far, far_labels), (near, near_labels)):
         for m, label in enumerate(labels):
@@ -39,21 +39,15 @@
             copies.append(pltpu.make_async_copy(pairs.at[:, rows, :], part.at[:, m], sems.at[len(copies)]))
     for copy in copies:
         copy.start()
-    half = weights.shape[0] // 3
-    turned = [weights[n * half : (n + 1) * half].astype(F32).T.astype(BF16) for n in range(2)] + [weights[2 * half :]]
-    turned = jnp.concatenate(turned + turned[:1], 0)
-    for row in range(first.shape[0]):
-        first[row, window:, :] = turned[row * 16 : row * 16 + 16]
     for copy in copies:
         copy.wait()
 
 
 def right_kernel(
-    chain_s, mask_s, meta, own, other, chain_cols, embed, gain, right_ref, w_left_ref, w_gate_ref, w_out_ref, band_ref,
+    chain_s, mask_s, meta, own, other, own_weights, other_weights, chain_cols, embed, gain, right_ref, w_left_ref, w_gate_ref, w_out_ref, band_ref,
     normed_scr, right_scr,
 ):
     rows, window, width = own.shape
-    window -= 16
     band = BAND
     both = 2 * rows
     pitch, turn = window + 8, band + 8
@@ -62,8 +56,13 @@
     first = meta[1] == 0
     chains = chain_cols[pl.ds(base, window), :]
     emb, gn = embed[...], gain[...]
-    w_own = own[:, window:, :].reshape(rows * 16, width)
-    w_other = other[:, window:, :].reshape(rows * 16, width)
+    half = own_weights.shape[0] // 3
+
+    def rows_first(ref):
+        turned = [ref[n * half : (n + 1) * half].astype(F32).T.astype(BF16) for n in range(2)]
+        return jnp.concatenate(turned + [ref[2 * half :]], 0)
+
+    w_own, w_other = rows_first(own_weights), rows_first(other_weights)
     low, high = jnp.where(first, w_own, w_other), jnp.where(first, w_other, w_own)
 
     def weight(start, size):
@@ -150,6 +149,14 @@
                 outs[slots[b][0]][slots[b][1] * band + j] = turned[b * size : (b + 1) * size].astype(out_type)
 
 
+def merge_kernel(starts, *refs):
+    out = refs[-1]
+    total = refs[0][...]
+    for ref, start in zip(refs[1:-1], starts[1:]):
+        total = total + ref[start : start + out.shape[0]].astype(F32)
+    out[...] = total.astype(BF16)
+
+
 def final_kernel(starts, *refs):
     pieces = refs[: len(starts)]
     gate_ref, gain, w_out, out_ref, scr = refs[len(starts) :]
@@ -199,15 +206,16 @@
     weights = jnp.concatenate([w_left, w_right, w_gate.T, w_out.T], 0)
     own_first, far, near = pl.pallas_call(
         functools.partial(pack_kernel, odd, even),
-        in_specs=[smem, hbm, vmem],
+        in_specs=[smem, hbm],
         out_specs=[vmem] * 3,
-        out_shape=[jax.ShapeDtypeStruct((rows, window + 16, width), BF16), part_shape, part_shape],
+        out_shape=[jax.ShapeDtypeStruct((rows, window, width), BF16), part_shape, part_shape],
         scratch_shapes=[pltpu.SemaphoreType.DMA((1 + n_ax,))],
         compiler_params=pltpu.CompilerParams(vmem_limit_bytes=10 << 20),
         name="pack",
-    )(meta, pair_map, weights)
+    )(meta, pair_map)
+    other_weights = swap_core(weights)
     other_first = swap_core(own_first)
-    other_far = swap_core(after(far, other_first))
+    other_far = swap_core(lax.optimization_barrier((far, other_first, other_weights))[0])
     own_blocks = pair_map.reshape(rows, tokens // rows, rows, width)
     chain_cols = jnp.broadcast_to(chain_ids[:, None], (tokens, 128))
     row_mask = jnp.broadcast_to(
@@ -220,7 +228,7 @@
         grid_spec=pltpu.PrefetchScalarGridSpec(
             num_scalar_prefetch=3,
             grid=(),
-            in_specs=[vmem] * 5,
+            in_specs=[vmem] * 7,
             out_specs=[vmem] * 5,
             scratch_shapes=[
                 pltpu.VMEM((both * (window + 8), width), F32),
@@ -237,7 +245,7 @@
         compiler_params=pltpu.CompilerParams(vmem_limit_bytes=18 << 20),
         cost_estimate=pl.CostEstimate(flops=4 * 10**9, bytes_accessed=2 * 10**6, transcendentals=0),
         name="right",
-    )(chain_ids, token_mask, meta, own_first, other_first, chain_cols, embed, gain)
+    )(chain_ids, token_mask, meta, own_first, other_first, weights, other_weights, chain_cols, embed, gain)
 
     other_near = swap_core(after(near, right))
 
@@ -320,6 +328,17 @@
         return moved
 
     def total(v):
+        if len(arrived[v]) > 2:
+            parts, offsets = zip(*arrived[v])
+            return pl.pallas_call(
+                functools.partial(merge_kernel, offsets),
+                in_specs=[vmem] * len(parts),
+                out_specs=vmem,
+                out_shape=jax.ShapeDtypeStruct((band, rows, width), BF16),
+                compiler_params=pltpu.CompilerParams(vmem_limit_bytes=8 << 20),
+                cost_estimate=pl.CostEstimate(flops=10**6, bytes_accessed=10**5, transcendentals=0),
+                name="merge",
+            )(*parts)
         return sum(piece[start : start + band].astype(F32) for piece, start in arrived[v]).astype(BF16)
 
     def send(v, x=None):

time: 60.7 us -> 59.8 us (0.985)
  other arithmetic: 2.09 us -> 1.08 us
    concatenate x1, other arithmetic: 0.82 us -> 0.01 us  [body(): weights = jnp.concatenate([w_left, w_right, w_gate.T, w_out.T], 0)]
    ppermute x3 -> x4, waiting for transfers between devices: 1.73 us -> 1.55 us  [swap_core(): return lax.ppermute(x, 'nr', [(0, 1), (1, 0)])]
    ppermute x3 -> x4, starting transfers between devices: 1.1 us -> 1.22 us  [swap_core(): return lax.ppermute(x, 'nr', [(0, 1), (1, 0)])]
    unnamed x14 -> x22, local copies, waits for them, and re-layouts: 2.22 us -> 2.23 us
  transfers between devices with their start and end apart: 9 -> 10, of which waited for: 6 -> 6; matrix products, arithmetic and copies ran while one was open for 2% -> 2% of each run, Pallas kernels for 34% -> 34%
where the time goes in v5:
time: 59.8 us; the launch traced here: 59.6 us
  Pallas kernels  22.8 us (38%)
  waiting for transfers between devices  21.3 us (36%)
  starting transfers between devices  11.1 us (19%)
  local copies, waits for them, and re-layouts  2.51 us (4%)
  other arithmetic  1.08 us (2%)
  between operations  0.87 us (1%)
    ppermute x6, waiting for transfers between devices, swap(): return lax.ppermute(x, ('ax', 'nr'), pairs)  19.7 us
    pallas_call x3, Pallas kernels, triangle(): pl.pallas_call(functools.partial(triangle_kernel, group, tile, stacks, ou...  16.8 us
    ppermute x6, starting transfers between devices, swap(): return lax.ppermute(x, ('ax', 'nr'), pairs)  9.86 us
    pallas_call x1, Pallas kernels, body(): pl.pallas_call(right_kernel, grid_spec=pltpu.PrefetchScalarGridSpec(num_s...  3.3 us
    unnamed x22, local copies, waits for them, and re-layouts  2.23 us
    ppermute x4, waiting for transfers between devices, swap_core(): return lax.ppermute(x, 'nr', [(0, 1), (1, 0)])  1.55 us
    pallas_call x1, Pallas kernels, body(): pl.pallas_call(functools.partial(final_kernel, starts), in_specs=[vmem] *...  1.47 us
    ppermute x4, starting transfers between devices, swap_core(): return lax.ppermute(x, 'nr', [(0, 1), (1, 0)])  1.22 us
  transfers between devices with their start and end apart: 10, of which 6 were waited for; matrix products, arithmetic and copies ran while one was open for 2% of the time, Pallas kernels for 34%

profile of v5, /device:TPU:0, one launch (start us, length us, event | category | flops | bytes accessed | tf_op | source)
XLA Modules:
  0.0 59.6 jit_solution(16604973859710664689)
XLA Ops:
  0.7 0.1 stack.23.meta
  0.8 2.2 %copy-done = bf16[32,512,128]{2,1,0:T(8,128)(2,1)S(1)} copy-done((bf16[32,512,128]{2,1,0:T(8,128)(2,1)S(1)}, bf16[32,512,128]{2,1,0:T(8,128)(2,1)}, u32[]{:S(2)}) %copy-start) | copy-done | bytes 4194328
  3.0 0.9 %pack.1 = (bf16[32,64,128]{2,1,0:T(8,128)(2,1)S(1)}, bf16[32,4,32,128]{3,2,1,0:T(8,128)(2,1)S(1)}, bf16[32,4,32,128]{3,2,1,0:T(8,128)(2,1)S(1)}) custom-call(s32[6]{0:T(128)S(1)} %stack.23.meta, bf16[32,512,128]{2,1,0:T(8,128)(2,1)S(1)} %copy-done), custom_call_target="tpu_custom_call" | custom-call | tf_op jit(solution)/shard_map/pack/pallas_call | solution.py:207
  3.9 0.5 collective-permute-start
  4.5 0.1 collective-permute-start.1
  4.6 1.5 %collective-permute-done.1.other_weights = bf16[384,128]{1,0:T(8,128)(2,1)S(1)} collective-permute-done((bf16[384,128]{1,0:T(8,128)(2,1)S(1)}, bf16[384,128]{1,0:T(8,128)(2,1)S(1)}, u32[]{:S(2)}, u32[]{:S(2)}) %collective-permute-start.1) | collective-permute-done | bytes 98336 | tf_op jit(solution)/shard_map/ppermute | solution.py:189
  6.1 0.4 collective-permute-start.2
  6.5 0.1 broadcast_in_dim.10.chain_cols.refs_4_.refs_5_.refs_8_.refs_9_.refs_10_.refs_11_
  6.7 0.0 copy-start.1
  6.7 3.3 %right.1 = (bf16[64,96,128]{2,1,0:T(8,128)(2,1)S(1)}, bf16[256,128]{1,0:T(8,128)(2,1)S(1)}, bf16[128,128]{1,0:T(8,128)(2,1)S(1)}, bf16[128,128]{1,0:T(8,128)(2,1)S(1)}, bf16[48,32,128]{2,1,0:T(8,128)(2,1)S(1)}) custom-call(s32[512]{0:T(512)S(1)} %copy-done.2, s32[512]{0:T(512)S(1)} %copy-done.3, s32[6]{0:T(128)S(1)} %stack.23.meta, ...), custom_call_target="tpu_custom_call" | custom-call | flops 4000000000 | bytes 2000000 | tf_op jit(solution)/shard_map/right/pallas_call | solution.py:226
  10.0 0.2 collective-permute-start.3
  10.2 5.1 %triangle.3 = bf16[96,32,128]{2,1,0:T(8,128)(2,1)S(1)} custom-call(s32[512]{0:T(512)S(1)} %copy-done.2, s32[512]{0:T(512)S(1)} %copy-done.3, s32[6]{0:T(128)S(1)} %stack.23.meta, bf16[32,16,32,128]{3,2,1,0:T(8,128)(2,1)S(1)} %bitcast.16, bf16[32,16,32,128]{3,2,1,0:T(8,128)(2,1)S(1)} %bitcast.17, ...), custom_call_target="tpu_custom_call" | custom-call | flops 8000000000 | bytes 4000000 | tf_op jit(solution)/shard_map/triangle/pallas_call | solution.py:269
  15.2 2.9 %collective-permute-start.4 = (bf16[96,32,128]{2,1,0:T(8,128)(2,1)S(1)}, bf16[96,32,128]{2,1,0:T(8,128)(2,1)S(1)}, u32[]{:S(2)}, u32[]{:S(2)}) collective-permute-start(bf16[96,32,128]{2,1,0:T(8,128)(2,1)S(1)} %triangle.3), channel_id=1, source_target_pairs={{0,2},{1,5},{2,0},{3,7},{4,6},{5,1},{6,4},{7,3},{8,10},{9,13},{10,... | collective-permute-start | bytes 2359304 | tf_op jit(solution)/shard_map/ppermute | solution.py:196
  18.2 6.7 %triangle.4 = (f32[48,32,128]{2,1,0:T(8,128)S(1)}, f32[48,32,128]{2,1,0:T(8,128)S(1)}, f32[48,32,128]{2,1,0:T(8,128)S(1)}, f32[48,32,128]{2,1,0:T(8,128)S(1)}) custom-call(s32[512]{0:T(512)S(1)} %copy-done.2, s32[512]{0:T(512)S(1)} %copy-done.3, s32[6]{0:T(128)S(1)} %stack.23.meta, bf16[32,16,32,128]{3,2,1,0:T(8,128)(2,1)S(1)} %bitcast.18, ...), custom_call_target="tpu_custom_call" | custom-call | flops 8000000000 | bytes 4000000 | tf_op jit(solution)/shard_map/triangle/pallas_call | solution.py:269
  24.9 3.3 %collective-permute-done.4.refs_1_ = bf16[96,32,128]{2,1,0:T(8,128)(2,1)S(1)} collective-permute-done((bf16[96,32,128]{2,1,0:T(8,128)(2,1)S(1)}, bf16[96,32,128]{2,1,0:T(8,128)(2,1)S(1)}, u32[]{:S(2)}, u32[]{:S(2)}) %collective-permute-start.4) | collective-permute-done | bytes 786464 | tf_op jit(solution)/shard_map/ppermute | solution.py:196
  28.1 0.1 add_convert_fusion.1
  28.3 2.1 %collective-permute-start.6 = (bf16[48,32,128]{2,1,0:T(8,128)(2,1)S(1)}, bf16[48,32,128]{2,1,0:T(8,128)(2,1)S(1)}, u32[]{:S(2)}, u32[]{:S(2)}) collective-permute-start(bf16[48,32,128]{2,1,0:T(8,128)(2,1)S(1)} %add_convert_fusion.1), channel_id=1, source_target_pairs={{0,4},{1,3},{2,6},{3,1},{4,0},{5,7},{6,2},{7,5},{8,12},{9,11},{10,... | collective-permute-start | bytes 1179656 | tf_op jit(solution)/shard_map/ppermute | solution.py:196
  30.4 5.0 %triangle.5 = (bf16[48,32,128]{2,1,0:T(8,128)(2,1)S(1)}, bf16[48,32,128]{2,1,0:T(8,128)(2,1)S(1)}) custom-call(s32[512]{0:T(512)S(1)} %copy-done.2, s32[512]{0:T(512)S(1)} %copy-done.3, s32[6]{0:T(128)S(1)} %stack.23.meta, bf16[32,16,32,128]{3,2,1,0:T(8,128)(2,1)S(1)} %bitcast.22, bf16[32,16,32,128]{3,2,1,0:T(8,128)(2,1)S(1)} %bitcast.23, ...), custom_call_target="tpu_custom_call" | custom-call | flops 8000000000 | bytes 4000000 | tf_op jit(solution)/shard_map/triangle/pallas_call | solution.py:269
  35.5 1.6 %collective-permute-start.8 = (bf16[48,32,128]{2,1,0:T(8,128)(2,1)S(1)}, bf16[48,32,128]{2,1,0:T(8,128)(2,1)S(1)}, u32[]{:S(2)}, u32[]{:S(2)}) collective-permute-start(bf16[48,32,128]{2,1,0:T(8,128)(2,1)S(1)} %get-tuple-element.38), channel_id=1, source_target_pairs={{0,2},{1,5},{2,0},{3,7},{4,6},{5,1},{6,4},{7,3},{8,10},{9,13},{10,... | collective-permute-start | bytes 1179656 | tf_op jit(solution)/shard_map/ppermute | solution.py:196
  37.1 0.5 collective-permute-start.5
  37.6 0.1 merge.1
  37.7 2.7 %collective-permute-start.7 = (bf16[48,32,128]{2,1,0:T(8,128)(2,1)S(1)}, bf16[48,32,128]{2,1,0:T(8,128)(2,1)S(1)}, u32[]{:S(2)}, u32[]{:S(2)}) collective-permute-start(bf16[48,32,128]{2,1,0:T(8,128)(2,1)S(1)} %merge.1), channel_id=1, source_target_pairs={{0,8},{1,9},{2,10},{3,11},{4,12},{5,13},{6,14},{7,15},{8,0},{9,1},... | collective-permute-start | bytes 1179656 | tf_op jit(solution)/shard_map/ppermute | solution.py:196
  40.3 3.0 %collective-permute-done.8 = bf16[48,32,128]{2,1,0:T(8,128)(2,1)S(1)} collective-permute-done((bf16[48,32,128]{2,1,0:T(8,128)(2,1)S(1)}, bf16[48,32,128]{2,1,0:T(8,128)(2,1)S(1)}, u32[]{:S(2)}, u32[]{:S(2)}) %collective-permute-start.8) | collective-permute-done | bytes 393248 | tf_op jit(solution)/shard_map/ppermute | solution.py:196
  43.3 0.9 %add_convert_fusion = bf16[48,32,128]{2,1,0:T(8,128)(2,1)} fusion(f32[48,32,128]{2,1,0:T(8,128)S(1)} %get-tuple-element.37, bf16[48,32,128]{2,1,0:T(8,128)(2,1)S(1)} %collective-permute-done.8), kind=kLoop, calls=%fused_computation | loop fusion | flops 589824 | bytes 1572864 | tf_op jit(solution)/shard_map/convert_element_type | solution.py:342
  44.2 0.0 collective-permute-start.9
  44.2 0.1 dynamic-slice_convert_fusion
  44.3 0.1 broadcast_in_dim.24.mask_i
  44.4 0.3 gate.1.refs_4_
  44.6 2.9 %collective-permute-done.5.refs_1_ = bf16[48,32,128]{2,1,0:T(8,128)(2,1)S(1)} collective-permute-done((bf16[48,32,128]{2,1,0:T(8,128)(2,1)S(1)}, bf16[48,32,128]{2,1,0:T(8,128)(2,1)S(1)}, u32[]{:S(2)}, u32[]{:S(2)}) %collective-permute-start.5) | collective-permute-done | bytes 393248 | tf_op jit(solution)/shard_map/ppermute | solution.py:196
  47.5 4.8 %collective-permute-done.7.refs_2_ = bf16[48,32,128]{2,1,0:T(8,128)(2,1)S(1)} collective-permute-done((bf16[48,32,128]{2,1,0:T(8,128)(2,1)S(1)}, bf16[48,32,128]{2,1,0:T(8,128)(2,1)S(1)}, u32[]{:S(2)}, u32[]{:S(2)}) %collective-permute-start.7) | collective-permute-done | bytes 393248 | tf_op jit(solution)/shard_map/ppermute | solution.py:196
  52.4 5.8 %collective-permute-done.9.refs_3_ = bf16[48,32,128]{2,1,0:T(8,128)(2,1)S(1)} collective-permute-done((bf16[48,32,128]{2,1,0:T(8,128)(2,1)}, bf16[48,32,128]{2,1,0:T(8,128)(2,1)S(1)}, u32[]{:S(2)}, u32[]{:S(2)}) %collective-permute-start.9) | collective-permute-done | bytes 393248 | tf_op jit(solution)/shard_map/ppermute | solution.py:196
  58.1 1.5 %final.1 = bf16[32,48,128]{2,1,0:T(8,128)(2,1)} custom-call(f32[48,32,128]{2,1,0:T(8,128)S(1)} %get-tuple-element.32.refs_0_, bf16[48,32,128]{2,1,0:T(8,128)(2,1)S(1)} %collective-permute-done.5.refs_1_, bf16[48,32,128]{2,1,0:T(8,128)(2,1)S(1)} %collective-permute-done.7.refs_2_, bf16[48,32,128]{2,1,0:T(8,128)(2,1)S(1)} %collective-permute-done.9.refs_3_, ...), custom_call_target="tpu_custom_call" | custom-call | flops 1000000000 | bytes 3000000 | tf_op jit(solution)/shard_map/final/pallas_call | solution.py:363
  (25 shorter events, 0.1 us)
Async XLA Ops:
  0.0 4.4 %copy-start.7 = (bf16[128,128]{1,0:T(8,128)(2,1)S(1)}, bf16[128,128]{1,0:T(8,128)(2,1)}, u32[]{:S(2)}) copy-start(bf16[128,128]{1,0:T(8,128)(2,1)} %param.19) | copy-start | bytes 98308
  0.0 4.4 %copy-start.8 = (bf16[128,128]{1,0:T(8,128)(2,1)S(1)}, bf16[128,128]{1,0:T(8,128)(2,1)}, u32[]{:S(2)}) copy-start(bf16[128,128]{1,0:T(8,128)(2,1)} %param.18) | copy-start | bytes 98308
  0.0 6.6 %copy-start.3 = (s32[512]{0:T(512)S(1)}, s32[512]{0:T(512)}, u32[]{:S(2)}) copy-start(s32[512]{0:T(512)} %mask_s.7) | copy-start | bytes 6148
  0.0 6.5 %copy-start.2 = (s32[512]{0:T(512)S(1)}, s32[512]{0:T(512)}, u32[]{:S(2)}) copy-start(s32[512]{0:T(512)} %chain_s.7) | copy-start | bytes 6148
  0.0 6.6 %copy-start.4 = (f32[128]{0:T(128)S(1)}, f32[128]{0:T(128)}, u32[]{:S(2)}) copy-start(f32[128]{0:T(128)} %param.15) | copy-start | bytes 1540
  0.0 6.6 %copy-start.5 = (f32[128]{0:T(128)S(1)}, f32[128]{0:T(128)}, u32[]{:S(2)}) copy-start(f32[128]{0:T(128)} %param.16) | copy-start | bytes 1540
  0.8 2.2 %copy-start = (bf16[32,512,128]{2,1,0:T(8,128)(2,1)S(1)}, bf16[32,512,128]{2,1,0:T(8,128)(2,1)}, u32[]{:S(2)}) copy-start(bf16[32,512,128]{2,1,0:T(8,128)(2,1)} %pairs.1) | copy-start | bytes 12582916
  3.0 1.4 %copy-start.9 = (bf16[128,64]{0,1:T(8,128)(2,1)S(1)}, bf16[128,64]{0,1:T(8,128)(2,1)}, u32[]{:S(2)}) copy-start(bf16[128,64]{0,1:T(8,128)(2,1)} %param.21) | copy-start | bytes 49156
  3.0 1.4 %copy-start.10 = (bf16[128,64]{0,1:T(8,128)(2,1)S(1)}, bf16[128,64]{0,1:T(8,128)(2,1)}, u32[]{:S(2)}) copy-start(bf16[128,64]{0,1:T(8,128)(2,1)} %param.20) | copy-start | bytes 49156
  3.9 2.2 %collective-permute-start = (bf16[32,64,128]{2,1,0:T(8,128)(2,1)S(1)}, bf16[32,64,128]{2,1,0:T(8,128)(2,1)S(1)}, u32[]{:S(2)}, u32[]{:S(2)}) collective-permute-start(bf16[32,64,128]{2,1,0:T(8,128)(2,1)S(1)} %get-tuple-element.25.own), channel_id=1, source_target_pairs={{0,1},{1,0},{2,3},{3,2},{4,5},{5,4},{6,7},{7,6},{8,9},{9,8},{10,11... | collective-permute-start | bytes 1572872 | tf_op jit(solution)/shard_map/ppermute | solution.py:189
  4.5 1.6 %collective-permute-start.1 = (bf16[384,128]{1,0:T(8,128)(2,1)S(1)}, bf16[384,128]{1,0:T(8,128)(2,1)S(1)}, u32[]{:S(2)}, u32[]{:S(2)}) collective-permute-start(bf16[384,128]{1,0:T(8,128)(2,1)S(1)} %pad_maximum_fusion.own_weights), channel_id=1, source_target_pairs={{0,1},{1,0},{2,3},{3,2},{4,5},{5,4},{6,7},{7,6},{8,9},{9,8},{10,11... | collective-permute-start | bytes 294920 | tf_op jit(solution)/shard_map/ppermute | solution.py:189
  6.1 4.1 %collective-permute-start.2 = (bf16[32,4,32,128]{3,2,1,0:T(8,128)(2,1)S(1)}, bf16[32,4,32,128]{3,2,1,0:T(8,128)(2,1)S(1)}, u32[]{:S(2)}, u32[]{:S(2)}) collective-permute-start(bf16[32,4,32,128]{3,2,1,0:T(8,128)(2,1)S(1)} %get-tuple-element.26), channel_id=1, source_target_pairs={{0,1},{1,0},{2,3},{3,2},{4,5},{5,4},{6,7},{7,6},{8,9},{9,8},{10,11... | collective-permute-start | bytes 3145736 | tf_op jit(solution)/shard_map/ppermute | solution.py:189
  6.7 3.5 %copy-start.1 = (bf16[32,512,128]{2,1,0:T(8,128)(2,1)S(1)}, bf16[32,512,128]{2,1,0:T(8,128)(2,1)}, u32[]{:S(2)}) copy-start(bf16[32,512,128]{2,1,0:T(8,128)(2,1)} %pairs.1) | copy-start | bytes 12582916
  10.0 8.2 %collective-permute-start.3 = (bf16[32,4,32,128]{3,2,1,0:T(8,128)(2,1)S(1)}, bf16[32,4,32,128]{3,2,1,0:T(8,128)(2,1)S(1)}, u32[]{:S(2)}, u32[]{:S(2)}) collective-permute-start(bf16[32,4,32,128]{3,2,1,0:T(8,128)(2,1)S(1)} %get-tuple-element.31), channel_id=1, source_target_pairs={{0,1},{1,0},{2,3},{3,2},{4,5},{5,4},{6,7},{7,6},{8,9},{9,8},{10,11... | collective-permute-start | bytes 3145736 | tf_op jit(solution)/shard_map/ppermute | solution.py:189
  15.2 12.9 %collective-permute-start.4 = (bf16[96,32,128]{2,1,0:T(8,128)(2,1)S(1)}, bf16[96,32,128]{2,1,0:T(8,128)(2,1)S(1)}, u32[]{:S(2)}, u32[]{:S(2)}) collective-permute-start(bf16[96,32,128]{2,1,0:T(8,128)(2,1)S(1)} %triangle.3), channel_id=1, source_target_pairs={{0,2},{1,5},{2,0},{3,7},{4,6},{5,1},{6,4},{7,3},{8,10},{9,13},{10,... | collective-permute-start | bytes 2359304 | tf_op jit(solution)/shard_map/ppermute | solution.py:196
  28.3 9.3 %collective-permute-start.6 = (bf16[48,32,128]{2,1,0:T(8,128)(2,1)S(1)}, bf16[48,32,128]{2,1,0:T(8,128)(2,1)S(1)}, u32[]{:S(2)}, u32[]{:S(2)}) collective-permute-start(bf16[48,32,128]{2,1,0:T(8,128)(2,1)S(1)} %add_convert_fusion.1), channel_id=1, source_target_pairs={{0,4},{1,3},{2,6},{3,1},{4,0},{5,7},{6,2},{7,5},{8,12},{9,11},{10,... | collective-permute-start | bytes 1179656 | tf_op jit(solution)/shard_map/ppermute | solution.py:196
  35.5 22.7 %copy-start.6 = (f32[128]{0:T(128)S(1)}, f32[128]{0:T(128)}, u32[]{:S(2)}) copy-start(f32[128]{0:T(128)} %param.17) | copy-start | bytes 1540
  35.5 7.8 %collective-permute-start.8 = (bf16[48,32,128]{2,1,0:T(8,128)(2,1)S(1)}, bf16[48,32,128]{2,1,0:T(8,128)(2,1)S(1)}, u32[]{:S(2)}, u32[]{:S(2)}) collective-permute-start(bf16[48,32,128]{2,1,0:T(8,128)(2,1)S(1)} %get-tuple-element.38), channel_id=1, source_target_pairs={{0,2},{1,5},{2,0},{3,7},{4,6},{5,1},{6,4},{7,3},{8,10},{9,13},{10,... | collective-permute-start | bytes 1179656 | tf_op jit(solution)/shard_map/ppermute | solution.py:196
  37.1 10.5 %collective-permute-start.5 = (bf16[48,32,128]{2,1,0:T(8,128)(2,1)S(1)}, bf16[48,32,128]{2,1,0:T(8,128)(2,1)S(1)}, u32[]{:S(2)}, u32[]{:S(2)}) collective-permute-start(bf16[48,32,128]{2,1,0:T(8,128)(2,1)S(1)} %get-tuple-element.35), channel_id=1, source_target_pairs={{0,2},{1,5},{2,0},{3,7},{4,6},{5,1},{6,4},{7,3},{8,10},{9,13},{10,... | collective-permute-start | bytes 1179656 | tf_op jit(solution)/shard_map/ppermute | solution.py:196
  37.7 14.7 %collective-permute-start.7 = (bf16[48,32,128]{2,1,0:T(8,128)(2,1)S(1)}, bf16[48,32,128]{2,1,0:T(8,128)(2,1)S(1)}, u32[]{:S(2)}, u32[]{:S(2)}) collective-permute-start(bf16[48,32,128]{2,1,0:T(8,128)(2,1)S(1)} %merge.1), channel_id=1, source_target_pairs={{0,8},{1,9},{2,10},{3,11},{4,12},{5,13},{6,14},{7,15},{8,0},{9,1},... | collective-permute-start | bytes 1179656 | tf_op jit(solution)/shard_map/ppermute | solution.py:196
  44.2 13.9 %collective-permute-start.9 = (bf16[48,32,128]{2,1,0:T(8,128)(2,1)}, bf16[48,32,128]{2,1,0:T(8,128)(2,1)S(1)}, u32[]{:S(2)}, u32[]{:S(2)}) collective-permute-start(bf16[48,32,128]{2,1,0:T(8,128)(2,1)} %add_convert_fusion), channel_id=1, source_target_pairs={{0,4},{1,3},{2,6},{3,1},{4,0},{5,7},{6,2},{7,5},{8,12},{9,11},{10,... | collective-permute-start | bytes 1179656 | tf_op jit(solution)/shard_map/ppermute | solution.py:196

commit v6 on v5

--- a/solution.py
+++ b/solution.py
@@ -231,8 +231,8 @@
             in_specs=[vmem] * 7,
             out_specs=[vmem] * 5,
             scratch_shapes=[
-                pltpu.VMEM((both * (window + 8), width), F32),
-                pltpu.VMEM((width * (band + 8), 2 * both), F32),
+                pltpu.VMEM(((both + 1) * (window + 8), width), F32),
+                pltpu.VMEM(((width + 1) * (band + 8), 2 * both), F32),
             ],
         ),
         out_shape=[
@@ -277,8 +277,8 @@
                 + [whole((1, width)), whole((1, width)), whole(w_left.shape), whole(right.shape)],
                 out_specs=[whole(shape) for shape in out_shapes],
                 scratch_shapes=[
-                    pltpu.VMEM((width * (both + 8), group * rows), F32),
-                    pltpu.VMEM((width * (band + 8), group * rows), F32),
+                    pltpu.VMEM(((width + 1) * (both + 8), group * rows), F32),
+                    pltpu.VMEM(((width + 1) * (band + 8), group * rows), F32),
                 ],
             ),
             out_shape=[jax.ShapeDtypeStruct(shape, out_type) for shape in out_shapes],
@@ -365,7 +365,7 @@
         in_specs=[vmem] * (len(pieces) + 3),
         out_specs=vmem,
         out_shape=jax.ShapeDtypeStruct((rows, band, width), BF16),
-        scratch_shapes=[pltpu.VMEM((rows * (band + 8), width), F32)],
+        scratch_shapes=[pltpu.VMEM(((rows + 1) * (band + 8), width), F32)],
         compiler_params=pltpu.CompilerParams(vmem_limit_bytes=14 << 20),
         cost_estimate=pl.CostEstimate(flops=10**9, bytes_accessed=3 * 10**6, transcendentals=0),
         name="final",

time: 59.8 us -> 59.8 us (level)
  no operation moved by 1% of the time
where the time goes in v6:
time: 59.8 us; the launch traced here: 59.6 us
  Pallas kernels  22.8 us (38%)
  waiting for transfers between devices  21.3 us (36%)
  starting transfers between devices  11.1 us (19%)
  local copies, waits for them, and re-layouts  2.51 us (4%)
  other arithmetic  1.08 us (2%)
  between operations  0.87 us (1%)
    ppermute x6, waiting for transfers between devices, swap(): return lax.ppermute(x, ('ax', 'nr'), pairs)  19.7 us
    pallas_call x3, Pallas kernels, triangle(): pl.pallas_call(functools.partial(triangle_kernel, group, tile, stacks, ou...  16.8 us
    ppermute x6, starting transfers between devices, swap(): return lax.ppermute(x, ('ax', 'nr'), pairs)  9.86 us
    pallas_call x1, Pallas kernels, body(): pl.pallas_call(right_kernel, grid_spec=pltpu.PrefetchScalarGridSpec(num_s...  3.29 us
    unnamed x22, local copies, waits for them, and re-layouts  2.23 us
    ppermute x4, waiting for transfers between devices, swap_core(): return lax.ppermute(x, 'nr', [(0, 1), (1, 0)])  1.55 us
    pallas_call x1, Pallas kernels, body(): pl.pallas_call(functools.partial(final_kernel, starts), in_specs=[vmem] *...  1.48 us
    ppermute x4, starting transfers between devices, swap_core(): return lax.ppermute(x, 'nr', [(0, 1), (1, 0)])  1.22 us
  transfers between devices with their start and end apart: 10, of which 6 were waited for; matrix products, arithmetic and copies ran while one was open for 2% of the time, Pallas kernels for 34%

profile of v6, /device:TPU:0, one launch (start us, length us, event | category | flops | bytes accessed | tf_op | source)
XLA Modules:
  0.0 59.6 jit_solution(14049651299685708469)
XLA Ops:
  0.7 0.1 stack.23.meta
  0.8 2.2 %copy-done = bf16[32,512,128]{2,1,0:T(8,128)(2,1)S(1)} copy-done((bf16[32,512,128]{2,1,0:T(8,128)(2,1)S(1)}, bf16[32,512,128]{2,1,0:T(8,128)(2,1)}, u32[]{:S(2)}) %copy-start) | copy-done | bytes 4194328
  3.0 0.9 %pack.1 = (bf16[32,64,128]{2,1,0:T(8,128)(2,1)S(1)}, bf16[32,4,32,128]{3,2,1,0:T(8,128)(2,1)S(1)}, bf16[32,4,32,128]{3,2,1,0:T(8,128)(2,1)S(1)}) custom-call(s32[6]{0:T(128)S(1)} %stack.23.meta, bf16[32,512,128]{2,1,0:T(8,128)(2,1)S(1)} %copy-done), custom_call_target="tpu_custom_call" | custom-call | tf_op jit(solution)/shard_map/pack/pallas_call | solution.py:207
  3.9 0.5 collective-permute-start
  4.5 0.1 collective-permute-start.1
  4.6 1.5 %collective-permute-done.1.other_weights = bf16[384,128]{1,0:T(8,128)(2,1)S(1)} collective-permute-done((bf16[384,128]{1,0:T(8,128)(2,1)S(1)}, bf16[384,128]{1,0:T(8,128)(2,1)S(1)}, u32[]{:S(2)}, u32[]{:S(2)}) %collective-permute-start.1) | collective-permute-done | bytes 98336 | tf_op jit(solution)/shard_map/ppermute | solution.py:189
  6.1 0.4 collective-permute-start.2
  6.5 0.1 broadcast_in_dim.10.chain_cols.refs_4_.refs_5_.refs_8_.refs_9_.refs_10_.refs_11_
  6.7 3.3 %right.1 = (bf16[64,96,128]{2,1,0:T(8,128)(2,1)S(1)}, bf16[256,128]{1,0:T(8,128)(2,1)S(1)}, bf16[128,128]{1,0:T(8,128)(2,1)S(1)}, bf16[128,128]{1,0:T(8,128)(2,1)S(1)}, bf16[48,32,128]{2,1,0:T(8,128)(2,1)S(1)}) custom-call(s32[512]{0:T(512)S(1)} %copy-done.2, s32[512]{0:T(512)S(1)} %copy-done.3, s32[6]{0:T(128)S(1)} %stack.23.meta, ...), custom_call_target="tpu_custom_call" | custom-call | flops 4000000000 | bytes 2000000 | tf_op jit(solution)/shard_map/right/pallas_call | solution.py:226
  10.0 0.2 collective-permute-start.3
  10.2 5.0 %triangle.3 = bf16[96,32,128]{2,1,0:T(8,128)(2,1)S(1)} custom-call(s32[512]{0:T(512)S(1)} %copy-done.2, s32[512]{0:T(512)S(1)} %copy-done.3, s32[6]{0:T(128)S(1)} %stack.23.meta, bf16[32,16,32,128]{3,2,1,0:T(8,128)(2,1)S(1)} %bitcast.16, bf16[32,16,32,128]{3,2,1,0:T(8,128)(2,1)S(1)} %bitcast.17, ...), custom_call_target="tpu_custom_call" | custom-call | flops 8000000000 | bytes 4000000 | tf_op jit(solution)/shard_map/triangle/pallas_call | solution.py:269
  15.2 2.9 %collective-permute-start.4 = (bf16[96,32,128]{2,1,0:T(8,128)(2,1)S(1)}, bf16[96,32,128]{2,1,0:T(8,128)(2,1)S(1)}, u32[]{:S(2)}, u32[]{:S(2)}) collective-permute-start(bf16[96,32,128]{2,1,0:T(8,128)(2,1)S(1)} %triangle.3), channel_id=1, source_target_pairs={{0,2},{1,5},{2,0},{3,7},{4,6},{5,1},{6,4},{7,3},{8,10},{9,13},{10,... | collective-permute-start | bytes 2359304 | tf_op jit(solution)/shard_map/ppermute | solution.py:196
  18.2 6.7 %triangle.4 = (f32[48,32,128]{2,1,0:T(8,128)S(1)}, f32[48,32,128]{2,1,0:T(8,128)S(1)}, f32[48,32,128]{2,1,0:T(8,128)S(1)}, f32[48,32,128]{2,1,0:T(8,128)S(1)}) custom-call(s32[512]{0:T(512)S(1)} %copy-done.2, s32[512]{0:T(512)S(1)} %copy-done.3, s32[6]{0:T(128)S(1)} %stack.23.meta, bf16[32,16,32,128]{3,2,1,0:T(8,128)(2,1)S(1)} %bitcast.18, ...), custom_call_target="tpu_custom_call" | custom-call | flops 8000000000 | bytes 4000000 | tf_op jit(solution)/shard_map/triangle/pallas_call | solution.py:269
  24.9 3.3 %collective-permute-done.4.refs_1_ = bf16[96,32,128]{2,1,0:T(8,128)(2,1)S(1)} collective-permute-done((bf16[96,32,128]{2,1,0:T(8,128)(2,1)S(1)}, bf16[96,32,128]{2,1,0:T(8,128)(2,1)S(1)}, u32[]{:S(2)}, u32[]{:S(2)}) %collective-permute-start.4) | collective-permute-done | bytes 786464 | tf_op jit(solution)/shard_map/ppermute | solution.py:196
  28.1 0.1 add_convert_fusion.1
  28.3 2.1 %collective-permute-start.6 = (bf16[48,32,128]{2,1,0:T(8,128)(2,1)S(1)}, bf16[48,32,128]{2,1,0:T(8,128)(2,1)S(1)}, u32[]{:S(2)}, u32[]{:S(2)}) collective-permute-start(bf16[48,32,128]{2,1,0:T(8,128)(2,1)S(1)} %add_convert_fusion.1), channel_id=1, source_target_pairs={{0,4},{1,3},{2,6},{3,1},{4,0},{5,7},{6,2},{7,5},{8,12},{9,11},{10,... | collective-permute-start | bytes 1179656 | tf_op jit(solution)/shard_map/ppermute | solution.py:196
  30.4 5.0 %triangle.5 = (bf16[48,32,128]{2,1,0:T(8,128)(2,1)S(1)}, bf16[48,32,128]{2,1,0:T(8,128)(2,1)S(1)}) custom-call(s32[512]{0:T(512)S(1)} %copy-done.2, s32[512]{0:T(512)S(1)} %copy-done.3, s32[6]{0:T(128)S(1)} %stack.23.meta, bf16[32,16,32,128]{3,2,1,0:T(8,128)(2,1)S(1)} %bitcast.22, bf16[32,16,32,128]{3,2,1,0:T(8,128)(2,1)S(1)} %bitcast.23, ...), custom_call_target="tpu_custom_call" | custom-call | flops 8000000000 | bytes 4000000 | tf_op jit(solution)/shard_map/triangle/pallas_call | solution.py:269
  35.5 0.0 copy-start.6
  35.5 1.6 %collective-permute-start.8 = (bf16[48,32,128]{2,1,0:T(8,128)(2,1)S(1)}, bf16[48,32,128]{2,1,0:T(8,128)(2,1)S(1)}, u32[]{:S(2)}, u32[]{:S(2)}) collective-permute-start(bf16[48,32,128]{2,1,0:T(8,128)(2,1)S(1)} %get-tuple-element.38), channel_id=1, source_target_pairs={{0,2},{1,5},{2,0},{3,7},{4,6},{5,1},{6,4},{7,3},{8,10},{9,13},{10,... | collective-permute-start | bytes 1179656 | tf_op jit(solution)/shard_map/ppermute | solution.py:196
  37.1 0.5 collective-permute-start.5
  37.6 0.1 merge.1
  37.7 2.7 %collective-permute-start.7 = (bf16[48,32,128]{2,1,0:T(8,128)(2,1)S(1)}, bf16[48,32,128]{2,1,0:T(8,128)(2,1)S(1)}, u32[]{:S(2)}, u32[]{:S(2)}) collective-permute-start(bf16[48,32,128]{2,1,0:T(8,128)(2,1)S(1)} %merge.1), channel_id=1, source_target_pairs={{0,8},{1,9},{2,10},{3,11},{4,12},{5,13},{6,14},{7,15},{8,0},{9,1},... | collective-permute-start | bytes 1179656 | tf_op jit(solution)/shard_map/ppermute | solution.py:196
  40.3 3.0 %collective-permute-done.8 = bf16[48,32,128]{2,1,0:T(8,128)(2,1)S(1)} collective-permute-done((bf16[48,32,128]{2,1,0:T(8,128)(2,1)S(1)}, bf16[48,32,128]{2,1,0:T(8,128)(2,1)S(1)}, u32[]{:S(2)}, u32[]{:S(2)}) %collective-permute-start.8) | collective-permute-done | bytes 393248 | tf_op jit(solution)/shard_map/ppermute | solution.py:196
  43.3 0.9 %add_convert_fusion = bf16[48,32,128]{2,1,0:T(8,128)(2,1)} fusion(f32[48,32,128]{2,1,0:T(8,128)S(1)} %get-tuple-element.37, bf16[48,32,128]{2,1,0:T(8,128)(2,1)S(1)} %collective-permute-done.8), kind=kLoop, calls=%fused_computation | loop fusion | flops 589824 | bytes 1572864 | tf_op jit(solution)/shard_map/convert_element_type | solution.py:342
  44.2 0.0 collective-permute-start.9
  44.2 0.1 dynamic-slice_convert_fusion
  44.3 0.1 broadcast_in_dim.24.mask_i
  44.4 0.3 gate.1.refs_4_
  44.6 2.9 %collective-permute-done.5.refs_1_ = bf16[48,32,128]{2,1,0:T(8,128)(2,1)S(1)} collective-permute-done((bf16[48,32,128]{2,1,0:T(8,128)(2,1)S(1)}, bf16[48,32,128]{2,1,0:T(8,128)(2,1)S(1)}, u32[]{:S(2)}, u32[]{:S(2)}) %collective-permute-start.5) | collective-permute-done | bytes 393248 | tf_op jit(solution)/shard_map/ppermute | solution.py:196
  47.5 4.8 %collective-permute-done.7.refs_2_ = bf16[48,32,128]{2,1,0:T(8,128)(2,1)S(1)} collective-permute-done((bf16[48,32,128]{2,1,0:T(8,128)(2,1)S(1)}, bf16[48,32,128]{2,1,0:T(8,128)(2,1)S(1)}, u32[]{:S(2)}, u32[]{:S(2)}) %collective-permute-start.7) | collective-permute-done | bytes 393248 | tf_op jit(solution)/shard_map/ppermute | solution.py:196
  52.4 5.8 %collective-permute-done.9.refs_3_ = bf16[48,32,128]{2,1,0:T(8,128)(2,1)S(1)} collective-permute-done((bf16[48,32,128]{2,1,0:T(8,128)(2,1)}, bf16[48,32,128]{2,1,0:T(8,128)(2,1)S(1)}, u32[]{:S(2)}, u32[]{:S(2)}) %collective-permute-start.9) | collective-permute-done | bytes 393248 | tf_op jit(solution)/shard_map/ppermute | solution.py:196
  58.1 1.5 %final.1 = bf16[32,48,128]{2,1,0:T(8,128)(2,1)} custom-call(f32[48,32,128]{2,1,0:T(8,128)S(1)} %get-tuple-element.32.refs_0_, bf16[48,32,128]{2,1,0:T(8,128)(2,1)S(1)} %collective-permute-done.5.refs_1_, bf16[48,32,128]{2,1,0:T(8,128)(2,1)S(1)} %collective-permute-done.7.refs_2_, bf16[48,32,128]{2,1,0:T(8,128)(2,1)S(1)} %collective-permute-done.9.refs_3_, ...), custom_call_target="tpu_custom_call" | custom-call | flops 1000000000 | bytes 3000000 | tf_op jit(solution)/shard_map/final/pallas_call | solution.py:363
  (25 shorter events, 0.1 us)
Async XLA Ops:
  0.0 4.4 %copy-start.7 = (bf16[128,128]{1,0:T(8,128)(2,1)S(1)}, bf16[128,128]{1,0:T(8,128)(2,1)}, u32[]{:S(2)}) copy-start(bf16[128,128]{1,0:T(8,128)(2,1)} %param.19) | copy-start | bytes 98308
  0.0 4.4 %copy-start.8 = (bf16[128,128]{1,0:T(8,128)(2,1)S(1)}, bf16[128,128]{1,0:T(8,128)(2,1)}, u32[]{:S(2)}) copy-start(bf16[128,128]{1,0:T(8,128)(2,1)} %param.18) | copy-start | bytes 98308
  0.0 6.6 %copy-start.3 = (s32[512]{0:T(512)S(1)}, s32[512]{0:T(512)}, u32[]{:S(2)}) copy-start(s32[512]{0:T(512)} %mask_s.7) | copy-start | bytes 6148
  0.0 6.5 %copy-start.2 = (s32[512]{0:T(512)S(1)}, s32[512]{0:T(512)}, u32[]{:S(2)}) copy-start(s32[512]{0:T(512)} %chain_s.7) | copy-start | bytes 6148
  0.0 6.6 %copy-start.4 = (f32[128]{0:T(128)S(1)}, f32[128]{0:T(128)}, u32[]{:S(2)}) copy-start(f32[128]{0:T(128)} %param.15) | copy-start | bytes 1540
  0.0 6.6 %copy-start.5 = (f32[128]{0:T(128)S(1)}, f32[128]{0:T(128)}, u32[]{:S(2)}) copy-start(f32[128]{0:T(128)} %param.16) | copy-start | bytes 1540
  0.8 2.2 %copy-start = (bf16[32,512,128]{2,1,0:T(8,128)(2,1)S(1)}, bf16[32,512,128]{2,1,0:T(8,128)(2,1)}, u32[]{:S(2)}) copy-start(bf16[32,512,128]{2,1,0:T(8,128)(2,1)} %pairs.1) | copy-start | bytes 12582916
  3.0 1.4 %copy-start.9 = (bf16[128,64]{0,1:T(8,128)(2,1)S(1)}, bf16[128,64]{0,1:T(8,128)(2,1)}, u32[]{:S(2)}) copy-start(bf16[128,64]{0,1:T(8,128)(2,1)} %param.21) | copy-start | bytes 49156
  3.0 1.4 %copy-start.10 = (bf16[128,64]{0,1:T(8,128)(2,1)S(1)}, bf16[128,64]{0,1:T(8,128)(2,1)}, u32[]{:S(2)}) copy-start(bf16[128,64]{0,1:T(8,128)(2,1)} %param.20) | copy-start | bytes 49156
  3.9 2.2 %collective-permute-start = (bf16[32,64,128]{2,1,0:T(8,128)(2,1)S(1)}, bf16[32,64,128]{2,1,0:T(8,128)(2,1)S(1)}, u32[]{:S(2)}, u32[]{:S(2)}) collective-permute-start(bf16[32,64,128]{2,1,0:T(8,128)(2,1)S(1)} %get-tuple-element.25.own), channel_id=1, source_target_pairs={{0,1},{1,0},{2,3},{3,2},{4,5},{5,4},{6,7},{7,6},{8,9},{9,8},{10,11... | collective-permute-start | bytes 1572872 | tf_op jit(solution)/shard_map/ppermute | solution.py:189
  4.5 1.6 %collective-permute-start.1 = (bf16[384,128]{1,0:T(8,128)(2,1)S(1)}, bf16[384,128]{1,0:T(8,128)(2,1)S(1)}, u32[]{:S(2)}, u32[]{:S(2)}) collective-permute-start(bf16[384,128]{1,0:T(8,128)(2,1)S(1)} %pad_maximum_fusion.own_weights), channel_id=1, source_target_pairs={{0,1},{1,0},{2,3},{3,2},{4,5},{5,4},{6,7},{7,6},{8,9},{9,8},{10,11... | collective-permute-start | bytes 294920 | tf_op jit(solution)/shard_map/ppermute | solution.py:189
  6.1 4.0 %collective-permute-start.2 = (bf16[32,4,32,128]{3,2,1,0:T(8,128)(2,1)S(1)}, bf16[32,4,32,128]{3,2,1,0:T(8,128)(2,1)S(1)}, u32[]{:S(2)}, u32[]{:S(2)}) collective-permute-start(bf16[32,4,32,128]{3,2,1,0:T(8,128)(2,1)S(1)} %get-tuple-element.26), channel_id=1, source_target_pairs={{0,1},{1,0},{2,3},{3,2},{4,5},{5,4},{6,7},{7,6},{8,9},{9,8},{10,11... | collective-permute-start | bytes 3145736 | tf_op jit(solution)/shard_map/ppermute | solution.py:189
  6.7 3.5 %copy-start.1 = (bf16[32,512,128]{2,1,0:T(8,128)(2,1)S(1)}, bf16[32,512,128]{2,1,0:T(8,128)(2,1)}, u32[]{:S(2)}) copy-start(bf16[32,512,128]{2,1,0:T(8,128)(2,1)} %pairs.1) | copy-start | bytes 12582916
  10.0 8.2 %collective-permute-start.3 = (bf16[32,4,32,128]{3,2,1,0:T(8,128)(2,1)S(1)}, bf16[32,4,32,128]{3,2,1,0:T(8,128)(2,1)S(1)}, u32[]{:S(2)}, u32[]{:S(2)}) collective-permute-start(bf16[32,4,32,128]{3,2,1,0:T(8,128)(2,1)S(1)} %get-tuple-element.31), channel_id=1, source_target_pairs={{0,1},{1,0},{2,3},{3,2},{4,5},{5,4},{6,7},{7,6},{8,9},{9,8},{10,11... | collective-permute-start | bytes 3145736 | tf_op jit(solution)/shard_map/ppermute | solution.py:189
  15.2 12.9 %collective-permute-start.4 = (bf16[96,32,128]{2,1,0:T(8,128)(2,1)S(1)}, bf16[96,32,128]{2,1,0:T(8,128)(2,1)S(1)}, u32[]{:S(2)}, u32[]{:S(2)}) collective-permute-start(bf16[96,32,128]{2,1,0:T(8,128)(2,1)S(1)} %triangle.3), channel_id=1, source_target_pairs={{0,2},{1,5},{2,0},{3,7},{4,6},{5,1},{6,4},{7,3},{8,10},{9,13},{10,... | collective-permute-start | bytes 2359304 | tf_op jit(solution)/shard_map/ppermute | solution.py:196
  28.3 9.3 %collective-permute-start.6 = (bf16[48,32,128]{2,1,0:T(8,128)(2,1)S(1)}, bf16[48,32,128]{2,1,0:T(8,128)(2,1)S(1)}, u32[]{:S(2)}, u32[]{:S(2)}) collective-permute-start(bf16[48,32,128]{2,1,0:T(8,128)(2,1)S(1)} %add_convert_fusion.1), channel_id=1, source_target_pairs={{0,4},{1,3},{2,6},{3,1},{4,0},{5,7},{6,2},{7,5},{8,12},{9,11},{10,... | collective-permute-start | bytes 1179656 | tf_op jit(solution)/shard_map/ppermute | solution.py:196
  35.5 22.7 %copy-start.6 = (f32[128]{0:T(128)S(1)}, f32[128]{0:T(128)}, u32[]{:S(2)}) copy-start(f32[128]{0:T(128)} %param.17) | copy-start | bytes 1540
  35.5 7.8 %collective-permute-start.8 = (bf16[48,32,128]{2,1,0:T(8,128)(2,1)S(1)}, bf16[48,32,128]{2,1,0:T(8,128)(2,1)S(1)}, u32[]{:S(2)}, u32[]{:S(2)}) collective-permute-start(bf16[48,32,128]{2,1,0:T(8,128)(2,1)S(1)} %get-tuple-element.38), channel_id=1, source_target_pairs={{0,2},{1,5},{2,0},{3,7},{4,6},{5,1},{6,4},{7,3},{8,10},{9,13},{10,... | collective-permute-start | bytes 1179656 | tf_op jit(solution)/shard_map/ppermute | solution.py:196
  37.1 10.5 %collective-permute-start.5 = (bf16[48,32,128]{2,1,0:T(8,128)(2,1)S(1)}, bf16[48,32,128]{2,1,0:T(8,128)(2,1)S(1)}, u32[]{:S(2)}, u32[]{:S(2)}) collective-permute-start(bf16[48,32,128]{2,1,0:T(8,128)(2,1)S(1)} %get-tuple-element.35), channel_id=1, source_target_pairs={{0,2},{1,5},{2,0},{3,7},{4,6},{5,1},{6,4},{7,3},{8,10},{9,13},{10,... | collective-permute-start | bytes 1179656 | tf_op jit(solution)/shard_map/ppermute | solution.py:196
  37.7 14.7 %collective-permute-start.7 = (bf16[48,32,128]{2,1,0:T(8,128)(2,1)S(1)}, bf16[48,32,128]{2,1,0:T(8,128)(2,1)S(1)}, u32[]{:S(2)}, u32[]{:S(2)}) collective-permute-start(bf16[48,32,128]{2,1,0:T(8,128)(2,1)S(1)} %merge.1), channel_id=1, source_target_pairs={{0,8},{1,9},{2,10},{3,11},{4,12},{5,13},{6,14},{7,15},{8,0},{9,1},... | collective-permute-start | bytes 1179656 | tf_op jit(solution)/shard_map/ppermute | solution.py:196
  44.2 13.9 %collective-permute-start.9 = (bf16[48,32,128]{2,1,0:T(8,128)(2,1)}, bf16[48,32,128]{2,1,0:T(8,128)(2,1)S(1)}, u32[]{:S(2)}, u32[]{:S(2)}) collective-permute-start(bf16[48,32,128]{2,1,0:T(8,128)(2,1)} %add_convert_fusion), channel_id=1, source_target_pairs={{0,4},{1,3},{2,6},{3,1},{4,0},{5,7},{6,2},{7,5},{8,12},{9,11},{10,... | collective-permute-start | bytes 1179656 | tf_op jit(solution)/shard_map/ppermute | solution.py:196

commit v7 on v6

--- a/solution.py
+++ b/solution.py
@@ -328,7 +328,7 @@
         return moved
 
     def total(v):
-        if len(arrived[v]) > 2:
+        if len(arrived[v]) > 1:
             parts, offsets = zip(*arrived[v])
             return pl.pallas_call(
                 functools.partial(merge_kernel, offsets),

time: 59.8 us -> 60.5 us (1.012)
  local copies, waits for them, and re-layouts: 2.51 us -> 4.25 us
  other arithmetic: 1.08 us -> 0.08 us
    unnamed x22 -> x26, local copies, waits for them, and re-layouts: 2.23 us -> 3.97 us
    convert_element_type x2 -> x0, other arithmetic: 1 us -> none  [total(): sum((piece[start:start + band].astype(F32) for piece, start in arrived[v]))]
  transfers between devices with their start and end apart: 10 -> 10, of which waited for: 6 -> 6; matrix products, arithmetic and copies ran while one was open for 2% -> 0% of each run, Pallas kernels for 34% -> 34%
where the time goes in v7:
time: 60.5 us; the launch traced here: 60.2 us
  Pallas kernels  22.9 us (38%)
  waiting for transfers between devices  21 us (35%)
  starting transfers between devices  11.1 us (18%)
  local copies, waits for them, and re-layouts  4.25 us (7%)
  between operations  0.88 us (1%)
    ppermute x6, waiting for transfers between devices, swap(): return lax.ppermute(x, ('ax', 'nr'), pairs)  19.5 us
    pallas_call x3, Pallas kernels, triangle(): pl.pallas_call(functools.partial(triangle_kernel, group, tile, stacks, ou...  16.8 us
    ppermute x6, starting transfers between devices, swap(): return lax.ppermute(x, ('ax', 'nr'), pairs)  9.94 us
    unnamed x26, local copies, waits for them, and re-layouts  3.97 us
    pallas_call x1, Pallas kernels, body(): pl.pallas_call(right_kernel, grid_spec=pltpu.PrefetchScalarGridSpec(num_s...  3.27 us
    ppermute x4, waiting for transfers between devices, swap_core(): return lax.ppermute(x, 'nr', [(0, 1), (1, 0)])  1.55 us
    pallas_call x1, Pallas kernels, body(): pl.pallas_call(functools.partial(final_kernel, starts), in_specs=[vmem] *...  1.48 us
  transfers between devices with their start and end apart: 10, of which 6 were waited for; matrix products, arithmetic and copies ran while one was open for 0% of the time, Pallas kernels for 34%

profile of v7, /device:TPU:0, one launch (start us, length us, event | category | flops | bytes accessed | tf_op | source)
XLA Modules:
  0.0 60.2 jit_solution(2680902673762029407)
XLA Ops:
  0.7 0.1 stack.23.meta
  0.8 2.2 %copy-done = bf16[32,512,128]{2,1,0:T(8,128)(2,1)S(1)} copy-done((bf16[32,512,128]{2,1,0:T(8,128)(2,1)S(1)}, bf16[32,512,128]{2,1,0:T(8,128)(2,1)}, u32[]{:S(2)}) %copy-start) | copy-done | bytes 4194328
  3.0 0.9 %pack.1 = (bf16[32,64,128]{2,1,0:T(8,128)(2,1)S(1)}, bf16[32,4,32,128]{3,2,1,0:T(8,128)(2,1)S(1)}, bf16[32,4,32,128]{3,2,1,0:T(8,128)(2,1)S(1)}) custom-call(s32[6]{0:T(128)S(1)} %stack.23.meta, bf16[32,512,128]{2,1,0:T(8,128)(2,1)S(1)} %copy-done), custom_call_target="tpu_custom_call" | custom-call | tf_op jit(solution)/shard_map/pack/pallas_call | solution.py:207
  3.9 0.5 collective-permute-start
  4.5 0.1 collective-permute-start.1
  4.6 1.5 %collective-permute-done.1.other_weights = bf16[384,128]{1,0:T(8,128)(2,1)S(1)} collective-permute-done((bf16[384,128]{1,0:T(8,128)(2,1)S(1)}, bf16[384,128]{1,0:T(8,128)(2,1)S(1)}, u32[]{:S(2)}, u32[]{:S(2)}) %collective-permute-start.1) | collective-permute-done | bytes 98336 | tf_op jit(solution)/shard_map/ppermute | solution.py:189
  6.1 0.4 collective-permute-start.2
  6.5 0.1 broadcast_in_dim.10.chain_cols.refs_4_.refs_5_.refs_8_.refs_9_.refs_10_.refs_11_
  6.7 3.3 %right.1 = (bf16[64,96,128]{2,1,0:T(8,128)(2,1)S(1)}, bf16[256,128]{1,0:T(8,128)(2,1)S(1)}, bf16[128,128]{1,0:T(8,128)(2,1)S(1)}, bf16[128,128]{1,0:T(8,128)(2,1)S(1)}, bf16[48,32,128]{2,1,0:T(8,128)(2,1)S(1)}) custom-call(s32[512]{0:T(512)S(1)} %copy-done.2, s32[512]{0:T(512)S(1)} %copy-done.3, s32[6]{0:T(128)S(1)} %stack.23.meta, ...), custom_call_target="tpu_custom_call" | custom-call | flops 4000000000 | bytes 2000000 | tf_op jit(solution)/shard_map/right/pallas_call | solution.py:226
  10.0 0.7 %copy-done.7 = bf16[48,32,128]{2,1,0:T(8,128)(2,1)} copy-done((bf16[48,32,128]{2,1,0:T(8,128)(2,1)}, bf16[48,32,128]{2,1,0:T(8,128)(2,1)S(1)}, u32[]{:S(2)}) %copy-start.7) | copy-done | bytes 393240
  10.7 0.1 collective-permute-start.3
  10.8 5.0 %triangle.3 = bf16[96,32,128]{2,1,0:T(8,128)(2,1)S(1)} custom-call(s32[512]{0:T(512)S(1)} %copy-done.2, s32[512]{0:T(512)S(1)} %copy-done.3, s32[6]{0:T(128)S(1)} %stack.23.meta, bf16[32,16,32,128]{3,2,1,0:T(8,128)(2,1)S(1)} %bitcast.16, bf16[32,16,32,128]{3,2,1,0:T(8,128)(2,1)S(1)} %bitcast.17, ...), custom_call_target="tpu_custom_call" | custom-call | flops 8000000000 | bytes 4000000 | tf_op jit(solution)/shard_map/triangle/pallas_call | solution.py:269
  15.9 2.9 %collective-permute-start.4 = (bf16[96,32,128]{2,1,0:T(8,128)(2,1)S(1)}, bf16[96,32,128]{2,1,0:T(8,128)(2,1)S(1)}, u32[]{:S(2)}, u32[]{:S(2)}) collective-permute-start(bf16[96,32,128]{2,1,0:T(8,128)(2,1)S(1)} %triangle.3), channel_id=1, source_target_pairs={{0,2},{1,5},{2,0},{3,7},{4,6},{5,1},{6,4},{7,3},{8,10},{9,13},{10,... | collective-permute-start | bytes 2359304 | tf_op jit(solution)/shard_map/ppermute | solution.py:196
  18.8 6.7 %triangle.4 = (f32[48,32,128]{2,1,0:T(8,128)S(1)}, f32[48,32,128]{2,1,0:T(8,128)S(1)}, f32[48,32,128]{2,1,0:T(8,128)S(1)}, f32[48,32,128]{2,1,0:T(8,128)S(1)}) custom-call(s32[512]{0:T(512)S(1)} %copy-done.2, s32[512]{0:T(512)S(1)} %copy-done.3, s32[6]{0:T(128)S(1)} %stack.23.meta, bf16[32,16,32,128]{3,2,1,0:T(8,128)(2,1)S(1)} %bitcast.18, ...), custom_call_target="tpu_custom_call" | custom-call | flops 8000000000 | bytes 4000000 | tf_op jit(solution)/shard_map/triangle/pallas_call | solution.py:269
  25.5 3.3 %collective-permute-done.4.refs_1_ = bf16[96,32,128]{2,1,0:T(8,128)(2,1)S(1)} collective-permute-done((bf16[96,32,128]{2,1,0:T(8,128)(2,1)S(1)}, bf16[96,32,128]{2,1,0:T(8,128)(2,1)S(1)}, u32[]{:S(2)}, u32[]{:S(2)}) %collective-permute-start.4) | collective-permute-done | bytes 786464 | tf_op jit(solution)/shard_map/ppermute | solution.py:196
  28.9 2.1 %collective-permute-start.6 = (bf16[48,32,128]{2,1,0:T(8,128)(2,1)S(1)}, bf16[48,32,128]{2,1,0:T(8,128)(2,1)S(1)}, u32[]{:S(2)}, u32[]{:S(2)}) collective-permute-start(bf16[48,32,128]{2,1,0:T(8,128)(2,1)S(1)} %merge.3), channel_id=1, source_target_pairs={{0,4},{1,3},{2,6},{3,1},{4,0},{5,7},{6,2},{7,5},{8,12},{9,11},{10,... | collective-permute-start | bytes 1179656 | tf_op jit(solution)/shard_map/ppermute | solution.py:196
  31.0 5.0 %triangle.5 = (bf16[48,32,128]{2,1,0:T(8,128)(2,1)S(1)}, bf16[48,32,128]{2,1,0:T(8,128)(2,1)S(1)}) custom-call(s32[512]{0:T(512)S(1)} %copy-done.2, s32[512]{0:T(512)S(1)} %copy-done.3, s32[6]{0:T(128)S(1)} %stack.23.meta, bf16[32,16,32,128]{3,2,1,0:T(8,128)(2,1)S(1)} %bitcast.22, bf16[32,16,32,128]{3,2,1,0:T(8,128)(2,1)S(1)} %bitcast.23, ...), custom_call_target="tpu_custom_call" | custom-call | flops 8000000000 | bytes 4000000 | tf_op jit(solution)/shard_map/triangle/pallas_call | solution.py:269
  36.1 1.6 %collective-permute-start.8 = (bf16[48,32,128]{2,1,0:T(8,128)(2,1)S(1)}, bf16[48,32,128]{2,1,0:T(8,128)(2,1)S(1)}, u32[]{:S(2)}, u32[]{:S(2)}) collective-permute-start(bf16[48,32,128]{2,1,0:T(8,128)(2,1)S(1)} %get-tuple-element.38), channel_id=1, source_target_pairs={{0,2},{1,5},{2,0},{3,7},{4,6},{5,1},{6,4},{7,3},{8,10},{9,13},{10,... | collective-permute-start | bytes 1179656 | tf_op jit(solution)/shard_map/ppermute | solution.py:196
  37.7 0.5 collective-permute-start.5
  38.2 0.1 merge.4
  38.3 2.7 %collective-permute-start.7 = (bf16[48,32,128]{2,1,0:T(8,128)(2,1)S(1)}, bf16[48,32,128]{2,1,0:T(8,128)(2,1)S(1)}, u32[]{:S(2)}, u32[]{:S(2)}) collective-permute-start(bf16[48,32,128]{2,1,0:T(8,128)(2,1)S(1)} %merge.4), channel_id=1, source_target_pairs={{0,8},{1,9},{2,10},{3,11},{4,12},{5,13},{6,14},{7,15},{8,0},{9,1},... | collective-permute-start | bytes 1179656 | tf_op jit(solution)/shard_map/ppermute | solution.py:196
  41.0 3.0 %collective-permute-done.8.refs_1_ = bf16[48,32,128]{2,1,0:T(8,128)(2,1)S(1)} collective-permute-done((bf16[48,32,128]{2,1,0:T(8,128)(2,1)S(1)}, bf16[48,32,128]{2,1,0:T(8,128)(2,1)S(1)}, u32[]{:S(2)}, u32[]{:S(2)}) %collective-permute-start.8) | collective-permute-done | bytes 393248 | tf_op jit(solution)/shard_map/ppermute | solution.py:196
  43.9 0.1 merge.5
  44.0 0.1 collective-permute-start.9
  44.1 0.1 dynamic-slice_convert_fusion
  44.2 0.1 broadcast_in_dim.24.mask_i
  44.3 1.0 %copy-done.8 = bf16[48,32,128]{2,1,0:T(8,128)(2,1)S(1)} copy-done((bf16[48,32,128]{2,1,0:T(8,128)(2,1)S(1)}, bf16[48,32,128]{2,1,0:T(8,128)(2,1)}, u32[]{:S(2)}) %copy-start.8) | copy-done | bytes 393240
  45.3 0.3 gate.1.refs_4_
  45.5 2.6 %collective-permute-done.5.refs_1_ = bf16[48,32,128]{2,1,0:T(8,128)(2,1)S(1)} collective-permute-done((bf16[48,32,128]{2,1,0:T(8,128)(2,1)S(1)}, bf16[48,32,128]{2,1,0:T(8,128)(2,1)S(1)}, u32[]{:S(2)}, u32[]{:S(2)}) %collective-permute-start.5) | collective-permute-done | bytes 393248 | tf_op jit(solution)/shard_map/ppermute | solution.py:196
  48.1 4.8 %collective-permute-done.7.refs_2_ = bf16[48,32,128]{2,1,0:T(8,128)(2,1)S(1)} collective-permute-done((bf16[48,32,128]{2,1,0:T(8,128)(2,1)S(1)}, bf16[48,32,128]{2,1,0:T(8,128)(2,1)S(1)}, u32[]{:S(2)}, u32[]{:S(2)}) %collective-permute-start.7) | collective-permute-done | bytes 393248 | tf_op jit(solution)/shard_map/ppermute | solution.py:196
  53.0 5.8 %collective-permute-done.9.refs_3_ = bf16[48,32,128]{2,1,0:T(8,128)(2,1)S(1)} collective-permute-done((bf16[48,32,128]{2,1,0:T(8,128)(2,1)S(1)}, bf16[48,32,128]{2,1,0:T(8,128)(2,1)S(1)}, u32[]{:S(2)}, u32[]{:S(2)}) %collective-permute-start.9) | collective-permute-done | bytes 393248 | tf_op jit(solution)/shard_map/ppermute | solution.py:196
  58.8 1.5 %final.1 = bf16[32,48,128]{2,1,0:T(8,128)(2,1)} custom-call(f32[48,32,128]{2,1,0:T(8,128)S(1)} %get-tuple-element.32.refs_0_, bf16[48,32,128]{2,1,0:T(8,128)(2,1)S(1)} %collective-permute-done.5.refs_1_, bf16[48,32,128]{2,1,0:T(8,128)(2,1)S(1)} %collective-permute-done.7.refs_2_, bf16[48,32,128]{2,1,0:T(8,128)(2,1)S(1)} %collective-permute-done.9.refs_3_, ...), custom_call_target="tpu_custom_call" | custom-call | flops 1000000000 | bytes 3000000 | tf_op jit(solution)/shard_map/final/pallas_call | solution.py:363
  (29 shorter events, 0.1 us)
Async XLA Ops:
  0.0 4.4 %copy-start.9 = (bf16[128,128]{1,0:T(8,128)(2,1)S(1)}, bf16[128,128]{1,0:T(8,128)(2,1)}, u32[]{:S(2)}) copy-start(bf16[128,128]{1,0:T(8,128)(2,1)} %param.19) | copy-start | bytes 98308
  0.0 4.4 %copy-start.10 = (bf16[128,128]{1,0:T(8,128)(2,1)S(1)}, bf16[128,128]{1,0:T(8,128)(2,1)}, u32[]{:S(2)}) copy-start(bf16[128,128]{1,0:T(8,128)(2,1)} %param.18) | copy-start | bytes 98308
  0.0 6.6 %copy-start.3 = (s32[512]{0:T(512)S(1)}, s32[512]{0:T(512)}, u32[]{:S(2)}) copy-start(s32[512]{0:T(512)} %mask_s.7) | copy-start | bytes 6148
  0.0 6.5 %copy-start.2 = (s32[512]{0:T(512)S(1)}, s32[512]{0:T(512)}, u32[]{:S(2)}) copy-start(s32[512]{0:T(512)} %chain_s.7) | copy-start | bytes 6148
  0.0 6.6 %copy-start.4 = (f32[128]{0:T(128)S(1)}, f32[128]{0:T(128)}, u32[]{:S(2)}) copy-start(f32[128]{0:T(128)} %param.15) | copy-start | bytes 1540
  0.0 6.6 %copy-start.5 = (f32[128]{0:T(128)S(1)}, f32[128]{0:T(128)}, u32[]{:S(2)}) copy-start(f32[128]{0:T(128)} %param.16) | copy-start | bytes 1540
  0.8 2.2 %copy-start = (bf16[32,512,128]{2,1,0:T(8,128)(2,1)S(1)}, bf16[32,512,128]{2,1,0:T(8,128)(2,1)}, u32[]{:S(2)}) copy-start(bf16[32,512,128]{2,1,0:T(8,128)(2,1)} %pairs.1) | copy-start | bytes 12582916
  3.0 1.4 %copy-start.11 = (bf16[128,64]{0,1:T(8,128)(2,1)S(1)}, bf16[128,64]{0,1:T(8,128)(2,1)}, u32[]{:S(2)}) copy-start(bf16[128,64]{0,1:T(8,128)(2,1)} %param.21) | copy-start | bytes 49156
  3.0 1.4 %copy-start.12 = (bf16[128,64]{0,1:T(8,128)(2,1)S(1)}, bf16[128,64]{0,1:T(8,128)(2,1)}, u32[]{:S(2)}) copy-start(bf16[128,64]{0,1:T(8,128)(2,1)} %param.20) | copy-start | bytes 49156
  3.9 2.2 %collective-permute-start = (bf16[32,64,128]{2,1,0:T(8,128)(2,1)S(1)}, bf16[32,64,128]{2,1,0:T(8,128)(2,1)S(1)}, u32[]{:S(2)}, u32[]{:S(2)}) collective-permute-start(bf16[32,64,128]{2,1,0:T(8,128)(2,1)S(1)} %get-tuple-element.25.own), channel_id=1, source_target_pairs={{0,1},{1,0},{2,3},{3,2},{4,5},{5,4},{6,7},{7,6},{8,9},{9,8},{10,11... | collective-permute-start | bytes 1572872 | tf_op jit(solution)/shard_map/ppermute | solution.py:189
  4.5 1.6 %collective-permute-start.1 = (bf16[384,128]{1,0:T(8,128)(2,1)S(1)}, bf16[384,128]{1,0:T(8,128)(2,1)S(1)}, u32[]{:S(2)}, u32[]{:S(2)}) collective-permute-start(bf16[384,128]{1,0:T(8,128)(2,1)S(1)} %pad_maximum_fusion.own_weights), channel_id=1, source_target_pairs={{0,1},{1,0},{2,3},{3,2},{4,5},{5,4},{6,7},{7,6},{8,9},{9,8},{10,11... | collective-permute-start | bytes 294920 | tf_op jit(solution)/shard_map/ppermute | solution.py:189
  6.1 4.7 %collective-permute-start.2 = (bf16[32,4,32,128]{3,2,1,0:T(8,128)(2,1)S(1)}, bf16[32,4,32,128]{3,2,1,0:T(8,128)(2,1)S(1)}, u32[]{:S(2)}, u32[]{:S(2)}) collective-permute-start(bf16[32,4,32,128]{3,2,1,0:T(8,128)(2,1)S(1)} %get-tuple-element.26), channel_id=1, source_target_pairs={{0,1},{1,0},{2,3},{3,2},{4,5},{5,4},{6,7},{7,6},{8,9},{9,8},{10,11... | collective-permute-start | bytes 3145736 | tf_op jit(solution)/shard_map/ppermute | solution.py:189
  6.7 4.2 %copy-start.1 = (bf16[32,512,128]{2,1,0:T(8,128)(2,1)S(1)}, bf16[32,512,128]{2,1,0:T(8,128)(2,1)}, u32[]{:S(2)}) copy-start(bf16[32,512,128]{2,1,0:T(8,128)(2,1)} %pairs.1) | copy-start | bytes 12582916
  9.9 0.7 %copy-start.7 = (bf16[48,32,128]{2,1,0:T(8,128)(2,1)}, bf16[48,32,128]{2,1,0:T(8,128)(2,1)S(1)}, u32[]{:S(2)}) copy-start(bf16[48,32,128]{2,1,0:T(8,128)(2,1)S(1)} %get-tuple-element.39.band_ref) | copy-start | bytes 1179652
  10.7 8.1 %collective-permute-start.3 = (bf16[32,4,32,128]{3,2,1,0:T(8,128)(2,1)S(1)}, bf16[32,4,32,128]{3,2,1,0:T(8,128)(2,1)S(1)}, u32[]{:S(2)}, u32[]{:S(2)}) collective-permute-start(bf16[32,4,32,128]{3,2,1,0:T(8,128)(2,1)S(1)} %get-tuple-element.31), channel_id=1, source_target_pairs={{0,1},{1,0},{2,3},{3,2},{4,5},{5,4},{6,7},{7,6},{8,9},{9,8},{10,11... | collective-permute-start | bytes 3145736 | tf_op jit(solution)/shard_map/ppermute | solution.py:189
  15.9 12.9 %collective-permute-start.4 = (bf16[96,32,128]{2,1,0:T(8,128)(2,1)S(1)}, bf16[96,32,128]{2,1,0:T(8,128)(2,1)S(1)}, u32[]{:S(2)}, u32[]{:S(2)}) collective-permute-start(bf16[96,32,128]{2,1,0:T(8,128)(2,1)S(1)} %triangle.3), channel_id=1, source_target_pairs={{0,2},{1,5},{2,0},{3,7},{4,6},{5,1},{6,4},{7,3},{8,10},{9,13},{10,... | collective-permute-start | bytes 2359304 | tf_op jit(solution)/shard_map/ppermute | solution.py:196
  28.9 9.3 %collective-permute-start.6 = (bf16[48,32,128]{2,1,0:T(8,128)(2,1)S(1)}, bf16[48,32,128]{2,1,0:T(8,128)(2,1)S(1)}, u32[]{:S(2)}, u32[]{:S(2)}) collective-permute-start(bf16[48,32,128]{2,1,0:T(8,128)(2,1)S(1)} %merge.3), channel_id=1, source_target_pairs={{0,4},{1,3},{2,6},{3,1},{4,0},{5,7},{6,2},{7,5},{8,12},{9,11},{10,... | collective-permute-start | bytes 1179656 | tf_op jit(solution)/shard_map/ppermute | solution.py:196
  36.1 22.7 %copy-start.6 = (f32[128]{0:T(128)S(1)}, f32[128]{0:T(128)}, u32[]{:S(2)}) copy-start(f32[128]{0:T(128)} %param.17) | copy-start | bytes 1540
  36.1 7.8 %collective-permute-start.8 = (bf16[48,32,128]{2,1,0:T(8,128)(2,1)S(1)}, bf16[48,32,128]{2,1,0:T(8,128)(2,1)S(1)}, u32[]{:S(2)}, u32[]{:S(2)}) collective-permute-start(bf16[48,32,128]{2,1,0:T(8,128)(2,1)S(1)} %get-tuple-element.38), channel_id=1, source_target_pairs={{0,2},{1,5},{2,0},{3,7},{4,6},{5,1},{6,4},{7,3},{8,10},{9,13},{10,... | collective-permute-start | bytes 1179656 | tf_op jit(solution)/shard_map/ppermute | solution.py:196
  37.7 10.5 %collective-permute-start.5 = (bf16[48,32,128]{2,1,0:T(8,128)(2,1)S(1)}, bf16[48,32,128]{2,1,0:T(8,128)(2,1)S(1)}, u32[]{:S(2)}, u32[]{:S(2)}) collective-permute-start(bf16[48,32,128]{2,1,0:T(8,128)(2,1)S(1)} %get-tuple-element.35), channel_id=1, source_target_pairs={{0,2},{1,5},{2,0},{3,7},{4,6},{5,1},{6,4},{7,3},{8,10},{9,13},{10,... | collective-permute-start | bytes 1179656 | tf_op jit(solution)/shard_map/ppermute | solution.py:196
  38.3 14.7 %collective-permute-start.7 = (bf16[48,32,128]{2,1,0:T(8,128)(2,1)S(1)}, bf16[48,32,128]{2,1,0:T(8,128)(2,1)S(1)}, u32[]{:S(2)}, u32[]{:S(2)}) collective-permute-start(bf16[48,32,128]{2,1,0:T(8,128)(2,1)S(1)} %merge.4), channel_id=1, source_target_pairs={{0,8},{1,9},{2,10},{3,11},{4,12},{5,13},{6,14},{7,15},{8,0},{9,1},... | collective-permute-start | bytes 1179656 | tf_op jit(solution)/shard_map/ppermute | solution.py:196
  44.0 14.7 %collective-permute-start.9 = (bf16[48,32,128]{2,1,0:T(8,128)(2,1)S(1)}, bf16[48,32,128]{2,1,0:T(8,128)(2,1)S(1)}, u32[]{:S(2)}, u32[]{:S(2)}) collective-permute-start(bf16[48,32,128]{2,1,0:T(8,128)(2,1)S(1)} %merge.5), channel_id=1, source_target_pairs={{0,4},{1,3},{2,6},{3,1},{4,0},{5,7},{6,2},{7,5},{8,12},{9,11},{10,... | collective-permute-start | bytes 1179656 | tf_op jit(solution)/shard_map/ppermute | solution.py:196
  44.3 1.0 %copy-start.8 = (bf16[48,32,128]{2,1,0:T(8,128)(2,1)S(1)}, bf16[48,32,128]{2,1,0:T(8,128)(2,1)}, u32[]{:S(2)}) copy-start(bf16[48,32,128]{2,1,0:T(8,128)(2,1)} %copy-done.7) | copy-start | bytes 1179652
